TPU v7x, 32 devices: a whole 2x2x4 slice. The times are simulated.
32 devices in a mesh: leaf: 8 (over z, x), rep: 4 (over y, core).
Axes of the slice: x: 2, y: 2, z: 4, core: 2. Of those that a mesh axis runs over, the one named last changes fastest.
Arguments:
- leaf_blocks: float32 [8192, 1024], P('leaf'), as said below
- generators: float32 [3, 128, 8192], P(None, 'rep', 'leaf'), may hold values from -0.5 to 0.5
- rhs: float32 [128, 8192], P('rep', 'leaf'), may hold values from -6 to 6
- order: int32 [8, 1024], P('leaf'), may hold values from 0 to 1023, each once within a row
- ranks: int32 [3, 8], P(None, 'leaf'), may hold values from 32 to 128, as said below
Outputs:
- solution: float32 [128, 8192], P('rep', 'leaf')
- determinants: float32 [4], replicated
Inputs may be any that keep to these rules, and one draw needn't show every extreme that they name: `leaf_blocks`: each block of 1024 rows is a symmetric positive definite leaf covariance block. ranks[k, i] is equal for all leaves i of one depth-k node (equal i // 2**(k+1)); every level has a node of full rank 128. Each row of order is a permutation of the 1024 positions.
All inputs are finite; a program needn't handle non-finite values.
Results may differ from a plain program's by a relative error of at most 0.0003.
Values sent between devices are 32-bit elements; how exact they have to be, the bound alone decides.
No kernel may reach another device: no remote copies, remote signals or barrier semaphores. Data moves between devices by JAX's collectives and lax.ppermute only.
A program may use at most 128 MiB of HBM per device.

v0:
```python
import functools

import jax
import jax.numpy as jnp
from jax import lax
from jax.experimental import pallas as pl
from jax.experimental.pallas import tpu as pltpu
from jax.sharding import PartitionSpec as P

F32 = jnp.float32
BF16 = jnp.bfloat16
B = 128
SUB = 8
PARAMS = pltpu.CompilerParams(vmem_limit_bytes=40 * 2**20)


def lanes_of(value, lane):
    index = jnp.full((SUB, B), lane, jnp.int32)
    return jnp.take_along_axis(value, index, axis=1, mode="promise_in_bounds")


def row_of(value, row):
    return jnp.broadcast_to(value[row : row + 1, :], (SUB, B))


def sweep(rows):
    lane = lax.broadcasted_iota(jnp.int32, (SUB, B), 1)
    sub = lax.broadcasted_iota(jnp.int32, (SUB, B), 0)
    count = B // SUB
    pivots = jnp.ones((SUB, B), F32)
    rows = list(rows)
    t, rt = [None] * count, [None] * count
    cols = [lanes_of(rows[0], l) for l in range(SUB)]
    for p in range(count):
        base = SUB * p
        inside = (lane >= base) & (lane < base + SUB)
        upto = lane < base + SUB
        panel = jnp.where(inside, jnp.where(lane - base == sub, 1.0, 0.0), rows[p])
        t[p] = jnp.where(upto, panel, 0.0)
        following = p + 1 < count
        ahead = None
        if following:
            first = [lanes_of(rows[p + 1], base + l) for l in range(SUB)]
            below = list(first)
            ahead = [lanes_of(rows[p + 1], base + SUB + l) for l in range(SUB)]
        for j in range(SUB):
            across = {l: row_of(cols[l], j) for l in range(j, SUB)}
            pivots = jnp.where(lane == base + j, across[j], pivots)
            inverse = pltpu.reciprocal(across[j], approx=True)
            scale = jnp.where(sub == j, 1.0 - inverse, cols[j] * inverse)
            for l in range(j + 1, SUB):
                cols[l] = cols[l] - scale * across[l]
            panel = panel - scale * row_of(panel, j)
            if following:
                factor = below[j] * inverse
                for l in range(SUB):
                    ahead[l] = ahead[l] - factor * row_of(below[j], l)
                for l in range(j + 1, SUB):
                    below[l] = below[l] - factor * across[l]
        rt[p] = jnp.where(upto, panel, 0.0)
        if following:
            spread = [row_of(panel, i) for i in range(SUB)]
        for q in range(p + 1, count):
            weight = first if q == p + 1 else [lanes_of(rows[q], base + l) for l in range(SUB)]
            even = jnp.where(inside, 0.0, rows[q]) - weight[0] * spread[0]
            odd = weight[1] * spread[1]
            for l in range(2, SUB, 2):
                even = even - weight[l] * spread[l]
                odd = odd + weight[l + 1] * spread[l + 1]
            rows[q] = even - odd
        cols = ahead
    return jnp.concatenate(t + rt, axis=0), pivots


def rows_from(ref):
    return [ref[SUB * p : SUB * (p + 1), :] for p in range(B // SUB)]


def split(value):
    high = value.astype(BF16)
    return high, (value - high.astype(F32)).astype(BF16)


def dot_nt(left, right):
    return lax.dot_general(left, right, (((1,), (1,)), ((), ())), preferred_element_type=F32)


def dot_nn(left, right):
    return lax.dot_general(left, right, (((1,), (0,)), ((), ())), preferred_element_type=F32)


def join(parts, axis):
    return jnp.concatenate(parts, axis=axis)


def product_nt(left, right):
    lh, ll = left
    rh, rl = right
    return dot_nt(join([lh, lh, ll], 1), join([rh, rl, rh], 1))


def product_nn(left, right):
    lh, ll = left
    rh, rl = right
    return dot_nn(join([lh, lh, ll], 1), join([rh, rl, rh], 0))


def log_sum(pivots):
    return jnp.sum(jnp.log(pivots[:1]), axis=1, keepdims=True)


def factor_kernel(
    blocks, low_hi, low_lo, tri_hi, tri_lo, logs, work, corner, mult_hi, mult_lo, sems
):
    points = work.shape[0]
    count = points // B
    whole_copy = pltpu.make_async_copy(blocks, work, sems.at[0])
    first_copy = pltpu.make_async_copy(blocks.at[:B, :B], corner, sems.at[1])
    first_copy.start()
    whole_copy.start()
    first_copy.wait()

    def step(k, total):
        tri, pivots = sweep(rows_from(corner))
        high, low = split(tri)
        tri_hi[k] = high
        tri_lo[k] = low

        for at in range(count - 1):

            @pl.when(k == at)
            def _():
                if at == 0:
                    whole_copy.wait()
                start, mid = at * B, (at + 1) * B
                both = product_nt(split(work[mid:, start:mid]), (tri_hi[at], tri_lo[at]))
                hi, lo = split(both[:, :B])
                low_hi[mid:, start:mid] = hi
                low_lo[mid:, start:mid] = lo
                hi, lo = split(both[:, B:])
                mult_hi[mid:, :] = hi
                mult_lo[mid:, :] = lo
                for col in range(mid, points, B):
                    change = product_nt(
                        (mult_hi[col:, :], mult_lo[col:, :]),
                        (
                            low_hi[col : col + B, start:mid],
                            low_lo[col : col + B, start:mid],
                        ),
                    )
                    fresh = work[col:, col : col + B] - change
                    work[col:, col : col + B] = fresh
                    if col == mid:
                        corner[...] = fresh[:B]

        return total + log_sum(pivots)

    total = lax.fori_loop(0, count, step, jnp.zeros((1, 1), F32))
    logs[...] = jnp.broadcast_to(total, logs.shape)


def factor_leaf(block):
    points = block.shape[1]
    count = points // B
    return pl.pallas_call(
        factor_kernel,
        out_shape=(
            jax.ShapeDtypeStruct((points, points), BF16),
            jax.ShapeDtypeStruct((points, points), BF16),
            jax.ShapeDtypeStruct((count, 2 * B, B), BF16),
            jax.ShapeDtypeStruct((count, 2 * B, B), BF16),
            jax.ShapeDtypeStruct((SUB, B), F32),
        ),
        in_specs=[pl.BlockSpec(memory_space=pl.ANY)],
        scratch_shapes=[
            pltpu.VMEM((points, points), F32),
            pltpu.VMEM((B, B), F32),
            pltpu.VMEM((points, B), BF16),
            pltpu.VMEM((points, B), BF16),
            pltpu.SemaphoreType.DMA((2,)),
        ],
        compiler_params=PARAMS,
        name="factor",
    )(block)


def permutation(order_ref, points):
    sensor = lax.broadcasted_iota(jnp.int32, (points, points), 0)
    return jnp.where(sensor == order_ref[...], 1.0, 0.0).astype(BF16)


def thirds(value):
    high = value.astype(BF16)
    rest = value - high.astype(F32)
    mid = rest.astype(BF16)
    return high, mid, (rest - mid.astype(F32)).astype(BF16)


def column_rows(levels, extra, entry):
    return (levels - entry) * B + extra


def forward_kernel(
    ranks, gathered, rhs, order, low_hi, low_lo, tri_hi, tri_lo, logs,
    message, w_hi, w_lo, perm, values, m_hi, m_lo,
):
    levels, _, points = gathered.shape
    extra = rhs.shape[0]
    count = points // B
    for level in range(levels):
        row = lax.broadcasted_iota(jnp.int32, (B, points), 0)
        values[level * B : (level + 1) * B, :] = jnp.where(
            row < ranks[level, 0], gathered[level], 0.0
        )
    perm[...] = permutation(order, points)
    moved = dot_nn(join(thirds(rhs[...]), 0), perm[...])
    values[levels * B :, :] = moved[:extra] + (moved[extra : 2 * extra] + moved[2 * extra :])
    for k in range(count):
        start, end = k * B, (k + 1) * B
        own = values[:, start:end]
        if k > 0:
            own = own - product_nt(
                (m_hi[:, :start], m_lo[:, :start]),
                (low_hi[start:end, :start], low_lo[start:end, :start]),
            )
        both = product_nt(split(own), (tri_hi[k], tri_lo[k]))
        hi, lo = split(both[:, :B])
        w_hi[:, start:end] = hi
        w_lo[:, start:end] = lo
        hi, lo = split(both[:, B:])
        m_hi[:, start:end] = hi
        m_lo[:, start:end] = lo
    at = 0
    for entry in range(levels):
        top = entry * B
        size = column_rows(levels, extra, entry)
        message[at : at + size, :] = product_nt(
            (m_hi[top:, :], m_lo[top:, :]), (w_hi[top : top + B, :], w_lo[top : top + B, :])
        )
        at += size
    lane = lax.broadcasted_iota(jnp.int32, (SUB, B), 1)
    message[at:, :] = jnp.where(lane == 0, logs[...] / points, 0.0)


def message_rows(levels, extra):
    return sum(column_rows(levels, extra, entry) for entry in range(levels)) + SUB


def vmem():
    return pl.BlockSpec(memory_space=pltpu.VMEM)


def forward(ranks, gathered, rhs, order, factors, logs):
    levels, _, points = gathered.shape
    extra = rhs.shape[0]
    rows = levels * B + extra
    return pl.pallas_call(
        forward_kernel,
        out_shape=(
            jax.ShapeDtypeStruct((message_rows(levels, extra), B), F32),
            jax.ShapeDtypeStruct((rows, points), BF16),
            jax.ShapeDtypeStruct((rows, points), BF16),
            jax.ShapeDtypeStruct((points, points), BF16),
        ),
        in_specs=[pl.BlockSpec(memory_space=pltpu.SMEM)] + [vmem()] * 8,
        out_specs=(vmem(),) * 4,
        scratch_shapes=[
            pltpu.VMEM((rows, points), F32),
            pltpu.VMEM((rows, points), BF16),
            pltpu.VMEM((rows, points), BF16),
        ],
        compiler_params=PARAMS,
        name="forward",
    )(ranks, gathered, rhs, order, *factors, logs)


def backward_kernel(low_hi, low_lo, tri_hi, tri_lo, w_hi, w_lo, perm, out, v_hi, v_lo, v_last):
    points = low_hi.shape[0]
    count = points // B
    for k in reversed(range(count)):
        start, end = k * B, (k + 1) * B
        own = w_hi[:, start:end].astype(F32) + w_lo[:, start:end].astype(F32)
        if end < points:
            own = own - product_nn(
                (v_hi[:, end:], v_lo[:, end:]), (low_hi[end:, start:end], low_lo[end:, start:end])
            )
        solved = product_nn(split(own), (tri_hi[k, B:, :], tri_lo[k, B:, :]))
        hi, mid, last = thirds(solved)
        v_hi[:, start:end] = hi
        v_lo[:, start:end] = mid
        v_last[:, start:end] = last
    sensors = perm[...]
    out[...] = dot_nt(v_hi[...], sensors) + (dot_nt(v_lo[...], sensors) + dot_nt(v_last[...], sensors))


def backward(factors, w_hi, w_lo, perm):
    rows, points = w_hi.shape
    return pl.pallas_call(
        backward_kernel,
        out_shape=jax.ShapeDtypeStruct((rows, points), F32),
        in_specs=[vmem()] * 7,
        out_specs=vmem(),
        scratch_shapes=[pltpu.VMEM((rows, points), BF16)] * 3,
        compiler_params=PARAMS,
        name="backward",
    )(*factors, w_hi, w_lo, perm)


def eliminate(depth, levels, extra, own, received, merged, corner):
    merged[...] = own[...] + received[...]
    size = column_rows(levels - depth, extra, 0)
    row = lax.broadcasted_iota(jnp.int32, (B, B), 0)
    column = lax.broadcasted_iota(jnp.int32, (B, B), 1)
    corner[...] = merged[:B, :] + jnp.where(row == column, 1.0, 0.0)
    tri, pivots = sweep(rows_from(corner))
    lane = lax.broadcasted_iota(jnp.int32, (SUB, B), 1)
    totals = merged[merged.shape[0] - SUB :, :] + jnp.where(
        lane == depth + 1, log_sum(pivots) / B, 0.0
    )
    pieces = split(tri)
    both = product_nt(split(merged[B:size, :]), pieces)
    return size, pieces, both, totals


def merge_kernel(depth, levels, own, received, message, w_out, tri_out, merged, corner):
    extra = w_out.shape[0] - (levels - depth - 1) * B
    size, pieces, both, totals = eliminate(
        depth, levels, extra, own, received, merged, corner
    )
    below = split(both[:, :B])
    mult = split(both[:, B:])
    w_out[...] = both[:, :B]
    tri_out[...] = pieces[0][B:].astype(F32) + pieces[1][B:].astype(F32)
    at = 0
    for entry in range(levels - depth - 1):
        top = entry * B
        rows = column_rows(levels - depth - 1, extra, entry)
        change = product_nt(
            tuple(part[top:] for part in mult), tuple(part[top : top + B] for part in below)
        )
        message[at : at + rows, :] = merged[size + at : size + at + rows, :] - change
        at += rows
    message[at:, :] = totals


def merge(depth, levels, extra, own, received):
    rows = column_rows(levels - depth, extra, 0) - B
    return pl.pallas_call(
        functools.partial(merge_kernel, depth, levels),
        out_shape=(
            jax.ShapeDtypeStruct((message_rows(levels - depth - 1, extra), B), F32),
            jax.ShapeDtypeStruct((rows, B), F32),
            jax.ShapeDtypeStruct((B, B), F32),
        ),
        in_specs=[vmem()] * 2,
        out_specs=(vmem(),) * 3,
        scratch_shapes=[pltpu.VMEM(own.shape, F32), pltpu.VMEM((B, B), F32)],
        compiler_params=PARAMS,
        name="merge",
    )(own, received)


def finish_kernel(levels, leaf_count, *refs):
    own, received, solved = refs[:3]
    saved = refs[3 : 3 + 2 * (levels - 1)]
    out, means, merged, corner = refs[3 + 2 * (levels - 1) :]
    extra = out.shape[0]
    depth = levels - 1
    _, pieces, both, totals = eliminate(depth, levels, extra, own, received, merged, corner)
    coeffs = [None] * levels
    coeffs[depth] = split(
        product_nn(split(both[:, :B]), tuple(part[B:] for part in pieces))
    )
    for level in reversed(range(levels - 1)):
        w_ref, tri_ref = saved[2 * level], saved[2 * level + 1]
        inner = (levels - level - 1) * B
        known = tuple(
            join([coeffs[m][part] for m in range(level + 1, levels)], 1) for part in range(2)
        )
        target = w_ref[inner:, :] - product_nn(known, split(w_ref[:inner, :]))
        coeffs[level] = split(product_nn(split(target), split(tri_ref[...])))
    known = tuple(join([coeffs[m][part] for m in range(levels)], 1) for part in range(2))
    out[...] = solved[levels * B :, :] - product_nn(known, split(solved[: levels * B, :]))
    lane = lax.broadcasted_iota(jnp.int32, (SUB, B), 1)
    scale = jnp.zeros((SUB, B), F32)
    for entry in range(levels + 1):
        scale = jnp.where(lane == entry, 2.0**entry / leaf_count, scale)
    means[...] = totals * scale


def finish(levels, leaf_count, extra, own, received, solved, saved):
    points = solved.shape[1]
    return pl.pallas_call(
        functools.partial(finish_kernel, levels, leaf_count),
        out_shape=(
            jax.ShapeDtypeStruct((extra, points), F32),
            jax.ShapeDtypeStruct((SUB, B), F32),
        ),
        in_specs=[vmem()] * (3 + len(saved)),
        out_specs=(vmem(),) * 2,
        scratch_shapes=[pltpu.VMEM(own.shape, F32), pltpu.VMEM((B, B), F32)],
        compiler_params=PARAMS,
        name="finish",
    )(own, received, solved, *saved)


def swapped(value, axis, bit):
    mask = 2**bit
    pairs = [(source, source ^ mask) for source in range(lax.axis_size(axis))]
    return lax.ppermute(value, axis, pairs)


def shards(leaf_blocks, generators, rhs, order, ranks):
    levels = generators.shape[0]
    extra = rhs.shape[0]
    gathered = lax.all_gather(generators, "rep", axis=1, tiled=True)
    *factors, logs = factor_leaf(leaf_blocks)
    message, w_hi, w_lo, perm = forward(ranks, gathered, rhs, order, factors, logs)
    saved = []
    for depth in range(levels - 1):
        received = swapped(message, "leaf", depth)
        if depth == 0:
            solved = backward(factors, w_hi, w_lo, perm)
        message, w_level, tri_level = merge(depth, levels, extra, message, received)
        saved += [w_level, tri_level]
    received = swapped(message, "leaf", levels - 1)
    out, means = finish(
        levels, lax.axis_size("leaf"), extra, message, received, solved, saved
    )
    return (out, means[0, : levels + 1])


def solution(mesh):
    placed = (
        P("leaf", None),
        P(None, "rep", "leaf"),
        P("rep", "leaf"),
        P("leaf", None),
        P(None, "leaf"),
    )
    return jax.shard_map(
        shards, mesh=mesh, in_specs=placed, out_specs=(P("rep", "leaf"), P()), check_vma=False
    )
```

profile of v0, /device:TPU:0, one launch (start us, length us, event | category | flops | bytes accessed | tf_op | source)
XLA Modules:
  0.0 105.6 jit_solution(7447291360829510197)
XLA Ops:
  7.2 0.0 all-gather.2.cloned.1.call-start
  7.2 0.7 all-gather.2.cloned.1.call-update
  7.9 0.7 copy.7.ranks
  8.6 2.2 %copy-done.3 = f32[1024,1024]{1,0:T(8,128)S(1)} copy-done((f32[1024,1024]{1,0:T(8,128)S(1)}, f32[1024,1024]{1,0:T(8,128)}, u32[]{:S(2)}) %copy-start.3) | copy-done | bytes 4194328
  10.8 29.3 %factor.1 = (bf16[1024,1024]{1,0:T(8,128)(2,1)S(1)}, bf16[1024,1024]{1,0:T(8,128)(2,1)S(1)}, bf16[8,256,128]{2,1,0:T(8,128)(2,1)S(1)}, bf16[8,256,128]{2,1,0:T(8,128)(2,1)S(1)}, f32[8,128]{1,0:T(8,128)S(1)}) custom-call(f32[1024,1024]{1,0:T(8,128)S(1)} %copy-done.3), custom_call_target="tpu_custom_call" | custom-call | tf_op jit(solution)/shard_map/factor/pallas_call | solution.py:165
  40.2 0.0 copy-start
  40.2 1.3 %copy-done = bf16[1024,1024]{1,0:T(8,128)(2,1)} copy-done((bf16[1024,1024]{1,0:T(8,128)(2,1)}, bf16[1024,1024]{1,0:T(8,128)(2,1)S(1)}, u32[]{:S(2)}) %copy-start) | copy-done | bytes 2097176
  41.5 0.0 copy-done.5
  41.5 0.0 copy-done.6
  41.5 1.6 %copy-done.1 = bf16[1024,1024]{1,0:T(8,128)(2,1)S(1)} copy-done((bf16[1024,1024]{1,0:T(8,128)(2,1)S(1)}, bf16[1024,1024]{1,0:T(8,128)(2,1)}, u32[]{:S(2)}) %copy-start.1) | copy-done | bytes 2097176
  43.1 1.4 %copy-done.4 = f32[3,128,1024]{2,1,0:T(8,128)S(1)} copy-done((f32[3,128,1024]{2,1,0:T(8,128)S(1)}, f32[3,128,1024]{2,1,0:T(8,128)}, u32[]{:S(2)}) %copy-start.4) | copy-done | bytes 1572888
  44.5 9.1 %forward.1 = (f32[872,128]{1,0:T(8,128)S(1)}, bf16[416,1024]{1,0:T(8,128)(2,1)S(1)}, bf16[416,1024]{1,0:T(8,128)(2,1)S(1)}, bf16[1024,1024]{1,0:T(8,128)(2,1)S(1)}) custom-call(s32[3,1]{1,0:T(4,128)S(1)} %copy.7.ranks, f32[3,128,1024]{2,1,0:T(8,128)S(1)} %copy-done.4, f32[32,1024]{1,0:T(8,128)S(1)} %copy-done.5, s32[1,1024]{1,0:T(1,128)S(1)} %copy-done.6, ...), custom_call_target="tpu_custom_call" | custom-call | tf_op jit(solution)/shard_map/forward/pallas_call | solution.py:257
  53.7 3.0 %collective-permute-start = (f32[872,128]{1,0:T(8,128)S(1)}, f32[872,128]{1,0:T(8,128)S(1)}, u32[]{:S(2)}, u32[]{:S(2)}) collective-permute-start(f32[872,128]{1,0:T(8,128)S(1)} %get-tuple-element.24.own), channel_id=1, source_target_pairs={{0,4},{4,0},{8,12},{12,8},{16,20},{20,16},{24,28},{28,24},{1,5},{5... | collective-permute-start | bytes 1339400 | tf_op jit(solution)/shard_map/ppermute | solution.py:410
  56.7 10.3 %collective-permute-done.received = f32[872,128]{1,0:T(8,128)S(1)} collective-permute-done((f32[872,128]{1,0:T(8,128)S(1)}, f32[872,128]{1,0:T(8,128)S(1)}, u32[]{:S(2)}, u32[]{:S(2)}) %collective-permute-start) | collective-permute-done | bytes 446496 | tf_op jit(solution)/shard_map/ppermute | solution.py:410
  67.0 3.7 %merge.2 = (f32[456,128]{1,0:T(8,128)S(1)}, f32[288,128]{1,0:T(8,128)S(1)}, f32[128,128]{1,0:T(8,128)S(1)}) custom-call(f32[872,128]{1,0:T(8,128)S(1)} %get-tuple-element.24.own, f32[872,128]{1,0:T(8,128)S(1)} %collective-permute-done.received), custom_call_target="tpu_custom_call" | custom-call | tf_op jit(solution)/shard_map/merge/pallas_call | solution.py:348
  70.7 1.9 %collective-permute-start.1 = (f32[456,128]{1,0:T(8,128)S(1)}, f32[456,128]{1,0:T(8,128)S(1)}, u32[]{:S(2)}, u32[]{:S(2)}) collective-permute-start(f32[456,128]{1,0:T(8,128)S(1)} %get-tuple-element.25.own), channel_id=1, source_target_pairs={{0,8},{4,12},{8,0},{12,4},{16,24},{20,28},{24,16},{28,20},{1,9},{5... | collective-permute-start | bytes 700424 | tf_op jit(solution)/shard_map/ppermute | solution.py:410
  72.6 5.0 %collective-permute-done.1.received = f32[456,128]{1,0:T(8,128)S(1)} collective-permute-done((f32[456,128]{1,0:T(8,128)S(1)}, f32[456,128]{1,0:T(8,128)S(1)}, u32[]{:S(2)}, u32[]{:S(2)}) %collective-permute-start.1) | collective-permute-done | bytes 233504 | tf_op jit(solution)/shard_map/ppermute | solution.py:410
  77.6 3.4 %merge.3 = (f32[168,128]{1,0:T(8,128)S(1)}, f32[160,128]{1,0:T(8,128)S(1)}, f32[128,128]{1,0:T(8,128)S(1)}) custom-call(f32[456,128]{1,0:T(8,128)S(1)} %get-tuple-element.25.own, f32[456,128]{1,0:T(8,128)S(1)} %collective-permute-done.1.received), custom_call_target="tpu_custom_call" | custom-call | tf_op jit(solution)/shard_map/merge/pallas_call | solution.py:348
  81.0 2.6 %collective-permute-start.2 = (f32[168,128]{1,0:T(8,128)S(1)}, f32[168,128]{1,0:T(8,128)S(1)}, u32[]{:S(2)}, u32[]{:S(2)}) collective-permute-start(f32[168,128]{1,0:T(8,128)S(1)} %get-tuple-element.26.refs_0_), channel_id=1, source_target_pairs={{0,16},{4,20},{8,24},{12,28},{16,0},{20,4},{24,8},{28,12},{1,17},{... | collective-permute-start | bytes 258056 | tf_op jit(solution)/shard_map/ppermute | solution.py:410
  83.6 0.0 copy-done.2
  83.6 9.4 %backward.1.refs_2_ = f32[416,1024]{1,0:T(8,128)S(1)} custom-call(bf16[1024,1024]{1,0:T(8,128)(2,1)S(1)} %get-tuple-element.19.low_hi, bf16[1024,1024]{1,0:T(8,128)(2,1)S(1)} %copy-done.2, bf16[8,256,128]{2,1,0:T(8,128)(2,1)S(1)} %get-tuple-element.21.tri_hi, bf16[8,256,128]{2,1,0:T(8,128)(2,1)S(1)} %get-tuple-element.22.tri_lo, ...), custom_call_target="tpu_custom_call" | custom-call | tf_op jit(solution)/shard_map/backward/pallas_call | solution.py:298
  93.0 0.0 collective-permute-done.2.refs_1_
  93.1 5.1 %finish.1 = (f32[32,1024]{1,0:T(8,128)}, f32[8,128]{1,0:T(8,128)S(1)}) custom-call(f32[168,128]{1,0:T(8,128)S(1)} %get-tuple-element.26.refs_0_, f32[168,128]{1,0:T(8,128)S(1)} %collective-permute-done.2.refs_1_, f32[416,1024]{1,0:T(8,128)S(1)} %backward.1.refs_2_, f32[288,128]{1,0:T(8,128)S(1)} %get-tuple-element.30.refs_3_, ...), custom_call_target="tpu_custom_call" | custom-call | tf_op jit(solution)/shard_map/finish/pallas_call | solution.py:393
  98.2 0.5 slice_bitcast_fusion
  (7 shorter events, 0.0 us)
Async XLA Ops:
  7.2 34.4 %all-gather.2.cloned.1.call-start = ((), (), s32[]{:S(2)}) async-start(), calls=%async_computation | async-start | bytes 1966080 | tf_op jit(solution)/shard_map/all_gather | solution.py:416
  8.6 2.2 %copy-start.3 = (f32[1024,1024]{1,0:T(8,128)S(1)}, f32[1024,1024]{1,0:T(8,128)}, u32[]{:S(2)}) copy-start(f32[1024,1024]{1,0:T(8,128)} %blocks.1) | copy-start | bytes 12582916
  10.8 30.7 %copy-start.5 = (f32[32,1024]{1,0:T(8,128)S(1)}, f32[32,1024]{1,0:T(8,128)}, u32[]{:S(2)}) copy-start(f32[32,1024]{1,0:T(8,128)} %rhs.1) | copy-start | bytes 393220
  10.8 30.7 %copy-start.6 = (s32[1,1024]{1,0:T(1,128)S(1)}, s32[1,1024]{1,0:T(1,128)}, u32[]{:S(2)}) copy-start(s32[1,1024]{1,0:T(1,128)} %order.1) | copy-start | bytes 12292
  40.2 1.3 %copy-start = (bf16[1024,1024]{1,0:T(8,128)(2,1)}, bf16[1024,1024]{1,0:T(8,128)(2,1)S(1)}, u32[]{:S(2)}) copy-start(bf16[1024,1024]{1,0:T(8,128)(2,1)S(1)} %get-tuple-element.20.low_lo) | copy-start | bytes 6291460
  41.5 1.6 %copy-start.1 = (bf16[1024,1024]{1,0:T(8,128)(2,1)S(1)}, bf16[1024,1024]{1,0:T(8,128)(2,1)}, u32[]{:S(2)}) copy-start(bf16[1024,1024]{1,0:T(8,128)(2,1)} %copy-done) | copy-start | bytes 6291460
  43.1 1.4 %copy-start.4 = (f32[3,128,1024]{2,1,0:T(8,128)S(1)}, f32[3,128,1024]{2,1,0:T(8,128)}, u32[]{:S(2)}) copy-start(f32[3,128,1024]{2,1,0:T(8,128)} %all-gather.2.cloned.1.call-done.gathered) | copy-start | bytes 4718596
  44.5 39.1 %copy-start.2 = (bf16[1024,1024]{1,0:T(8,128)(2,1)S(1)}, bf16[1024,1024]{1,0:T(8,128)(2,1)}, u32[]{:S(2)}) copy-start(bf16[1024,1024]{1,0:T(8,128)(2,1)} %copy-done) | copy-start | bytes 6291460
  53.7 13.3 %collective-permute-start = (f32[872,128]{1,0:T(8,128)S(1)}, f32[872,128]{1,0:T(8,128)S(1)}, u32[]{:S(2)}, u32[]{:S(2)}) collective-permute-start(f32[872,128]{1,0:T(8,128)S(1)} %get-tuple-element.24.own), channel_id=1, source_target_pairs={{0,4},{4,0},{8,12},{12,8},{16,20},{20,16},{24,28},{28,24},{1,5},{5... | collective-permute-start | bytes 1339400 | tf_op jit(solution)/shard_map/ppermute | solution.py:410
  70.7 6.9 %collective-permute-start.1 = (f32[456,128]{1,0:T(8,128)S(1)}, f32[456,128]{1,0:T(8,128)S(1)}, u32[]{:S(2)}, u32[]{:S(2)}) collective-permute-start(f32[456,128]{1,0:T(8,128)S(1)} %get-tuple-element.25.own), channel_id=1, source_target_pairs={{0,8},{4,12},{8,0},{12,4},{16,24},{20,28},{24,16},{28,20},{1,9},{5... | collective-permute-start | bytes 700424 | tf_op jit(solution)/shard_map/ppermute | solution.py:410
  81.0 12.0 %collective-permute-start.2 = (f32[168,128]{1,0:T(8,128)S(1)}, f32[168,128]{1,0:T(8,128)S(1)}, u32[]{:S(2)}, u32[]{:S(2)}) collective-permute-start(f32[168,128]{1,0:T(8,128)S(1)} %get-tuple-element.26.refs_0_), channel_id=1, source_target_pairs={{0,16},{4,20},{8,24},{12,28},{16,0},{20,4},{24,8},{28,12},{1,17},{... | collective-permute-start | bytes 258056 | tf_op jit(solution)/shard_map/ppermute | solution.py:410
Sparse Core Ops, SparseCore 0:
  9.6 22.3 all-gather.1
where the time goes:
time: 106 us
  Pallas kernels  60.2 us (57%)
  waiting for transfers between devices  16 us (15%)
  between operations  14.1 us (13%)
  local copies, waits for them, and re-layouts  7.78 us (7%)
  starting transfers between devices  7.52 us (7%)
    pallas_call x1, Pallas kernels, factor_leaf(): pl.pallas_call(factor_kernel, out_shape=(jax.ShapeDtypeStruct((points, po...  29.3 us
    ppermute x3, waiting for transfers between devices, swapped(): return lax.ppermute(value, axis, pairs)  15.3 us
    pallas_call x1, Pallas kernels, backward(): pl.pallas_call(backward_kernel, out_shape=jax.ShapeDtypeStruct((rows, poi...  9.42 us
    pallas_call x1, Pallas kernels, forward(): pl.pallas_call(forward_kernel, out_shape=(jax.ShapeDtypeStruct((message_r...  9.14 us
    ppermute x3, starting transfers between devices, swapped(): return lax.ppermute(value, axis, pairs)  7.48 us
    unnamed x15, local copies, waits for them, and re-layouts  7.27 us
    pallas_call x2, Pallas kernels, merge(): pl.pallas_call(functools.partial(merge_kernel, depth, levels), out_shape=...  7.11 us
    pallas_call x1, Pallas kernels, finish(): pl.pallas_call(functools.partial(finish_kernel, levels, leaf_count), out_...  5.14 us
  transfers between devices with their start and end apart: 4, of which 2 were waited for; matrix products, arithmetic and copies ran while one was open for 1% of the time, Pallas kernels for 37%

commit v1 on v0

--- a/solution.py
+++ b/solution.py
@@ -11,7 +11,13 @@
 BF16 = jnp.bfloat16
 B = 128
 SUB = 8
-PARAMS = pltpu.CompilerParams(vmem_limit_bytes=40 * 2**20)
+
+
+def limit(mebibytes, flops=0):
+    return dict(
+        compiler_params=pltpu.CompilerParams(vmem_limit_bytes=mebibytes * 2**20),
+        cost_estimate=pl.CostEstimate(flops=flops, bytes_accessed=2**20, transcendentals=0),
+    )
 
 
 def lanes_of(value, lane):
@@ -159,6 +165,10 @@
     logs[...] = jnp.broadcast_to(total, logs.shape)
 
 
+def vmem():
+    return pl.BlockSpec(memory_space=pltpu.VMEM)
+
+
 def factor_leaf(block):
     points = block.shape[1]
     count = points // B
@@ -171,7 +181,8 @@
             jax.ShapeDtypeStruct((count, 2 * B, B), BF16),
             jax.ShapeDtypeStruct((SUB, B), F32),
         ),
-        in_specs=[pl.BlockSpec(memory_space=pl.ANY)],
+        in_specs=[pl.BlockSpec(memory_space=pltpu.HBM)],
+        out_specs=(vmem(),) * 5,
         scratch_shapes=[
             pltpu.VMEM((points, points), F32),
             pltpu.VMEM((B, B), F32),
@@ -179,7 +190,7 @@
             pltpu.VMEM((points, B), BF16),
             pltpu.SemaphoreType.DMA((2,)),
         ],
-        compiler_params=PARAMS,
+        **limit(10),
         name="factor",
     )(block)
 
@@ -200,30 +211,41 @@
     return (levels - entry) * B + extra
 
 
-def forward_kernel(
-    ranks, gathered, rhs, order, low_hi, low_lo, tri_hi, tri_lo, logs,
-    message, w_hi, w_lo, perm, values, m_hi, m_lo,
-):
-    levels, _, points = gathered.shape
+def halves(levels):
+    shared = sum((levels - entry) * B for entry in range(levels))
+    return shared, shared // 2 if levels > 1 else shared
+
+
+def forward_kernel(levels, size, *refs):
+    ranks, *pieces = refs[: size + 1]
+    rhs, order, low_hi, low_lo, tri_hi, tri_lo, logs = refs[size + 1 : size + 8]
+    shared, tail, send, w_hi, w_lo, perm, values, m_hi, m_lo = refs[size + 8 :]
+    points = rhs.shape[1]
     extra = rhs.shape[0]
     count = points // B
+    quarter = pieces[0].shape[1]
+    own = lax.axis_index("rep")
     for level in range(levels):
-        row = lax.broadcasted_iota(jnp.int32, (B, points), 0)
-        values[level * B : (level + 1) * B, :] = jnp.where(
-            row < ranks[level, 0], gathered[level], 0.0
-        )
+        limit_here = ranks[:, level : level + 1]
+        for shift in range(size):
+            first = (own ^ shift) * quarter
+            row = lax.broadcasted_iota(jnp.int32, (quarter, points), 0) + first
+            at = pl.multiple_of(level * B + first, SUB)
+            values[pl.ds(at, quarter), :] = jnp.where(
+                row < limit_here, pieces[shift][level], 0.0
+            )
     perm[...] = permutation(order, points)
     moved = dot_nn(join(thirds(rhs[...]), 0), perm[...])
     values[levels * B :, :] = moved[:extra] + (moved[extra : 2 * extra] + moved[2 * extra :])
     for k in range(count):
         start, end = k * B, (k + 1) * B
-        own = values[:, start:end]
+        here = values[:, start:end]
         if k > 0:
-            own = own - product_nt(
+            here = here - product_nt(
                 (m_hi[:, :start], m_lo[:, :start]),
                 (low_hi[start:end, :start], low_lo[start:end, :start]),
             )
-        both = product_nt(split(own), (tri_hi[k], tri_lo[k]))
+        both = product_nt(split(here), (tri_hi[k], tri_lo[k]))
         hi, lo = split(both[:, :B])
         w_hi[:, start:end] = hi
         w_lo[:, start:end] = lo
@@ -233,48 +255,59 @@
     at = 0
     for entry in range(levels):
         top = entry * B
-        size = column_rows(levels, extra, entry)
-        message[at : at + size, :] = product_nt(
+        rows = (levels - entry) * B
+        block = product_nt(
             (m_hi[top:, :], m_lo[top:, :]), (w_hi[top : top + B, :], w_lo[top : top + B, :])
         )
-        at += size
+        shared[at : at + rows, :] = block[:rows]
+        tail[entry * extra : (entry + 1) * extra, :] = block[rows:]
+        at += rows
     lane = lax.broadcasted_iota(jnp.int32, (SUB, B), 1)
-    message[at:, :] = jnp.where(lane == 0, logs[...] / points, 0.0)
-
-
-def message_rows(levels, extra):
-    return sum(column_rows(levels, extra, entry) for entry in range(levels)) + SUB
-
-
-def vmem():
-    return pl.BlockSpec(memory_space=pltpu.VMEM)
-
-
-def forward(ranks, gathered, rhs, order, factors, logs):
-    levels, _, points = gathered.shape
+    tail[levels * extra :, :] = jnp.where(lane == 0, logs[...] / points, 0.0)
+    outgoing(shared, tail, send)
+
+
+def outgoing(shared, tail, send):
+    half = send.shape[0] - tail.shape[0]
+    if half == shared.shape[0]:
+        send[:half, :] = shared[...]
+    else:
+        start = pl.multiple_of((lax.axis_index("rep") % 2) * half, SUB)
+        send[:half, :] = shared[pl.ds(start, half), :]
+    send[half:, :] = tail[...]
+
+
+def message_shapes(levels, extra):
+    shared, half = halves(levels)
+    tail = levels * extra + SUB
+    return [jax.ShapeDtypeStruct((rows, B), F32) for rows in (shared, tail, half + tail)]
+
+
+def forward(ranks, pieces, rhs, order, factors, logs):
+    levels, _, points = pieces[0].shape
     extra = rhs.shape[0]
     rows = levels * B + extra
     return pl.pallas_call(
-        forward_kernel,
+        functools.partial(forward_kernel, levels, len(pieces)),
         out_shape=(
-            jax.ShapeDtypeStruct((message_rows(levels, extra), B), F32),
+            *message_shapes(levels, extra),
             jax.ShapeDtypeStruct((rows, points), BF16),
             jax.ShapeDtypeStruct((rows, points), BF16),
             jax.ShapeDtypeStruct((points, points), BF16),
         ),
-        in_specs=[pl.BlockSpec(memory_space=pltpu.SMEM)] + [vmem()] * 8,
-        out_specs=(vmem(),) * 4,
+        in_specs=[vmem()] * (8 + len(pieces)),
+        out_specs=(vmem(),) * 6,
         scratch_shapes=[
             pltpu.VMEM((rows, points), F32),
             pltpu.VMEM((rows, points), BF16),
             pltpu.VMEM((rows, points), BF16),
         ],
-        compiler_params=PARAMS,
+        **limit(12),
         name="forward",
-    )(ranks, gathered, rhs, order, *factors, logs)
-
-
-def backward_kernel(low_hi, low_lo, tri_hi, tri_lo, w_hi, w_lo, perm, out, v_hi, v_lo, v_last):
+    )(ranks, *pieces, rhs, order, *factors, logs)
+
+
+def backward_kernel(low_hi, low_lo, tri_hi, tri_lo, w_hi, w_lo, v_hi, v_mid, v_last):
     points = low_hi.shape[0]
     count = points // B
     for k in reversed(range(count)):
@@ -282,91 +315,132 @@
         own = w_hi[:, start:end].astype(F32) + w_lo[:, start:end].astype(F32)
         if end < points:
             own = own - product_nn(
-                (v_hi[:, end:], v_lo[:, end:]), (low_hi[end:, start:end], low_lo[end:, start:end])
+                (v_hi[:, end:], v_mid[:, end:]),
+                (low_hi[end:, start:end], low_lo[end:, start:end]),
             )
         solved = product_nn(split(own), (tri_hi[k, B:, :], tri_lo[k, B:, :]))
         hi, mid, last = thirds(solved)
         v_hi[:, start:end] = hi
-        v_lo[:, start:end] = mid
+        v_mid[:, start:end] = mid
         v_last[:, start:end] = last
-    sensors = perm[...]
-    out[...] = dot_nt(v_hi[...], sensors) + (dot_nt(v_lo[...], sensors) + dot_nt(v_last[...], sensors))
-
-
-def backward(factors, w_hi, w_lo, perm):
-    rows, points = w_hi.shape
+
+
+def backward(factors, w_hi, w_lo):
     return pl.pallas_call(
         backward_kernel,
-        out_shape=jax.ShapeDtypeStruct((rows, points), F32),
-        in_specs=[vmem()] * 7,
+        out_shape=(jax.ShapeDtypeStruct(w_hi.shape, BF16),) * 3,
+        in_specs=[vmem()] * 6,
+        out_specs=(vmem(),) * 3,
+        **limit(8, 4 * 10**9),
+        name="backward",
+    )(*factors, w_hi, w_lo)
+
+
+def unorder_kernel(v_hi, v_mid, v_last, perm, out):
+    sensors = perm[...]
+    out[...] = dot_nt(v_hi[...], sensors) + (dot_nt(v_mid[...], sensors) + dot_nt(v_last[...], sensors))
+
+
+def unorder(solved, perm):
+    return pl.pallas_call(
+        unorder_kernel,
+        out_shape=jax.ShapeDtypeStruct(solved[0].shape, F32),
+        in_specs=[vmem()] * 4,
         out_specs=vmem(),
-        scratch_shapes=[pltpu.VMEM((rows, points), BF16)] * 3,
-        compiler_params=PARAMS,
-        name="backward",
-    )(*factors, w_hi, w_lo, perm)
-
-
-def eliminate(depth, levels, extra, own, received, merged, corner):
-    merged[...] = own[...] + received[...]
-    size = column_rows(levels - depth, extra, 0)
+        **limit(12, 4 * 10**9),
+        name="unorder",
+    )(*solved, perm)
+
+
+def eliminate(depth, levels, extra, refs):
+    shared, tail, received, *other, merged, below, corner = refs
+    left = levels - depth
+    whole, half = halves(left)
+    if other:
+        start = pl.multiple_of((lax.axis_index("rep") % 2) * half, SUB)
+        across = pl.multiple_of(half - start, SUB)
+        merged[pl.ds(start, half), :] = shared[pl.ds(start, half), :] + received[:half, :]
+        merged[pl.ds(across, half), :] = shared[pl.ds(across, half), :] + other[0][...]
+    else:
+        merged[...] = shared[...] + received[:half, :]
+    below[...] = tail[...] + received[half:, :]
     row = lax.broadcasted_iota(jnp.int32, (B, B), 0)
     column = lax.broadcasted_iota(jnp.int32, (B, B), 1)
     corner[...] = merged[:B, :] + jnp.where(row == column, 1.0, 0.0)
     tri, pivots = sweep(rows_from(corner))
     lane = lax.broadcasted_iota(jnp.int32, (SUB, B), 1)
-    totals = merged[merged.shape[0] - SUB :, :] + jnp.where(
+    totals = below[left * extra :, :] + jnp.where(
         lane == depth + 1, log_sum(pivots) / B, 0.0
     )
     pieces = split(tri)
-    both = product_nt(split(merged[B:size, :]), pieces)
-    return size, pieces, both, totals
-
-
-def merge_kernel(depth, levels, own, received, message, w_out, tri_out, merged, corner):
-    extra = w_out.shape[0] - (levels - depth - 1) * B
-    size, pieces, both, totals = eliminate(
-        depth, levels, extra, own, received, merged, corner
-    )
-    below = split(both[:, :B])
-    mult = split(both[:, B:])
+    panel = join([merged[B : left * B, :], below[:extra, :]], 0) if left > 1 else below[:extra, :]
+    both = product_nt(split(panel), pieces)
+    return pieces, both, totals
+
+
+def merge_kernel(depth, levels, extra, *refs):
+    inputs = refs[:4]
+    next_shared, next_tail, send, w_out, tri_out = refs[4:9]
+    scratch = refs[9:]
+    merged, below = scratch[:2]
+    pieces, both, totals = eliminate(depth, levels, extra, inputs + scratch)
+    left = levels - depth - 1
+    w_parts = split(both[:, :B])
+    m_parts = split(both[:, B:])
     w_out[...] = both[:, :B]
     tri_out[...] = pieces[0][B:].astype(F32) + pieces[1][B:].astype(F32)
     at = 0
-    for entry in range(levels - depth - 1):
+    for entry in range(left):
         top = entry * B
-        rows = column_rows(levels - depth - 1, extra, entry)
+        rows = (left - entry) * B
         change = product_nt(
-            tuple(part[top:] for part in mult), tuple(part[top : top + B] for part in below)
+            tuple(part[top:] for part in m_parts),
+            tuple(part[top : top + B] for part in w_parts),
         )
-        message[at : at + rows, :] = merged[size + at : size + at + rows, :] - change
+        base = (left + 1) * B + at
+        next_shared[at : at + rows, :] = merged[base : base + rows, :] - change[:rows]
+        next_tail[entry * extra : (entry + 1) * extra, :] = (
+            below[(entry + 1) * extra : (entry + 2) * extra, :] - change[rows:]
+        )
         at += rows
-    message[at:, :] = totals
-
-
-def merge(depth, levels, extra, own, received):
-    rows = column_rows(levels - depth, extra, 0) - B
+    next_tail[left * extra :, :] = totals
+    outgoing(next_shared, next_tail, send)
+
+
+def scratch_for(levels, extra):
+    shared, tail, _ = message_shapes(levels, extra)
+    return [
+        pltpu.VMEM(shared.shape, F32),
+        pltpu.VMEM(tail.shape, F32),
+        pltpu.VMEM((B, B), F32),
+    ]
+
+
+def merge(depth, levels, extra, message):
+    left = levels - depth
     return pl.pallas_call(
-        functools.partial(merge_kernel, depth, levels),
+        functools.partial(merge_kernel, depth, levels, extra),
         out_shape=(
-            jax.ShapeDtypeStruct((message_rows(levels - depth - 1, extra), B), F32),
-            jax.ShapeDtypeStruct((rows, B), F32),
+            *message_shapes(left - 1, extra),
+            jax.ShapeDtypeStruct(((left - 1) * B + extra, B), F32),
             jax.ShapeDtypeStruct((B, B), F32),
         ),
-        in_specs=[vmem()] * 2,
-        out_specs=(vmem(),) * 3,
-        scratch_shapes=[pltpu.VMEM(own.shape, F32), pltpu.VMEM((B, B), F32)],
-        compiler_params=PARAMS,
+        in_specs=[vmem()] * 4,
+        out_specs=(vmem(),) * 5,
+        scratch_shapes=scratch_for(left, extra),
+        **limit(6),
         name="merge",
-    )(own, received)
+    )(*message)
 
 
 def finish_kernel(levels, leaf_count, *refs):
-    own, received, solved = refs[:3]
-    saved = refs[3 : 3 + 2 * (levels - 1)]
-    out, means, merged, corner = refs[3 + 2 * (levels - 1) :]
+    solved = refs[3]
+    last = 4 + 2 * (levels - 1)
+    saved = refs[4:last]
+    out, means = refs[last : last + 2]
     extra = out.shape[0]
     depth = levels - 1
-    _, pieces, both, totals = eliminate(depth, levels, extra, own, received, merged, corner)
+    pieces, both, totals = eliminate(depth, levels, extra, refs[:3] + refs[last + 2 :])
     coeffs = [None] * levels
     coeffs[depth] = split(
         product_nn(split(both[:, :B]), tuple(part[B:] for part in pieces))
@@ -385,49 +459,60 @@
     scale = jnp.zeros((SUB, B), F32)
     for entry in range(levels + 1):
         scale = jnp.where(lane == entry, 2.0**entry / leaf_count, scale)
-    means[...] = totals * scale
-
-
-def finish(levels, leaf_count, extra, own, received, solved, saved):
+    means[...] = (totals * scale)[:1, : levels + 1]
+
+
+def finish(levels, leaf_count, extra, message, solved, saved):
     points = solved.shape[1]
     return pl.pallas_call(
         functools.partial(finish_kernel, levels, leaf_count),
         out_shape=(
             jax.ShapeDtypeStruct((extra, points), F32),
-            jax.ShapeDtypeStruct((SUB, B), F32),
+            jax.ShapeDtypeStruct((1, levels + 1), F32),
         ),
-        in_specs=[vmem()] * (3 + len(saved)),
+        in_specs=[vmem()] * (4 + len(saved)),
         out_specs=(vmem(),) * 2,
-        scratch_shapes=[pltpu.VMEM(own.shape, F32), pltpu.VMEM((B, B), F32)],
-        compiler_params=PARAMS,
+        scratch_shapes=scratch_for(1, extra),
+        **limit(6),
         name="finish",
-    )(own, received, solved, *saved)
-
-
-def swapped(value, axis, bit):
-    mask = 2**bit
+    )(*message, solved, *saved)
+
+
+def swapped(value, axis, mask):
     pairs = [(source, source ^ mask) for source in range(lax.axis_size(axis))]
     return lax.ppermute(value, axis, pairs)
+
+
+def exchange(message, depth, left, meanwhile=None):
+    shared, tail, send = message
+    received = swapped(send, "leaf", 2**depth)
+    done = None
+    if meanwhile is not None:
+        received, done = lax.optimization_barrier((received, meanwhile()))
+    if send.shape[0] == shared.shape[0] + tail.shape[0]:
+        return (shared, tail, received), done
+    other = swapped(received[: halves(left)[1]], "rep", 1)
+    return (shared, tail, received, other), done
 
 
 def shards(leaf_blocks, generators, rhs, order, ranks):
     levels = generators.shape[0]
     extra = rhs.shape[0]
-    gathered = lax.all_gather(generators, "rep", axis=1, tiled=True)
+    pieces = [generators]
+    pieces += [swapped(generators, "rep", shift) for shift in range(1, lax.axis_size("rep"))]
+    leaf_blocks = pltpu.with_memory_space_constraint(leaf_blocks, pltpu.HBM)
     *factors, logs = factor_leaf(leaf_blocks)
-    message, w_hi, w_lo, perm = forward(ranks, gathered, rhs, order, factors, logs)
-    saved = []
+    *message, w_hi, w_lo, perm = forward(ranks.T, pieces, rhs, order, factors, logs)
+    saved, solved = [], None
+    jobs = [lambda: backward(factors, w_hi, w_lo), lambda: unorder(solved, perm)]
     for depth in range(levels - 1):
-        received = swapped(message, "leaf", depth)
-        if depth == 0:
-            solved = backward(factors, w_hi, w_lo, perm)
-        message, w_level, tri_level = merge(depth, levels, extra, message, received)
+        arrived, done = exchange(message, depth, levels - depth, jobs.pop(0) if jobs else None)
+        solved = solved if done is None else done
+        *message, w_level, tri_level = merge(depth, levels, extra, arrived)
         saved += [w_level, tri_level]
-    received = swapped(message, "leaf", levels - 1)
-    out, means = finish(
-        levels, lax.axis_size("leaf"), extra, message, received, solved, saved
-    )
-    return (out, means[0, : levels + 1])
+    arrived, _ = exchange(message, levels - 1, 1)
+    out, means = finish(levels, lax.axis_size("leaf"), extra, arrived, solved, saved)
+    return (out, means.reshape(levels + 1))
 
 
 def solution(mesh):

time: 106 us -> 79.5 us (0.75)
  between operations: 14.1 us -> 0.8 us
  local copies, waits for them, and re-layouts: 7.78 us -> 0.04 us
  waiting for transfers between devices: 16 us -> 8.68 us
  starting transfers between devices: 7.52 us -> 9.65 us
    unnamed x15 -> x8, local copies, waits for them, and re-layouts: 7.27 us -> 0.02 us
    ppermute x3 -> x8, waiting for transfers between devices: 15.3 us -> 8.68 us  [swapped(): return lax.ppermute(value, axis, pairs)]
    ppermute x3 -> x8, starting transfers between devices: 7.48 us -> 9.65 us  [swapped(): return lax.ppermute(value, axis, pairs)]
    pallas_call x4 -> x5, Pallas kernels: 25.7 us -> 25.1 us  [the longest x1 8.62 us: forward(): pl.pallas_call(functools.partial(forward_kernel, levels, len(pieces)), ou...]
  transfers between devices with their start and end apart: 4 -> 8, of which waited for: 2 -> 4; matrix products, arithmetic and copies ran while one was open for 1% -> 0% of each run, Pallas kernels for 37% -> 49%
where the time goes in v1:
time: 79.5 us; the launch traced here: 79.3 us
  Pallas kernels  60.2 us (76%)
  starting transfers between devices  9.65 us (12%)
  waiting for transfers between devices  8.68 us (11%)
  between operations  0.8 us (1%)
    pallas_call x1, Pallas kernels, factor_leaf(): pl.pallas_call(factor_kernel, out_shape=(jax.ShapeDtypeStruct((points, po...  29.9 us
    ppermute x8, starting transfers between devices, swapped(): return lax.ppermute(value, axis, pairs)  9.65 us
    ppermute x8, waiting for transfers between devices, swapped(): return lax.ppermute(value, axis, pairs)  8.68 us
    pallas_call x1, Pallas kernels, forward(): pl.pallas_call(functools.partial(forward_kernel, levels, len(pieces)), ou...  8.62 us
    pallas_call x2, Pallas kernels, merge(): pl.pallas_call(functools.partial(merge_kernel, depth, levels, extra), out...  7.2 us
    pallas_call x1, Pallas kernels, backward(): pl.pallas_call(backward_kernel, out_shape=(jax.ShapeDtypeStruct(w_hi.shap...  6.45 us
    pallas_call x1, Pallas kernels, finish(): pl.pallas_call(functools.partial(finish_kernel, levels, leaf_count), out_...  5.14 us
    pallas_call x1, Pallas kernels, unorder(): pl.pallas_call(unorder_kernel, out_shape=jax.ShapeDtypeStruct(solved[0].s...  2.83 us
  transfers between devices with their start and end apart: 8, of which 4 were waited for; matrix products, arithmetic and copies ran while one was open for 0% of the time, Pallas kernels for 49%

profile of v1, /device:TPU:0, one launch (start us, length us, event | category | flops | bytes accessed | tf_op | source)
XLA Modules:
  0.0 79.3 jit_solution(14324408464506780219)
XLA Ops:
  0.6 0.0 copy-start
  0.7 3.0 %collective-permute-start.1 = (f32[3,32,1024]{2,1,0:T(8,128)}, f32[3,32,1024]{2,1,0:T(8,128)S(1)}, u32[]{:S(2)}, u32[]{:S(2)}) collective-permute-start(f32[3,32,1024]{2,1,0:T(8,128)} %refs_1_.1), channel_id=1, source_target_pairs={{0,2},{1,3},{2,0},{3,1},{4,6},{5,7},{6,4},{7,5},{8,10},{9,11},{10,... | collective-permute-start | bytes 1179656 | tf_op jit(solution)/shard_map/ppermute | solution.py:483
  3.7 0.0 collective-permute-start
  3.7 0.2 collective-permute-start.2
  3.9 29.9 %factor.1 = (bf16[1024,1024]{1,0:T(8,128)(2,1)S(1)}, bf16[1024,1024]{1,0:T(8,128)(2,1)S(1)}, bf16[8,256,128]{2,1,0:T(8,128)(2,1)S(1)}, bf16[8,256,128]{2,1,0:T(8,128)(2,1)S(1)}, f32[8,128]{1,0:T(8,128)S(1)}) custom-call(f32[1024,1024]{1,0:T(8,128)} %blocks.1), custom_call_target="tpu_custom_call" | custom-call | bytes 1048576 | tf_op jit(solution)/shard_map/factor/pallas_call | solution.py:175
  33.8 0.0 collective-permute-done.1.refs_3_
  33.8 0.0 collective-permute-done.refs_2_
  33.9 0.0 collective-permute-done.2.refs_4_
  33.9 8.6 %forward.1 = (f32[768,128]{1,0:T(8,128)S(1)}, f32[104,128]{1,0:T(8,128)S(1)}, f32[488,128]{1,0:T(8,128)S(1)}, bf16[416,1024]{1,0:T(8,128)(2,1)S(1)}, bf16[416,10...) custom-call(s32[1,3]{1,0:T(1,128)S(1)} %bitcast.2, f32[3,32,1024]{2,1,0:T(8,128)S(1)} %copy-done, ...), custom_call_target="tpu_custom_call" | custom-call | bytes 1048576 | tf_op jit(solution)/shard_map/forward/pallas_call | solution.py:290
  42.5 2.0 %collective-permute-start.3 = (f32[488,128]{1,0:T(8,128)S(1)}, f32[488,128]{1,0:T(8,128)S(1)}, u32[]{:S(2)}, u32[]{:S(2)}) collective-permute-start(f32[488,128]{1,0:T(8,128)S(1)} %get-tuple-element.41), channel_id=1, source_target_pairs={{0,4},{4,0},{8,12},{12,8},{16,20},{20,16},{24,28},{28,24},{1,5},{5... | collective-permute-start | bytes 749576 | tf_op jit(solution)/shard_map/ppermute | solution.py:483
  44.5 6.4 %backward.1 = (bf16[416,1024]{1,0:T(8,128)(2,1)S(1)}, bf16[416,1024]{1,0:T(8,128)(2,1)S(1)}, bf16[416,1024]{1,0:T(8,128)(2,1)S(1)}) custom-call(bf16[1024,1024]{1,0:T(8,128)(2,1)S(1)} %get-tuple-element.34.refs_7_.low_hi, bf16[1024,1024]{1,0:T(8,128)(2,1)S(1)} %get-tuple-element.35.refs_8_.low_lo, bf16[8,256,128]{2,1,0:T(8,128)(2,1)S(1)} %get-tuple-element.36.refs_9_.tri_hi, ...), custom_call_target="tpu_custom_call" | custom-call | flops 4000000000 | bytes 1048576 | tf_op jit(solution)/shard_map/backward/pallas_call | solution.py:329
  51.0 0.0 collective-permute-done.3.refs_2_
  51.0 0.1 collective-permute-start.4
  51.1 1.4 %collective-permute-done.4.refs_3_ = f32[384,128]{1,0:T(8,128)S(1)} collective-permute-done((f32[384,128]{1,0:T(8,128)S(1)}, f32[384,128]{1,0:T(8,128)S(1)}, u32[]{:S(2)}, u32[]{:S(2)}) %collective-permute-start.4) | collective-permute-done | bytes 196640 | tf_op jit(solution)/shard_map/ppermute | solution.py:483
  52.5 3.9 %merge.2 = (f32[384,128]{1,0:T(8,128)S(1)}, f32[72,128]{1,0:T(8,128)S(1)}, f32[264,128]{1,0:T(8,128)S(1)}, f32[288,128]{1,0:T(8,128)S(1)}, f32[128,128]{1,0:T(8,128)S(1)}) custom-call(f32[768,128]{1,0:T(8,128)S(1)} %get-tuple-element.39.refs_0_, f32[104,128]{1,0:T(8,128)S(1)} %get-tuple-element.40.refs_1_, f32[488,128]{1,0:T(8,128)S(1)} %collective-permute-done.3.refs_2_, ...), custom_call_target="tpu_custom_call" | custom-call | bytes 1048576 | tf_op jit(solution)/shard_map/merge/pallas_call | solution.py:421
  56.4 1.6 %collective-permute-start.5 = (f32[264,128]{1,0:T(8,128)S(1)}, f32[264,128]{1,0:T(8,128)S(1)}, u32[]{:S(2)}, u32[]{:S(2)}) collective-permute-start(f32[264,128]{1,0:T(8,128)S(1)} %get-tuple-element.50), channel_id=1, source_target_pairs={{0,8},{4,12},{8,0},{12,4},{16,24},{20,28},{24,16},{28,20},{1,9},{5... | collective-permute-start | bytes 405512 | tf_op jit(solution)/shard_map/ppermute | solution.py:483
  58.0 2.8 %unorder.1.refs_3_ = f32[416,1024]{1,0:T(8,128)S(1)} custom-call(bf16[416,1024]{1,0:T(8,128)(2,1)S(1)} %get-tuple-element.51.v_hi, bf16[416,1024]{1,0:T(8,128)(2,1)S(1)} %get-tuple-element.52.v_mid, bf16[416,1024]{1,0:T(8,128)(2,1)S(1)} %get-tuple-element.53.v_last, bf16[1024,1024]{1,0:T(8,128)(2,1)S(1)} %get-tuple-element.54.perm), custom_call_target="tpu_custom_call" | custom-call | flops 4000000000 | bytes 1048576 | tf_op jit(solution)/shard_map/unorder/pallas_call | solution.py:345
  60.9 1.2 %collective-permute-done.5.refs_2_ = f32[264,128]{1,0:T(8,128)S(1)} collective-permute-done((f32[264,128]{1,0:T(8,128)S(1)}, f32[264,128]{1,0:T(8,128)S(1)}, u32[]{:S(2)}, u32[]{:S(2)}) %collective-permute-start.5) | collective-permute-done | bytes 135200 | tf_op jit(solution)/shard_map/ppermute | solution.py:483
  62.1 0.1 collective-permute-start.6
  62.2 1.3 %collective-permute-done.6.refs_3_ = f32[192,128]{1,0:T(8,128)S(1)} collective-permute-done((f32[192,128]{1,0:T(8,128)S(1)}, f32[192,128]{1,0:T(8,128)S(1)}, u32[]{:S(2)}, u32[]{:S(2)}) %collective-permute-start.6) | collective-permute-done | bytes 98336 | tf_op jit(solution)/shard_map/ppermute | solution.py:483
  63.5 3.3 %merge.3 = (f32[128,128]{1,0:T(8,128)S(1)}, f32[40,128]{1,0:T(8,128)S(1)}, f32[168,128]{1,0:T(8,128)S(1)}, f32[160,128]{1,0:T(8,128)S(1)}, f32[128,128]{1,0:T(8,128)S(1)}) custom-call(f32[384,128]{1,0:T(8,128)S(1)} %get-tuple-element.48.refs_0_, f32[72,128]{1,0:T(8,128)S(1)} %get-tuple-element.49.refs_1_, f32[264,128]{1,0:T(8,128)S(1)} %collective-permute-done.5.refs_2_, ...), custom_call_target="tpu_custom_call" | custom-call | bytes 1048576 | tf_op jit(solution)/shard_map/merge/pallas_call | solution.py:421
  66.8 2.7 %collective-permute-start.7 = (f32[168,128]{1,0:T(8,128)S(1)}, f32[168,128]{1,0:T(8,128)S(1)}, u32[]{:S(2)}, u32[]{:S(2)}) collective-permute-start(f32[168,128]{1,0:T(8,128)S(1)} %get-tuple-element.58), channel_id=1, source_target_pairs={{0,16},{4,20},{8,24},{12,28},{16,0},{20,4},{24,8},{28,12},{1,17},{... | collective-permute-start | bytes 258056 | tf_op jit(solution)/shard_map/ppermute | solution.py:483
  69.4 4.7 %collective-permute-done.7.refs_2_ = f32[168,128]{1,0:T(8,128)S(1)} collective-permute-done((f32[168,128]{1,0:T(8,128)S(1)}, f32[168,128]{1,0:T(8,128)S(1)}, u32[]{:S(2)}, u32[]{:S(2)}) %collective-permute-start.7) | collective-permute-done | bytes 86048 | tf_op jit(solution)/shard_map/ppermute | solution.py:483
  74.2 5.1 %finish.1 = (f32[32,1024]{1,0:T(8,128)}, f32[1,4]{1,0:T(1,128)}) custom-call(f32[128,128]{1,0:T(8,128)S(1)} %get-tuple-element.56.refs_0_, f32[40,128]{1,0:T(8,128)S(1)} %get-tuple-element.57.refs_1_, f32[168,128]{1,0:T(8,128)S(1)} %collective-permute-done.7.refs_2_, f32[416,1024]{1,0:T(8,128)S(1)} %unorder.1.refs_3_, ...), custom_call_target="tpu_custom_call" | custom-call | bytes 1048576 | tf_op jit(solution)/shard_map/finish/pallas_call | solution.py:467
  (9 shorter events, 0.0 us)
Async XLA Ops:
  0.6 33.2 %copy-start = (f32[3,32,1024]{2,1,0:T(8,128)S(1)}, f32[3,32,1024]{2,1,0:T(8,128)}, u32[]{:S(2)}) copy-start(f32[3,32,1024]{2,1,0:T(8,128)} %refs_1_.1) | copy-start | bytes 1179652
  0.6 33.2 %copy-start.3 = (s32[3,1]{0,1:T(1,128)S(1)}, s32[3,1]{0,1:T(1,128)}, u32[]{:S(2)}) copy-start(s32[3,1]{0,1:T(1,128)} %param.9) | copy-start | bytes 40
  0.7 33.2 %copy-start.2 = (s32[1,1024]{1,0:T(1,128)S(1)}, s32[1,1024]{1,0:T(1,128)}, u32[]{:S(2)}) copy-start(s32[1,1024]{1,0:T(1,128)} %refs_6_.1) | copy-start | bytes 12292
  0.7 33.2 %copy-start.1 = (f32[32,1024]{1,0:T(8,128)S(1)}, f32[32,1024]{1,0:T(8,128)}, u32[]{:S(2)}) copy-start(f32[32,1024]{1,0:T(8,128)} %refs_5_.1) | copy-start | bytes 393220
  0.7 33.2 %collective-permute-start.1 = (f32[3,32,1024]{2,1,0:T(8,128)}, f32[3,32,1024]{2,1,0:T(8,128)S(1)}, u32[]{:S(2)}, u32[]{:S(2)}) collective-permute-start(f32[3,32,1024]{2,1,0:T(8,128)} %refs_1_.1), channel_id=1, source_target_pairs={{0,2},{1,3},{2,0},{3,1},{4,6},{5,7},{6,4},{7,5},{8,10},{9,11},{10,... | collective-permute-start | bytes 1179656 | tf_op jit(solution)/shard_map/ppermute | solution.py:483
  3.7 30.1 %collective-permute-start = (f32[3,32,1024]{2,1,0:T(8,128)}, f32[3,32,1024]{2,1,0:T(8,128)S(1)}, u32[]{:S(2)}, u32[]{:S(2)}) collective-permute-start(f32[3,32,1024]{2,1,0:T(8,128)} %refs_1_.1), channel_id=1, source_target_pairs={{0,1},{1,0},{2,3},{3,2},{4,5},{5,4},{6,7},{7,6},{8,9},{9,8},{10,11... | collective-permute-start | bytes 1179656 | tf_op jit(solution)/shard_map/ppermute | solution.py:483
  3.7 30.2 %collective-permute-start.2 = (f32[3,32,1024]{2,1,0:T(8,128)}, f32[3,32,1024]{2,1,0:T(8,128)S(1)}, u32[]{:S(2)}, u32[]{:S(2)}) collective-permute-start(f32[3,32,1024]{2,1,0:T(8,128)} %refs_1_.1), channel_id=1, source_target_pairs={{0,3},{1,2},{2,1},{3,0},{4,7},{5,6},{6,5},{7,4},{8,11},{9,10},{10,... | collective-permute-start | bytes 1179656 | tf_op jit(solution)/shard_map/ppermute | solution.py:483
  42.5 8.4 %collective-permute-start.3 = (f32[488,128]{1,0:T(8,128)S(1)}, f32[488,128]{1,0:T(8,128)S(1)}, u32[]{:S(2)}, u32[]{:S(2)}) collective-permute-start(f32[488,128]{1,0:T(8,128)S(1)} %get-tuple-element.41), channel_id=1, source_target_pairs={{0,4},{4,0},{8,12},{12,8},{16,20},{20,16},{24,28},{28,24},{1,5},{5... | collective-permute-start | bytes 749576 | tf_op jit(solution)/shard_map/ppermute | solution.py:483
  51.0 1.5 %collective-permute-start.4 = (f32[384,128]{1,0:T(8,128)S(1)}, f32[384,128]{1,0:T(8,128)S(1)}, u32[]{:S(2)}, u32[]{:S(2)}) collective-permute-start(f32[384,128]{1,0:T(8,128)S(1)} %slice.6), channel_id=1, source_target_pairs={{0,1},{1,0},{2,3},{3,2},{4,5},{5,4},{6,7},{7,6},{8,9},{9,8},{10,11... | collective-permute-start | bytes 589832 | tf_op jit(solution)/shard_map/ppermute | solution.py:483
  56.4 5.7 %collective-permute-start.5 = (f32[264,128]{1,0:T(8,128)S(1)}, f32[264,128]{1,0:T(8,128)S(1)}, u32[]{:S(2)}, u32[]{:S(2)}) collective-permute-start(f32[264,128]{1,0:T(8,128)S(1)} %get-tuple-element.50), channel_id=1, source_target_pairs={{0,8},{4,12},{8,0},{12,4},{16,24},{20,28},{24,16},{28,20},{1,9},{5... | collective-permute-start | bytes 405512 | tf_op jit(solution)/shard_map/ppermute | solution.py:483
  62.1 1.4 %collective-permute-start.6 = (f32[192,128]{1,0:T(8,128)S(1)}, f32[192,128]{1,0:T(8,128)S(1)}, u32[]{:S(2)}, u32[]{:S(2)}) collective-permute-start(f32[192,128]{1,0:T(8,128)S(1)} %slice.7), channel_id=1, source_target_pairs={{0,1},{1,0},{2,3},{3,2},{4,5},{5,4},{6,7},{7,6},{8,9},{9,8},{10,11... | collective-permute-start | bytes 294920 | tf_op jit(solution)/shard_map/ppermute | solution.py:483
  66.8 7.4 %collective-permute-start.7 = (f32[168,128]{1,0:T(8,128)S(1)}, f32[168,128]{1,0:T(8,128)S(1)}, u32[]{:S(2)}, u32[]{:S(2)}) collective-permute-start(f32[168,128]{1,0:T(8,128)S(1)} %get-tuple-element.58), channel_id=1, source_target_pairs={{0,16},{4,20},{8,24},{12,28},{16,0},{20,4},{24,8},{28,12},{1,17},{... | collective-permute-start | bytes 258056 | tf_op jit(solution)/shard_map/ppermute | solution.py:483

commit v2 on v1

--- a/solution.py
+++ b/solution.py
@@ -18,6 +18,10 @@
         compiler_params=pltpu.CompilerParams(vmem_limit_bytes=mebibytes * 2**20),
         cost_estimate=pl.CostEstimate(flops=flops, bytes_accessed=2**20, transcendentals=0),
     )
+
+
+def vmem():
+    return pl.BlockSpec(memory_space=pltpu.VMEM)
 
 
 def lanes_of(value, lane):
@@ -79,7 +83,7 @@
 
 
 def rows_from(ref):
-    return [ref[SUB * p : SUB * (p + 1), :] for p in range(B // SUB)]
+    return [ref[SUB * p : SUB * (p + 1), :B] for p in range(B // SUB)]
 
 
 def split(value):
@@ -115,84 +119,76 @@
     return jnp.sum(jnp.log(pivots[:1]), axis=1, keepdims=True)
 
 
-def factor_kernel(
-    blocks, low_hi, low_lo, tri_hi, tri_lo, logs, work, corner, mult_hi, mult_lo, sems
+def eliminate_column(panel, corner, tri):
+    both = product_nt(split(panel[:B]), tri)
+    below, mult = split(both[:, :B]), split(both[:, B:])
+    corner = corner - product_nt(mult, below)
+    if panel.shape[0] > B:
+        both = product_nt(split(panel[B:]), tri)
+        below = tuple(join(pair, 0) for pair in zip(below, split(both[:, :B])))
+        mult = tuple(join(pair, 0) for pair in zip(mult, split(both[:, B:])))
+    return below, mult, [corner[SUB * p : SUB * (p + 1)] for p in range(B // SUB)]
+
+
+def trail(source, target, mult, below):
+    src, src_off = source
+    dst, dst_off = target
+    size = mult[0].shape[0]
+    for col in range(0, size, B):
+        change = product_nt(
+            tuple(part[col:] for part in mult), tuple(part[col : col + B] for part in below)
+        )
+        fresh = src[src_off + col : src_off + size, src_off + col : src_off + col + B] - change
+        dst[dst_off + col : dst_off + size, dst_off + col : dst_off + col + B] = fresh
+
+
+def head_kernel(
+    cut, blocks, low_hi, low_lo, tri_hi, tri_lo, logs, work, corner, sems
 ):
     points = work.shape[0]
-    count = points // B
     whole_copy = pltpu.make_async_copy(blocks, work, sems.at[0])
     first_copy = pltpu.make_async_copy(blocks.at[:B, :B], corner, sems.at[1])
     first_copy.start()
     whole_copy.start()
     first_copy.wait()
+    tri, pivots = sweep(rows_from(corner))
+    tri_hi[0], tri_lo[0] = split(tri)
+    whole_copy.wait()
 
     def step(k, total):
-        tri, pivots = sweep(rows_from(corner))
-        high, low = split(tri)
-        tri_hi[k] = high
-        tri_lo[k] = low
-
-        for at in range(count - 1):
-
-            @pl.when(k == at)
-            def _():
-                if at == 0:
-                    whole_copy.wait()
-                start, mid = at * B, (at + 1) * B
-                both = product_nt(split(work[mid:, start:mid]), (tri_hi[at], tri_lo[at]))
-                hi, lo = split(both[:, :B])
-                low_hi[mid:, start:mid] = hi
-                low_lo[mid:, start:mid] = lo
-                hi, lo = split(both[:, B:])
-                mult_hi[mid:, :] = hi
-                mult_lo[mid:, :] = lo
-                for col in range(mid, points, B):
-                    change = product_nt(
-                        (mult_hi[col:, :], mult_lo[col:, :]),
-                        (
-                            low_hi[col : col + B, start:mid],
-                            low_lo[col : col + B, start:mid],
-                        ),
-                    )
-                    fresh = work[col:, col : col + B] - change
-                    work[col:, col : col + B] = fresh
-                    if col == mid:
-                        corner[...] = fresh[:B]
-
+        below, mult, rows = eliminate_column(
+            work[B:, :B], work[B : 2 * B, B : 2 * B], (tri_hi[k], tri_lo[k])
+        )
+        low_hi[k], low_lo[k] = below
+        tri, pivots = sweep(rows)
+        tri_hi[k + 1], tri_lo[k + 1] = split(tri)
+        trail((work, B), (work, 0), mult, below)
         return total + log_sum(pivots)
 
-    total = lax.fori_loop(0, count, step, jnp.zeros((1, 1), F32))
+    total = lax.fori_loop(0, cut, step, log_sum(pivots))
     logs[...] = jnp.broadcast_to(total, logs.shape)
 
 
-def vmem():
-    return pl.BlockSpec(memory_space=pltpu.VMEM)
-
-
-def factor_leaf(block):
+def head(cut, block):
     points = block.shape[1]
-    count = points // B
+    low = jax.ShapeDtypeStruct((cut, points - B, B), BF16)
+    tri = jax.ShapeDtypeStruct((cut + 1, 2 * B, B), BF16)
     return pl.pallas_call(
-        factor_kernel,
+        functools.partial(head_kernel, cut),
         out_shape=(
-            jax.ShapeDtypeStruct((points, points), BF16),
-            jax.ShapeDtypeStruct((points, points), BF16),
-            jax.ShapeDtypeStruct((count, 2 * B, B), BF16),
-            jax.ShapeDtypeStruct((count, 2 * B, B), BF16),
+            low,
+            low,
+            tri,
+            tri,
             jax.ShapeDtypeStruct((SUB, B), F32),
+            jax.ShapeDtypeStruct((points, points), F32),
         ),
         in_specs=[pl.BlockSpec(memory_space=pltpu.HBM)],
-        out_specs=(vmem(),) * 5,
-        scratch_shapes=[
-            pltpu.VMEM((points, points), F32),
-            pltpu.VMEM((B, B), F32),
-            pltpu.VMEM((points, B), BF16),
-            pltpu.VMEM((points, B), BF16),
-            pltpu.SemaphoreType.DMA((2,)),
-        ],
+        out_specs=(vmem(),) * 6,
+        scratch_shapes=[pltpu.VMEM((B, B), F32), pltpu.SemaphoreType.DMA((2,))],
         **limit(10),
-        name="factor",
-    )(block)
+        name="head",
+    )(pltpu.with_memory_space_constraint(block, pltpu.HBM))
 
 
 def permutation(order_ref, points):
@@ -216,13 +212,50 @@
     return shared, shared // 2 if levels > 1 else shared
 
 
+def gram_tiles(levels, extra):
+    bottom = levels * B + extra
+    tiles = []
+    for entry in range(0, levels, 2):
+        left, mid, right = entry * B, (entry + 1) * B, (entry + 2) * B
+        if entry + 1 < levels:
+            tiles += [(left, mid, left, mid), (mid, bottom, left, right)]
+        else:
+            tiles.append((left, bottom, left, mid))
+    return tiles
+
+
+def prepare_kernel(rhs, order, perm, moved):
+    extra, points = rhs.shape
+    perm[...] = permutation(order, points)
+    parts = dot_nn(join(thirds(rhs[...]), 0), perm[...])
+    moved[...] = parts[:extra] + (parts[extra : 2 * extra] + parts[2 * extra :])
+
+
+def prepare(rhs, order):
+    points = rhs.shape[1]
+    return pl.pallas_call(
+        prepare_kernel,
+        out_shape=(
+            jax.ShapeDtypeStruct((points, points), BF16),
+            jax.ShapeDtypeStruct(rhs.shape, F32),
+        ),
+        in_specs=[vmem()] * 2,
+        out_specs=(vmem(),) * 2,
+        **limit(8, 10**9),
+        name="prepare",
+    )(rhs, order)
+
+
 def forward_kernel(levels, size, *refs):
-    ranks, *pieces = refs[: size + 1]
-    rhs, order, low_hi, low_lo, tri_hi, tri_lo, logs = refs[size + 1 : size + 8]
-    shared, tail, send, w_hi, w_lo, perm, values, m_hi, m_lo = refs[size + 8 :]
-    points = rhs.shape[1]
-    extra = rhs.shape[0]
+    head_hi, head_lo, first_hi, first_lo, logs, before, ranks = refs[:7]
+    pieces = refs[7 : 7 + size]
+    moved, shared, tail, send, w_hi, w_lo, low_hi, low_lo, last_hi, last_lo = refs[
+        7 + size : 17 + size
+    ]
+    work, values, m_hi, m_lo = refs[17 + size :]
+    extra, points = moved.shape
     count = points // B
+    cut = head_hi.shape[0]
     quarter = pieces[0].shape[1]
     own = lax.axis_index("rep")
     for level in range(levels):
@@ -234,36 +267,83 @@
             values[pl.ds(at, quarter), :] = jnp.where(
                 row < limit_here, pieces[shift][level], 0.0
             )
-    perm[...] = permutation(order, points)
-    moved = dot_nn(join(thirds(rhs[...]), 0), perm[...])
-    values[levels * B :, :] = moved[:extra] + (moved[extra : 2 * extra] + moved[2 * extra :])
-    for k in range(count):
+    values[levels * B :, :] = moved[...]
+
+    def tri_of(k):
+        if k <= cut:
+            return first_hi[k], first_lo[k]
+        return last_hi[k - cut - 1], last_lo[k - cut - 1]
+
+    def low_of(k, left, right):
+        parts = []
+        for old, new in ((head_hi, low_hi), (head_lo, low_lo)):
+            blocks = [old[j, (k - j - 1) * B : (k - j) * B, :] for j in range(left, min(right, cut))]
+            start = max(left, cut)
+            if start < right:
+                rows = slice((k - cut - 1) * B, (k - cut) * B)
+                blocks.append(new[rows, (start - cut) * B : (right - cut) * B])
+            parts.append(join(blocks, 1))
+        return tuple(parts)
+
+    def advance(k):
         start, end = k * B, (k + 1) * B
         here = values[:, start:end]
-        if k > 0:
-            here = here - product_nt(
-                (m_hi[:, :start], m_lo[:, :start]),
-                (low_hi[start:end, :start], low_lo[start:end, :start]),
+        for left, right in ((0, k - 1), (max(k - 1, 0), k)):
+            if left < right:
+                held = slice(left * B, right * B)
+                here = here - product_nt((m_hi[:, held], m_lo[:, held]), low_of(k, left, right))
+        both = product_nt(split(here), tri_of(k))
+        w_hi[:, start:end], w_lo[:, start:end] = split(both[:, :B])
+        m_hi[:, start:end], m_lo[:, start:end] = split(both[:, B:])
+
+    total = logs[:1, :1]
+    tiles = gram_tiles(levels, extra)
+    sums = [None] * len(tiles)
+    done, summed = 0, 0
+
+    def accumulate(stop):
+        held = slice(summed * B, stop * B)
+        for i, (top, bottom, left, right) in enumerate(tiles):
+            piece = product_nt(
+                (m_hi[top:bottom, held], m_lo[top:bottom, held]),
+                (w_hi[left:right, held], w_lo[left:right, held]),
             )
-        both = product_nt(split(here), (tri_hi[k], tri_lo[k]))
-        hi, lo = split(both[:, :B])
-        w_hi[:, start:end] = hi
-        w_lo[:, start:end] = lo
-        hi, lo = split(both[:, B:])
-        m_hi[:, start:end] = hi
-        m_lo[:, start:end] = lo
-    at = 0
-    for entry in range(levels):
-        top = entry * B
-        rows = (levels - entry) * B
-        block = product_nt(
-            (m_hi[top:, :], m_lo[top:, :]), (w_hi[top : top + B, :], w_lo[top : top + B, :])
+            sums[i] = piece if sums[i] is None else sums[i] + piece
+        return stop
+
+    for at in range(cut, count - 1):
+        src = before if at == cut else work
+        base = (at - cut) * B
+        size_here = points - at * B
+        below, mult, rows = eliminate_column(
+            src[base + B : base + size_here, base : base + B],
+            src[base + B : base + 2 * B, base + B : base + 2 * B],
+            tri_of(at),
         )
-        shared[at : at + rows, :] = block[:rows]
-        tail[entry * extra : (entry + 1) * extra, :] = block[rows:]
-        at += rows
+        low_hi[base:, base : base + B], low_lo[base:, base : base + B] = below
+        tri, pivots = sweep(rows)
+        last_hi[at - cut], last_lo[at - cut] = split(tri)
+        total = total + log_sum(pivots)
+        trail((src, base + B), (work, base + B), mult, below)
+        goal = min(at + 1, (at - cut + 1) * count // (count - 1 - cut))
+        while done < goal:
+            advance(done)
+            done += 1
+        if at + 3 >= count:
+            summed = accumulate(done)
+    for k in range(done, count):
+        advance(k)
+    accumulate(count)
+    for (top, bottom, left, right), block in zip(tiles, sums):
+        for entry in range(left // B, right // B):
+            base = sum((levels - i) * B for i in range(entry)) - entry * B
+            part = block[:, entry * B - left : (entry + 1) * B - left]
+            stop = min(bottom, levels * B)
+            shared[base + top : base + stop, :] = part[: stop - top]
+            if bottom > stop:
+                tail[entry * extra : (entry + 1) * extra, :] = part[stop - top :]
     lane = lax.broadcasted_iota(jnp.int32, (SUB, B), 1)
-    tail[levels * extra :, :] = jnp.where(lane == 0, logs[...] / points, 0.0)
+    tail[levels * extra :, :] = jnp.where(lane == 0, total / points, 0.0)
     outgoing(shared, tail, send)
 
 
@@ -283,73 +363,97 @@
     return [jax.ShapeDtypeStruct((rows, B), F32) for rows in (shared, tail, half + tail)]
 
 
-def forward(ranks, pieces, rhs, order, factors, logs):
+def forward(ranks, pieces, moved, factors):
     levels, _, points = pieces[0].shape
-    extra = rhs.shape[0]
+    extra = moved.shape[0]
     rows = levels * B + extra
+    count = points // B
+    cut = factors[0].shape[0]
+    left = (count - 1 - cut) * B
+    low = jax.ShapeDtypeStruct((left, left), BF16)
+    tri = jax.ShapeDtypeStruct((count - 1 - cut, 2 * B, B), BF16)
+    half = jax.ShapeDtypeStruct((rows, points), BF16)
     return pl.pallas_call(
         functools.partial(forward_kernel, levels, len(pieces)),
-        out_shape=(
-            *message_shapes(levels, extra),
-            jax.ShapeDtypeStruct((rows, points), BF16),
-            jax.ShapeDtypeStruct((rows, points), BF16),
-            jax.ShapeDtypeStruct((points, points), BF16),
-        ),
+        out_shape=(*message_shapes(levels, extra), half, half, low, low, tri, tri),
         in_specs=[vmem()] * (8 + len(pieces)),
-        out_specs=(vmem(),) * 6,
+        out_specs=(vmem(),) * 9,
         scratch_shapes=[
+            pltpu.VMEM((left + B, left + B), F32),
             pltpu.VMEM((rows, points), F32),
             pltpu.VMEM((rows, points), BF16),
             pltpu.VMEM((rows, points), BF16),
         ],
-        **limit(12),
+        **limit(16),
         name="forward",
-    )(ranks, *pieces, rhs, order, *factors, logs)
-
-
-def backward_kernel(low_hi, low_lo, tri_hi, tri_lo, w_hi, w_lo, v_hi, v_mid, v_last):
-    points = low_hi.shape[0]
+    )(*factors, ranks, *pieces, moved)
+
+
+def reduce_rows(w_panel, tri, w_hi, w_lo):
+    coeffs = split(product_nn(split(w_panel[...]), split(tri[...])))
+    rest = w_hi[B:, :].astype(F32) + w_lo[B:, :].astype(F32)
+    return split(rest - product_nn(coeffs, (w_hi[:B, :], w_lo[:B, :])))
+
+
+def reduce_kernel(w_panel, tri, w_hi, w_lo, out_hi, out_lo):
+    out_hi[...], out_lo[...] = reduce_rows(w_panel, tri, w_hi, w_lo)
+
+
+def reduce(w_panel, tri, w_hi, w_lo):
+    shape = jax.ShapeDtypeStruct((w_hi.shape[0] - B, w_hi.shape[1]), BF16)
+    return pl.pallas_call(
+        reduce_kernel,
+        out_shape=(shape, shape),
+        in_specs=[vmem()] * 4,
+        out_specs=(vmem(),) * 2,
+        **limit(8, 4 * 10**9),
+        name="reduce",
+    )(w_panel, tri, w_hi, w_lo)
+
+
+def solve_kernel(
+    head_hi, head_lo, first_hi, first_lo, low_hi, low_lo, last_hi, last_lo, perm,
+    w_hi, w_lo, out, v_hi, v_mid, v_last,
+):
+    points = w_hi.shape[1]
     count = points // B
+    cut = head_hi.shape[0]
     for k in reversed(range(count)):
         start, end = k * B, (k + 1) * B
-        own = w_hi[:, start:end].astype(F32) + w_lo[:, start:end].astype(F32)
-        if end < points:
-            own = own - product_nn(
-                (v_hi[:, end:], v_mid[:, end:]),
-                (low_hi[end:, start:end], low_lo[end:, start:end]),
-            )
-        solved = product_nn(split(own), (tri_hi[k, B:, :], tri_lo[k, B:, :]))
-        hi, mid, last = thirds(solved)
-        v_hi[:, start:end] = hi
-        v_mid[:, start:end] = mid
-        v_last[:, start:end] = last
-
-
-def backward(factors, w_hi, w_lo):
+        here = w_hi[:, start:end].astype(F32) + w_lo[:, start:end].astype(F32)
+        for left, right in ((end + B, points), (end, min(end + B, points))):
+            if left >= right:
+                continue
+            if k < cut:
+                rows = slice(left - end, right - end)
+                below = head_hi[k, rows, :], head_lo[k, rows, :]
+            else:
+                rows = slice(left - (cut + 1) * B, right - (cut + 1) * B)
+                columns = slice((k - cut) * B, (k - cut + 1) * B)
+                below = low_hi[rows, columns], low_lo[rows, columns]
+            here = here - product_nn((v_hi[:, left:right], v_mid[:, left:right]), below)
+        if k <= cut:
+            tri = first_hi[k, B:, :], first_lo[k, B:, :]
+        else:
+            tri = last_hi[k - cut - 1, B:, :], last_lo[k - cut - 1, B:, :]
+        parts = thirds(product_nn(split(here), tri))
+        v_hi[:, start:end], v_mid[:, start:end], v_last[:, start:end] = parts
+    sensors = perm[...]
+    out[...] = dot_nt(v_hi[...], sensors) + (
+        dot_nt(v_mid[...], sensors) + dot_nt(v_last[...], sensors)
+    )
+
+
+def solve(factors, perm, w_hi, w_lo):
     return pl.pallas_call(
-        backward_kernel,
-        out_shape=(jax.ShapeDtypeStruct(w_hi.shape, BF16),) * 3,
-        in_specs=[vmem()] * 6,
-        out_specs=(vmem(),) * 3,
-        **limit(8, 4 * 10**9),
-        name="backward",
-    )(*factors, w_hi, w_lo)
-
-
-def unorder_kernel(v_hi, v_mid, v_last, perm, out):
-    sensors = perm[...]
-    out[...] = dot_nt(v_hi[...], sensors) + (dot_nt(v_mid[...], sensors) + dot_nt(v_last[...], sensors))
-
-
-def unorder(solved, perm):
-    return pl.pallas_call(
-        unorder_kernel,
-        out_shape=jax.ShapeDtypeStruct(solved[0].shape, F32),
-        in_specs=[vmem()] * 4,
+        solve_kernel,
+        out_shape=jax.ShapeDtypeStruct(w_hi.shape, F32),
+        in_specs=[vmem()] * (3 + len(factors)),
         out_specs=vmem(),
-        **limit(12, 4 * 10**9),
-        name="unorder",
-    )(*solved, perm)
+        scratch_shapes=[pltpu.VMEM(w_hi.shape, BF16)] * 3,
+        **limit(10, 4 * 10**9),
+        name="solve",
+    )(*factors, perm, w_hi, w_lo)
 
 
 def eliminate(depth, levels, extra, refs):
@@ -434,27 +538,11 @@
 
 
 def finish_kernel(levels, leaf_count, *refs):
-    solved = refs[3]
-    last = 4 + 2 * (levels - 1)
-    saved = refs[4:last]
-    out, means = refs[last : last + 2]
+    solved, out, means = refs[3:6]
     extra = out.shape[0]
-    depth = levels - 1
-    pieces, both, totals = eliminate(depth, levels, extra, refs[:3] + refs[last + 2 :])
-    coeffs = [None] * levels
-    coeffs[depth] = split(
-        product_nn(split(both[:, :B]), tuple(part[B:] for part in pieces))
-    )
-    for level in reversed(range(levels - 1)):
-        w_ref, tri_ref = saved[2 * level], saved[2 * level + 1]
-        inner = (levels - level - 1) * B
-        known = tuple(
-            join([coeffs[m][part] for m in range(level + 1, levels)], 1) for part in range(2)
-        )
-        target = w_ref[inner:, :] - product_nn(known, split(w_ref[:inner, :]))
-        coeffs[level] = split(product_nn(split(target), split(tri_ref[...])))
-    known = tuple(join([coeffs[m][part] for m in range(levels)], 1) for part in range(2))
-    out[...] = solved[levels * B :, :] - product_nn(known, split(solved[: levels * B, :]))
+    pieces, both, totals = eliminate(levels - 1, levels, extra, refs[:3] + refs[6:])
+    coeffs = split(product_nn(split(both[:, :B]), tuple(part[B:] for part in pieces)))
+    out[...] = solved[B:, :] - product_nn(coeffs, split(solved[:B, :]))
     lane = lax.broadcasted_iota(jnp.int32, (SUB, B), 1)
     scale = jnp.zeros((SUB, B), F32)
     for entry in range(levels + 1):
@@ -462,20 +550,19 @@
     means[...] = (totals * scale)[:1, : levels + 1]
 
 
-def finish(levels, leaf_count, extra, message, solved, saved):
-    points = solved.shape[1]
+def finish(levels, leaf_count, extra, message, solved):
     return pl.pallas_call(
         functools.partial(finish_kernel, levels, leaf_count),
         out_shape=(
-            jax.ShapeDtypeStruct((extra, points), F32),
+            jax.ShapeDtypeStruct((extra, solved.shape[1]), F32),
             jax.ShapeDtypeStruct((1, levels + 1), F32),
         ),
-        in_specs=[vmem()] * (4 + len(saved)),
+        in_specs=[vmem()] * 4,
         out_specs=(vmem(),) * 2,
         scratch_shapes=scratch_for(1, extra),
         **limit(6),
         name="finish",
-    )(*message, solved, *saved)
+    )(*message, solved)
 
 
 def swapped(value, axis, mask):
@@ -498,20 +585,31 @@
 def shards(leaf_blocks, generators, rhs, order, ranks):
     levels = generators.shape[0]
     extra = rhs.shape[0]
-    pieces = [generators]
-    pieces += [swapped(generators, "rep", shift) for shift in range(1, lax.axis_size("rep"))]
-    leaf_blocks = pltpu.with_memory_space_constraint(leaf_blocks, pltpu.HBM)
-    *factors, logs = factor_leaf(leaf_blocks)
-    *message, w_hi, w_lo, perm = forward(ranks.T, pieces, rhs, order, factors, logs)
-    saved, solved = [], None
-    jobs = [lambda: backward(factors, w_hi, w_lo), lambda: unorder(solved, perm)]
-    for depth in range(levels - 1):
-        arrived, done = exchange(message, depth, levels - depth, jobs.pop(0) if jobs else None)
-        solved = solved if done is None else done
-        *message, w_level, tri_level = merge(depth, levels, extra, arrived)
-        saved += [w_level, tri_level]
-    arrived, _ = exchange(message, levels - 1, 1)
-    out, means = finish(levels, lax.axis_size("leaf"), extra, arrived, solved, saved)
+    cut = leaf_blocks.shape[1] // B // 2 - 1
+    pieces = [generators, swapped(generators, "rep", 1)]
+    far = [swapped(generators, "rep", mask) for mask in range(2, lax.axis_size("rep"), 2)]
+    *factors, logs, rest = head(cut, leaf_blocks)
+    far, logs = lax.optimization_barrier((far, logs))
+    for arrived in far:
+        pieces += [arrived, swapped(arrived, "rep", 1)]
+    perm, moved = prepare(rhs, order)
+    *message, w_hi, w_lo, a, b, c, d = forward(
+        ranks.T, pieces, moved, (*factors, logs, rest)
+    )
+    factors += [a, b, c, d]
+    halves_of = (w_hi, w_lo)
+    level = None
+    for depth in range(levels):
+
+        def meanwhile():
+            rows = halves_of if level is None else reduce(*level, *halves_of)
+            return solve(factors, perm, *rows) if depth + 1 == levels else rows
+
+        arrived, halves_of = exchange(message, depth, levels - depth, meanwhile)
+        if depth + 1 < levels:
+            *message, w_level, tri_level = merge(depth, levels, extra, arrived)
+            level = (w_level, tri_level)
+    out, means = finish(levels, lax.axis_size("leaf"), extra, arrived, halves_of)
     return (out, means.reshape(levels + 1))
 
 

time: 79.5 us -> 69.7 us (0.88)
  Pallas kernels: 60.2 us -> 45.5 us
  waiting for transfers between devices: 8.68 us -> 13.7 us
    pallas_call x3 -> x5, Pallas kernels: 39.2 us -> 20.1 us  [the longest x1 13.9 us: head(): pl.pallas_call(functools.partial(head_kernel, cut), out_shape=(low, low,...]
    pallas_call x1, Pallas kernels: 8.62 us -> 14 us  [forward(): pl.pallas_call(functools.partial(forward_kernel, levels, len(pieces)), ou...]
    ppermute x8, waiting for transfers between devices: 8.68 us -> 13.7 us  [swapped(): return lax.ppermute(value, axis, pairs)]
    pallas_call x1, Pallas kernels: 5.14 us -> 4.33 us  [finish(): pl.pallas_call(functools.partial(finish_kernel, levels, leaf_count), out_...]
  transfers between devices with their start and end apart: 8 -> 8, of which waited for: 4 -> 5; matrix products, arithmetic and copies ran while one was open for 0% -> 0% of each run, Pallas kernels for 49% -> 29%
where the time goes in v2:
time: 69.7 us; the launch traced here: 69.5 us
  Pallas kernels  45.5 us (65%)
  waiting for transfers between devices  13.7 us (20%)
  starting transfers between devices  9.63 us (14%)
  between operations  0.76 us (1%)
    pallas_call x1, Pallas kernels, forward(): pl.pallas_call(functools.partial(forward_kernel, levels, len(pieces)), ou...  14 us
    pallas_call x1, Pallas kernels, head(): pl.pallas_call(functools.partial(head_kernel, cut), out_shape=(low, low,...  13.9 us
    ppermute x8, waiting for transfers between devices, swapped(): return lax.ppermute(value, axis, pairs)  13.7 us
    ppermute x8, starting transfers between devices, swapped(): return lax.ppermute(value, axis, pairs)  9.63 us
    pallas_call x2, Pallas kernels, merge(): pl.pallas_call(functools.partial(merge_kernel, depth, levels, extra), out...  6.99 us
    pallas_call x1, Pallas kernels, solve(): pl.pallas_call(solve_kernel, out_shape=jax.ShapeDtypeStruct(w_hi.shape, F...  4.45 us
    pallas_call x1, Pallas kernels, finish(): pl.pallas_call(functools.partial(finish_kernel, levels, leaf_count), out_...  4.33 us
  transfers between devices with their start and end apart: 8, of which 5 were waited for; matrix products, arithmetic and copies ran while one was open for 0% of the time, Pallas kernels for 29%

profile of v2, /device:TPU:0, one launch (start us, length us, event | category | flops | bytes accessed | tf_op | source)
XLA Modules:
  0.0 69.5 jit_solution(18123187453467677034)
XLA Ops:
  0.7 3.0 %collective-permute-start = (f32[3,32,1024]{2,1,0:T(8,128)}, f32[3,32,1024]{2,1,0:T(8,128)S(1)}, u32[]{:S(2)}, u32[]{:S(2)}) collective-permute-start(f32[3,32,1024]{2,1,0:T(8,128)} %refs_7_.1), channel_id=1, source_target_pairs={{0,2},{1,3},{2,0},{3,1},{4,6},{5,7},{6,4},{7,5},{8,10},{9,11},{10,... | collective-permute-start | bytes 1179656 | tf_op jit(solution)/shard_map/ppermute | solution.py:570
  3.7 0.0 collective-permute-start.1
  3.7 13.9 %head.1 = (bf16[3,896,128]{2,1,0:T(8,128)(2,1)S(1)}, bf16[3,896,128]{2,1,0:T(8,128)(2,1)S(1)}, bf16[4,256,128]{2,1,0:T(8,128)(2,1)S(1)}, bf16[4,256,128]{2,1,0:T...) custom-call(f32[1024,1024]{1,0:T(8,128)} %blocks.1), custom_call_target="tpu_custom_call" | custom-call | bytes 1048576 | tf_op jit(solution)/shard_map/head/pallas_call | solution.py:176
  17.7 0.0 collective-permute-done.refs_9_
  17.7 0.6 collective-permute-start.2
  18.2 0.6 prepare.1
  18.9 0.0 collective-permute-done.1.refs_8_
  18.9 0.7 collective-permute-done.2.refs_10_
  19.6 14.0 %forward.1 = (f32[768,128]{1,0:T(8,128)S(1)}, f32[104,128]{1,0:T(8,128)S(1)}, f32[488,128]{1,0:T(8,128)S(1)}, bf16[416,1024]{1,0:T(8,128)(2,1)S(1)}, bf16[416,10...) custom-call(bf16[3,896,128]{2,1,0:T(8,128)(2,1)S(1)} %get-tuple-elem, ...), custom_call_target="tpu_custom_call" | custom-call | bytes 1048576 | tf_op jit(solution)/shard_map/forward/pallas_call | solution.py:376
  33.6 1.6 %collective-permute-start.3 = (f32[488,128]{1,0:T(8,128)S(1)}, f32[488,128]{1,0:T(8,128)S(1)}, u32[]{:S(2)}, u32[]{:S(2)}) collective-permute-start(f32[488,128]{1,0:T(8,128)S(1)} %get-tuple-element.56), channel_id=1, source_target_pairs={{0,4},{4,0},{8,12},{12,8},{16,20},{20,16},{24,28},{28,24},{1,5},{5... | collective-permute-start | bytes 749576 | tf_op jit(solution)/shard_map/ppermute | solution.py:570
  35.2 6.8 %collective-permute-done.3.refs_2_ = f32[488,128]{1,0:T(8,128)S(1)} collective-permute-done((f32[488,128]{1,0:T(8,128)S(1)}, f32[488,128]{1,0:T(8,128)S(1)}, u32[]{:S(2)}, u32[]{:S(2)}) %collective-permute-start.3) | collective-permute-done | bytes 249888 | tf_op jit(solution)/shard_map/ppermute | solution.py:570
  42.0 0.1 collective-permute-start.4
  42.1 1.4 %collective-permute-done.4.refs_3_ = f32[384,128]{1,0:T(8,128)S(1)} collective-permute-done((f32[384,128]{1,0:T(8,128)S(1)}, f32[384,128]{1,0:T(8,128)S(1)}, u32[]{:S(2)}, u32[]{:S(2)}) %collective-permute-start.4) | collective-permute-done | bytes 196640 | tf_op jit(solution)/shard_map/ppermute | solution.py:570
  43.5 3.7 %merge.2 = (f32[384,128]{1,0:T(8,128)S(1)}, f32[72,128]{1,0:T(8,128)S(1)}, f32[264,128]{1,0:T(8,128)S(1)}, f32[288,128]{1,0:T(8,128)S(1)}, f32[128,128]{1,0:T(8,128)S(1)}) custom-call(f32[768,128]{1,0:T(8,128)S(1)} %get-tuple-element.54.refs_0_, f32[104,128]{1,0:T(8,128)S(1)} %get-tuple-element.55.refs_1_, f32[488,128]{1,0:T(8,128)S(1)} %collective-permute-done.3.refs_2_, ...), custom_call_target="tpu_custom_call" | custom-call | bytes 1048576 | tf_op jit(solution)/shard_map/merge/pallas_call | solution.py:525
  47.2 1.6 %collective-permute-start.5 = (f32[264,128]{1,0:T(8,128)S(1)}, f32[264,128]{1,0:T(8,128)S(1)}, u32[]{:S(2)}, u32[]{:S(2)}) collective-permute-start(f32[264,128]{1,0:T(8,128)S(1)} %get-tuple-element.62), channel_id=1, source_target_pairs={{0,8},{4,12},{8,0},{12,4},{16,24},{20,28},{24,16},{28,20},{1,9},{5... | collective-permute-start | bytes 405512 | tf_op jit(solution)/shard_map/ppermute | solution.py:570
  48.9 0.6 reduce.2
  49.5 3.4 %collective-permute-done.5.refs_2_ = f32[264,128]{1,0:T(8,128)S(1)} collective-permute-done((f32[264,128]{1,0:T(8,128)S(1)}, f32[264,128]{1,0:T(8,128)S(1)}, u32[]{:S(2)}, u32[]{:S(2)}) %collective-permute-start.5) | collective-permute-done | bytes 135200 | tf_op jit(solution)/shard_map/ppermute | solution.py:570
  52.9 0.1 collective-permute-start.6
  53.0 1.3 %collective-permute-done.6.refs_3_ = f32[192,128]{1,0:T(8,128)S(1)} collective-permute-done((f32[192,128]{1,0:T(8,128)S(1)}, f32[192,128]{1,0:T(8,128)S(1)}, u32[]{:S(2)}, u32[]{:S(2)}) %collective-permute-start.6) | collective-permute-done | bytes 98336 | tf_op jit(solution)/shard_map/ppermute | solution.py:570
  54.3 3.3 %merge.3 = (f32[128,128]{1,0:T(8,128)S(1)}, f32[40,128]{1,0:T(8,128)S(1)}, f32[168,128]{1,0:T(8,128)S(1)}, f32[160,128]{1,0:T(8,128)S(1)}, f32[128,128]{1,0:T(8,128)S(1)}) custom-call(f32[384,128]{1,0:T(8,128)S(1)} %get-tuple-element.60.refs_0_, f32[72,128]{1,0:T(8,128)S(1)} %get-tuple-element.61.refs_1_, f32[264,128]{1,0:T(8,128)S(1)} %collective-permute-done.5.refs_2_, ...), custom_call_target="tpu_custom_call" | custom-call | bytes 1048576 | tf_op jit(solution)/shard_map/merge/pallas_call | solution.py:525
  57.6 2.7 %collective-permute-start.7 = (f32[168,128]{1,0:T(8,128)S(1)}, f32[168,128]{1,0:T(8,128)S(1)}, u32[]{:S(2)}, u32[]{:S(2)}) collective-permute-start(f32[168,128]{1,0:T(8,128)S(1)} %get-tuple-element.72), channel_id=1, source_target_pairs={{0,16},{4,20},{8,24},{12,28},{16,0},{20,4},{24,8},{28,12},{1,17},{... | collective-permute-start | bytes 258056 | tf_op jit(solution)/shard_map/ppermute | solution.py:570
  60.3 0.5 reduce.3
  60.7 4.5 %solve.1.refs_3_ = f32[160,1024]{1,0:T(8,128)S(1)} custom-call(bf16[3,896,128]{2,1,0:T(8,128)(2,1)S(1)} %get-tuple-element.45.refs_0_.head_hi, bf16[3,896,128]{2,1,0:T(8,128)(2,1)S(1)} %get-tuple-element.46.refs_1_.head_lo, bf16[4,256,128]{2,1,0:T(8,128)(2,1)S(1)} %get-tuple-element.47.refs_2_.first_hi, ...), custom_call_target="tpu_custom_call" | custom-call | flops 4000000000 | bytes 1048576 | tf_op jit(solution)/shard_map/solve/pallas_call | solution.py:448
  65.2 4.3 %finish.1 = (f32[32,1024]{1,0:T(8,128)}, f32[1,4]{1,0:T(1,128)}) custom-call(f32[128,128]{1,0:T(8,128)S(1)} %get-tuple-element.70.refs_0_, f32[40,128]{1,0:T(8,128)S(1)} %get-tuple-element.71.refs_1_, f32[168,128]{1,0:T(8,128)S(1)} %collective-permute-done.7.refs_2_, f32[160,1024]{1,0:T(8,128)S(1)} %solve.1.refs_3_), custom_call_target="tpu_custom_call" | custom-call | bytes 1048576 | tf_op jit(solution)/shard_map/finish/pallas_call | solution.py:554
  (11 shorter events, 0.0 us)
Async XLA Ops:
  0.6 19.0 %copy-start = (f32[3,32,1024]{2,1,0:T(8,128)S(1)}, f32[3,32,1024]{2,1,0:T(8,128)}, u32[]{:S(2)}) copy-start(f32[3,32,1024]{2,1,0:T(8,128)} %refs_7_.1) | copy-start | bytes 1179652
  0.6 17.6 %copy-start.3 = (s32[1,1024]{1,0:T(1,128)S(1)}, s32[1,1024]{1,0:T(1,128)}, u32[]{:S(2)}) copy-start(s32[1,1024]{1,0:T(1,128)} %order.1) | copy-start | bytes 12292
  0.7 17.6 %copy-start.2 = (f32[32,1024]{1,0:T(8,128)S(1)}, f32[32,1024]{1,0:T(8,128)}, u32[]{:S(2)}) copy-start(f32[32,1024]{1,0:T(8,128)} %rhs.1) | copy-start | bytes 393220
  0.7 18.9 %copy-start.1 = (s32[3,1]{0,1:T(1,128)S(1)}, s32[3,1]{0,1:T(1,128)}, u32[]{:S(2)}) copy-start(s32[3,1]{0,1:T(1,128)} %param.9) | copy-start | bytes 40
  0.7 17.0 %collective-permute-start = (f32[3,32,1024]{2,1,0:T(8,128)}, f32[3,32,1024]{2,1,0:T(8,128)S(1)}, u32[]{:S(2)}, u32[]{:S(2)}) collective-permute-start(f32[3,32,1024]{2,1,0:T(8,128)} %refs_7_.1), channel_id=1, source_target_pairs={{0,2},{1,3},{2,0},{3,1},{4,6},{5,7},{6,4},{7,5},{8,10},{9,11},{10,... | collective-permute-start | bytes 1179656 | tf_op jit(solution)/shard_map/ppermute | solution.py:570
  3.7 15.2 %collective-permute-start.1 = (f32[3,32,1024]{2,1,0:T(8,128)}, f32[3,32,1024]{2,1,0:T(8,128)S(1)}, u32[]{:S(2)}, u32[]{:S(2)}) collective-permute-start(f32[3,32,1024]{2,1,0:T(8,128)} %refs_7_.1), channel_id=1, source_target_pairs={{0,1},{1,0},{2,3},{3,2},{4,5},{5,4},{6,7},{7,6},{8,9},{9,8},{10,11... | collective-permute-start | bytes 1179656 | tf_op jit(solution)/shard_map/ppermute | solution.py:570
  17.7 1.9 %collective-permute-start.2 = (f32[3,32,1024]{2,1,0:T(8,128)S(1)}, f32[3,32,1024]{2,1,0:T(8,128)S(1)}, u32[]{:S(2)}, u32[]{:S(2)}) collective-permute-start(f32[3,32,1024]{2,1,0:T(8,128)S(1)} %collective-permute-done.refs_9_), channel_id=1, source_target_pairs={{0,1},{1,0},{2,3},{3,2},{4,5},{5,4},{6,7},{7,6},{8,9},{9,8},{10,11... | collective-permute-start | bytes 1179656 | tf_op jit(solution)/shard_map/ppermute | solution.py:570
  33.6 8.4 %collective-permute-start.3 = (f32[488,128]{1,0:T(8,128)S(1)}, f32[488,128]{1,0:T(8,128)S(1)}, u32[]{:S(2)}, u32[]{:S(2)}) collective-permute-start(f32[488,128]{1,0:T(8,128)S(1)} %get-tuple-element.56), channel_id=1, source_target_pairs={{0,4},{4,0},{8,12},{12,8},{16,20},{20,16},{24,28},{28,24},{1,5},{5... | collective-permute-start | bytes 749576 | tf_op jit(solution)/shard_map/ppermute | solution.py:570
  42.0 1.5 %collective-permute-start.4 = (f32[384,128]{1,0:T(8,128)S(1)}, f32[384,128]{1,0:T(8,128)S(1)}, u32[]{:S(2)}, u32[]{:S(2)}) collective-permute-start(f32[384,128]{1,0:T(8,128)S(1)} %slice.6), channel_id=1, source_target_pairs={{0,1},{1,0},{2,3},{3,2},{4,5},{5,4},{6,7},{7,6},{8,9},{9,8},{10,11... | collective-permute-start | bytes 589832 | tf_op jit(solution)/shard_map/ppermute | solution.py:570
  47.2 5.7 %collective-permute-start.5 = (f32[264,128]{1,0:T(8,128)S(1)}, f32[264,128]{1,0:T(8,128)S(1)}, u32[]{:S(2)}, u32[]{:S(2)}) collective-permute-start(f32[264,128]{1,0:T(8,128)S(1)} %get-tuple-element.62), channel_id=1, source_target_pairs={{0,8},{4,12},{8,0},{12,4},{16,24},{20,28},{24,16},{28,20},{1,9},{5... | collective-permute-start | bytes 405512 | tf_op jit(solution)/shard_map/ppermute | solution.py:570
  52.9 1.4 %collective-permute-start.6 = (f32[192,128]{1,0:T(8,128)S(1)}, f32[192,128]{1,0:T(8,128)S(1)}, u32[]{:S(2)}, u32[]{:S(2)}) collective-permute-start(f32[192,128]{1,0:T(8,128)S(1)} %slice.7), channel_id=1, source_target_pairs={{0,1},{1,0},{2,3},{3,2},{4,5},{5,4},{6,7},{7,6},{8,9},{9,8},{10,11... | collective-permute-start | bytes 294920 | tf_op jit(solution)/shard_map/ppermute | solution.py:570
  57.6 7.6 %collective-permute-start.7 = (f32[168,128]{1,0:T(8,128)S(1)}, f32[168,128]{1,0:T(8,128)S(1)}, u32[]{:S(2)}, u32[]{:S(2)}) collective-permute-start(f32[168,128]{1,0:T(8,128)S(1)} %get-tuple-element.72), channel_id=1, source_target_pairs={{0,16},{4,20},{8,24},{12,28},{16,0},{20,4},{24,8},{28,12},{1,17},{... | collective-permute-start | bytes 258056 | tf_op jit(solution)/shard_map/ppermute | solution.py:570

commit v3 on v2

--- a/solution.py
+++ b/solution.py
@@ -33,7 +33,7 @@
     return jnp.broadcast_to(value[row : row + 1, :], (SUB, B))
 
 
-def sweep(rows):
+def sweep(rows, spare):
     lane = lax.broadcasted_iota(jnp.int32, (SUB, B), 1)
     sub = lax.broadcasted_iota(jnp.int32, (SUB, B), 0)
     count = B // SUB
@@ -41,6 +41,23 @@
     rows = list(rows)
     t, rt = [None] * count, [None] * count
     cols = [lanes_of(rows[0], l) for l in range(SUB)]
+
+    def update(group, base, inside, spread):
+        weights = [[] for _ in group]
+        for l in range(SUB):
+            for weight, q in zip(weights, group):
+                weight.append(lanes_of(rows[q], base + l))
+        for weight, q in zip(weights, group):
+            apply(q, inside, spread, weight)
+
+    def apply(q, inside, spread, weight):
+        even = jnp.where(inside, 0.0, rows[q]) - weight[0] * spread[0]
+        odd = weight[1] * spread[1]
+        for l in range(2, SUB, 2):
+            even = even - weight[l] * spread[l]
+            odd = odd + weight[l + 1] * spread[l + 1]
+        rows[q] = even - odd
+
     for p in range(count):
         base = SUB * p
         inside = (lane >= base) & (lane < base + SUB)
@@ -62,24 +79,26 @@
                 cols[l] = cols[l] - scale * across[l]
             panel = panel - scale * row_of(panel, j)
             if following:
+                slot = (p % 2) * SUB + j
+                spare[slot, :SUB, :] = below[j]
                 factor = below[j] * inverse
                 for l in range(SUB):
-                    ahead[l] = ahead[l] - factor * row_of(below[j], l)
+                    ahead[l] = ahead[l] - factor * spare[slot, pl.ds(l, SUB, stride=0), :]
                 for l in range(j + 1, SUB):
                     below[l] = below[l] - factor * across[l]
         rt[p] = jnp.where(upto, panel, 0.0)
         if following:
             spread = [row_of(panel, i) for i in range(SUB)]
-        for q in range(p + 1, count):
-            weight = first if q == p + 1 else [lanes_of(rows[q], base + l) for l in range(SUB)]
-            even = jnp.where(inside, 0.0, rows[q]) - weight[0] * spread[0]
-            odd = weight[1] * spread[1]
-            for l in range(2, SUB, 2):
-                even = even - weight[l] * spread[l]
-                odd = odd + weight[l + 1] * spread[l + 1]
-            rows[q] = even - odd
+            apply(p + 1, inside, spread, first)
+            update(list(range(p + 2, min(p + 3, count))), base, inside, spread)
+            for q in range(p + 3, count, 3):
+                update(list(range(q, min(q + 3, count))), base, inside, spread)
         cols = ahead
     return jnp.concatenate(t + rt, axis=0), pivots
+
+
+def spare_rows():
+    return pltpu.VMEM((2 * SUB, 2 * SUB, B), F32)
 
 
 def rows_from(ref):
@@ -143,7 +162,7 @@
 
 
 def head_kernel(
-    cut, blocks, low_hi, low_lo, tri_hi, tri_lo, logs, work, corner, sems
+    cut, blocks, low_hi, low_lo, tri_hi, tri_lo, logs, work, corner, spare, sems
 ):
     points = work.shape[0]
     whole_copy = pltpu.make_async_copy(blocks, work, sems.at[0])
@@ -151,7 +170,7 @@
     first_copy.start()
     whole_copy.start()
     first_copy.wait()
-    tri, pivots = sweep(rows_from(corner))
+    tri, pivots = sweep(rows_from(corner), spare)
     tri_hi[0], tri_lo[0] = split(tri)
     whole_copy.wait()
 
@@ -160,7 +179,7 @@
             work[B:, :B], work[B : 2 * B, B : 2 * B], (tri_hi[k], tri_lo[k])
         )
         low_hi[k], low_lo[k] = below
-        tri, pivots = sweep(rows)
+        tri, pivots = sweep(rows, spare)
         tri_hi[k + 1], tri_lo[k + 1] = split(tri)
         trail((work, B), (work, 0), mult, below)
         return total + log_sum(pivots)
@@ -185,7 +204,11 @@
         ),
         in_specs=[pl.BlockSpec(memory_space=pltpu.HBM)],
         out_specs=(vmem(),) * 6,
-        scratch_shapes=[pltpu.VMEM((B, B), F32), pltpu.SemaphoreType.DMA((2,))],
+        scratch_shapes=[
+            pltpu.VMEM((B, B), F32),
+            spare_rows(),
+            pltpu.SemaphoreType.DMA((2,)),
+        ],
         **limit(10),
         name="head",
     )(pltpu.with_memory_space_constraint(block, pltpu.HBM))
@@ -208,8 +231,13 @@
 
 
 def halves(levels):
-    shared = sum((levels - entry) * B for entry in range(levels))
-    return shared, shared // 2 if levels > 1 else shared
+    rest = sum((levels - entry) * B for entry in range(levels)) - B
+    return B, rest, B // 2 if levels > 1 else B, rest // 2
+
+
+def half_of(size):
+    start = pl.multiple_of((lax.axis_index("rep") % 2) * size, SUB)
+    return start, pl.multiple_of(size - start, SUB)
 
 
 def gram_tiles(levels, extra):
@@ -249,10 +277,10 @@
 def forward_kernel(levels, size, *refs):
     head_hi, head_lo, first_hi, first_lo, logs, before, ranks = refs[:7]
     pieces = refs[7 : 7 + size]
-    moved, shared, tail, send, w_hi, w_lo, low_hi, low_lo, last_hi, last_lo = refs[
-        7 + size : 17 + size
-    ]
-    work, values, m_hi, m_lo = refs[17 + size :]
+    moved = refs[7 + size]
+    *sends, w_hi, w_lo, low_hi, low_lo, last_hi, last_lo = refs[10 + size : -5]
+    shared, tail = refs[8 + size : 10 + size]
+    work, values, m_hi, m_lo, spare = refs[-5:]
     extra, points = moved.shape
     count = points // B
     cut = head_hi.shape[0]
@@ -321,7 +349,7 @@
             tri_of(at),
         )
         low_hi[base:, base : base + B], low_lo[base:, base : base + B] = below
-        tri, pivots = sweep(rows)
+        tri, pivots = sweep(rows, spare)
         last_hi[at - cut], last_lo[at - cut] = split(tri)
         total = total + log_sum(pivots)
         trail((src, base + B), (work, base + B), mult, below)
@@ -344,23 +372,29 @@
                 tail[entry * extra : (entry + 1) * extra, :] = part[stop - top :]
     lane = lax.broadcasted_iota(jnp.int32, (SUB, B), 1)
     tail[levels * extra :, :] = jnp.where(lane == 0, total / points, 0.0)
-    outgoing(shared, tail, send)
-
-
-def outgoing(shared, tail, send):
-    half = send.shape[0] - tail.shape[0]
-    if half == shared.shape[0]:
-        send[:half, :] = shared[...]
+    outgoing(shared, tail, *sends)
+
+
+def outgoing(shared, tail, *sends):
+    if len(sends) == 1:
+        sends[0][:B, :] = shared[...]
+        sends[0][B:, :] = tail[...]
+        return
+    corner, others = sends
+    corner[...] = shared[pl.ds(half_of(B // 2)[0], B // 2), :]
+    half = others.shape[0] - tail.shape[0]
+    others[:half, :] = shared[pl.ds(B + half_of(half)[0], half), :]
+    others[half:, :] = tail[...]
+
+
+def message_shapes(levels, extra):
+    first, rest, half_first, half_rest = halves(levels)
+    tail = levels * extra + SUB
+    if levels > 1:
+        sends = (half_first, half_rest + tail)
     else:
-        start = pl.multiple_of((lax.axis_index("rep") % 2) * half, SUB)
-        send[:half, :] = shared[pl.ds(start, half), :]
-    send[half:, :] = tail[...]
-
-
-def message_shapes(levels, extra):
-    shared, half = halves(levels)
-    tail = levels * extra + SUB
-    return [jax.ShapeDtypeStruct((rows, B), F32) for rows in (shared, tail, half + tail)]
+        sends = (first + tail,)
+    return [jax.ShapeDtypeStruct((rows, B), F32) for rows in (first + rest, tail, *sends)]
 
 
 def forward(ranks, pieces, moved, factors):
@@ -377,12 +411,13 @@
         functools.partial(forward_kernel, levels, len(pieces)),
         out_shape=(*message_shapes(levels, extra), half, half, low, low, tri, tri),
         in_specs=[vmem()] * (8 + len(pieces)),
-        out_specs=(vmem(),) * 9,
+        out_specs=(vmem(),) * (6 + len(message_shapes(levels, extra))),
         scratch_shapes=[
             pltpu.VMEM((left + B, left + B), F32),
             pltpu.VMEM((rows, points), F32),
             pltpu.VMEM((rows, points), BF16),
             pltpu.VMEM((rows, points), BF16),
+            spare_rows(),
         ],
         **limit(16),
         name="forward",
@@ -456,43 +491,54 @@
     )(*factors, perm, w_hi, w_lo)
 
 
-def eliminate(depth, levels, extra, refs):
-    shared, tail, received, *other, merged, below, corner = refs
-    left = levels - depth
-    whole, half = halves(left)
-    if other:
-        start = pl.multiple_of((lax.axis_index("rep") % 2) * half, SUB)
-        across = pl.multiple_of(half - start, SUB)
-        merged[pl.ds(start, half), :] = shared[pl.ds(start, half), :] + received[:half, :]
-        merged[pl.ds(across, half), :] = shared[pl.ds(across, half), :] + other[0][...]
-    else:
-        merged[...] = shared[...] + received[:half, :]
-    below[...] = tail[...] + received[half:, :]
+def pivot_block(corner, spare):
     row = lax.broadcasted_iota(jnp.int32, (B, B), 0)
     column = lax.broadcasted_iota(jnp.int32, (B, B), 1)
-    corner[...] = merged[:B, :] + jnp.where(row == column, 1.0, 0.0)
-    tri, pivots = sweep(rows_from(corner))
-    lane = lax.broadcasted_iota(jnp.int32, (SUB, B), 1)
-    totals = below[left * extra :, :] + jnp.where(
-        lane == depth + 1, log_sum(pivots) / B, 0.0
-    )
-    pieces = split(tri)
-    panel = join([merged[B : left * B, :], below[:extra, :]], 0) if left > 1 else below[:extra, :]
-    both = product_nt(split(panel), pieces)
-    return pieces, both, totals
+    corner[...] = corner[...] + jnp.where(row == column, 1.0, 0.0)
+    tri, pivots = sweep(rows_from(corner), spare)
+    return split(tri), log_sum(pivots) / B
+
+
+def pivot_kernel(shared, received, other, tri_hi, tri_lo, logs, corner, spare):
+    half = B // 2
+    start, across = half_of(half)
+    corner[pl.ds(start, half), :] = shared[pl.ds(start, half), :] + received[...]
+    corner[pl.ds(across, half), :] = shared[pl.ds(across, half), :] + other[...]
+    (tri_hi[...], tri_lo[...]), log = pivot_block(corner, spare)
+    logs[...] = jnp.broadcast_to(log, logs.shape)
+
+
+def pivot(depth, shared, received, other):
+    tri = jax.ShapeDtypeStruct((2 * B, B), BF16)
+    return pl.pallas_call(
+        pivot_kernel,
+        out_shape=(tri, tri, jax.ShapeDtypeStruct((SUB, B), F32)),
+        in_specs=[vmem()] * 3,
+        out_specs=(vmem(),) * 3,
+        scratch_shapes=[pltpu.VMEM((B, B), F32), spare_rows()],
+        **limit(6, 18 * 10**8 if depth == 0 else 5 * 10**8),
+        name="pivot",
+    )(shared, received, other)
 
 
 def merge_kernel(depth, levels, extra, *refs):
-    inputs = refs[:4]
-    next_shared, next_tail, send, w_out, tri_out = refs[4:9]
-    scratch = refs[9:]
-    merged, below = scratch[:2]
-    pieces, both, totals = eliminate(depth, levels, extra, inputs + scratch)
-    left = levels - depth - 1
+    shared, tail, received, other, tri_hi, tri_lo, logs = refs[:7]
+    next_shared, next_tail = refs[7:9]
+    *sends, w_out, tri_out = refs[9:-2]
+    merged, below = refs[-2:]
+    left = levels - depth
+    half = halves(left)[3]
+    start, across = half_of(half)
+    merged[pl.ds(start, half), :] = shared[pl.ds(B + start, half), :] + received[:half, :]
+    merged[pl.ds(across, half), :] = shared[pl.ds(B + across, half), :] + other[...]
+    below[...] = tail[...] + received[half:, :]
+    left -= 1
+    panel = join([merged[: left * B, :], below[:extra, :]], 0)
+    both = product_nt(split(panel), (tri_hi[...], tri_lo[...]))
     w_parts = split(both[:, :B])
     m_parts = split(both[:, B:])
     w_out[...] = both[:, :B]
-    tri_out[...] = pieces[0][B:].astype(F32) + pieces[1][B:].astype(F32)
+    tri_out[...] = tri_hi[B:, :].astype(F32) + tri_lo[B:, :].astype(F32)
     at = 0
     for entry in range(left):
         top = entry * B
@@ -501,52 +547,54 @@
             tuple(part[top:] for part in m_parts),
             tuple(part[top : top + B] for part in w_parts),
         )
-        base = (left + 1) * B + at
+        base = left * B + at
         next_shared[at : at + rows, :] = merged[base : base + rows, :] - change[:rows]
         next_tail[entry * extra : (entry + 1) * extra, :] = (
             below[(entry + 1) * extra : (entry + 2) * extra, :] - change[rows:]
         )
         at += rows
-    next_tail[left * extra :, :] = totals
-    outgoing(next_shared, next_tail, send)
-
-
-def scratch_for(levels, extra):
-    shared, tail, _ = message_shapes(levels, extra)
-    return [
-        pltpu.VMEM(shared.shape, F32),
-        pltpu.VMEM(tail.shape, F32),
-        pltpu.VMEM((B, B), F32),
-    ]
-
-
-def merge(depth, levels, extra, message):
+    lane = lax.broadcasted_iota(jnp.int32, (SUB, B), 1)
+    next_tail[left * extra :, :] = below[(left + 1) * extra :, :] + jnp.where(
+        lane == depth + 1, logs[...], 0.0
+    )
+    outgoing(next_shared, next_tail, *sends)
+
+
+def merge(depth, levels, extra, arrived):
     left = levels - depth
+    messages = message_shapes(left - 1, extra)
     return pl.pallas_call(
         functools.partial(merge_kernel, depth, levels, extra),
         out_shape=(
-            *message_shapes(left - 1, extra),
+            *messages,
             jax.ShapeDtypeStruct(((left - 1) * B + extra, B), F32),
             jax.ShapeDtypeStruct((B, B), F32),
         ),
-        in_specs=[vmem()] * 4,
-        out_specs=(vmem(),) * 5,
-        scratch_shapes=scratch_for(left, extra),
+        in_specs=[vmem()] * 7,
+        out_specs=(vmem(),) * (2 + len(messages)),
+        scratch_shapes=[
+            pltpu.VMEM((halves(left)[1], B), F32),
+            pltpu.VMEM((left * extra + SUB, B), F32),
+        ],
         **limit(6),
         name="merge",
-    )(*message)
-
-
-def finish_kernel(levels, leaf_count, *refs):
-    solved, out, means = refs[3:6]
+    )(*arrived)
+
+
+def finish_kernel(levels, leaf_count, shared, tail, received, solved, out, means, corner, spare):
     extra = out.shape[0]
-    pieces, both, totals = eliminate(levels - 1, levels, extra, refs[:3] + refs[6:])
-    coeffs = split(product_nn(split(both[:, :B]), tuple(part[B:] for part in pieces)))
+    corner[...] = shared[...] + received[:B, :]
+    tri, log = pivot_block(corner, spare)
+    below = tail[...] + received[B:, :]
+    target = product_nt(split(below[:extra]), tuple(part[:B] for part in tri))
+    coeffs = split(product_nn(split(target), tuple(part[B:] for part in tri)))
     out[...] = solved[B:, :] - product_nn(coeffs, split(solved[:B, :]))
+    totals = below[extra:]
     lane = lax.broadcasted_iota(jnp.int32, (SUB, B), 1)
     scale = jnp.zeros((SUB, B), F32)
     for entry in range(levels + 1):
         scale = jnp.where(lane == entry, 2.0**entry / leaf_count, scale)
+    totals = totals + jnp.where(lane == levels, log, 0.0)
     means[...] = (totals * scale)[:1, : levels + 1]
 
 
@@ -559,7 +607,7 @@
         ),
         in_specs=[vmem()] * 4,
         out_specs=(vmem(),) * 2,
-        scratch_shapes=scratch_for(1, extra),
+        scratch_shapes=[pltpu.VMEM((B, B), F32), spare_rows()],
         **limit(6),
         name="finish",
     )(*message, solved)
@@ -570,16 +618,16 @@
     return lax.ppermute(value, axis, pairs)
 
 
-def exchange(message, depth, left, meanwhile=None):
-    shared, tail, send = message
-    received = swapped(send, "leaf", 2**depth)
-    done = None
-    if meanwhile is not None:
-        received, done = lax.optimization_barrier((received, meanwhile()))
-    if send.shape[0] == shared.shape[0] + tail.shape[0]:
-        return (shared, tail, received), done
-    other = swapped(received[: halves(left)[1]], "rep", 1)
-    return (shared, tail, received, other), done
+def exchange(message, depth, left, meanwhile):
+    shared, tail, *sends = message
+    received = [swapped(send, "leaf", 2**depth) for send in sends]
+    received[0], done = lax.optimization_barrier((received[0], meanwhile()))
+    if len(sends) == 1:
+        return (shared, tail, received[0]), done
+    tri = pivot(depth, shared, received[0], swapped(received[0], "rep", 1))
+    late, tri = lax.optimization_barrier((received[1], tri))
+    other = swapped(late[: halves(left)[3]], "rep", 1)
+    return (shared, tail, late, other, *tri), done
 
 
 def shards(leaf_blocks, generators, rhs, order, ranks):

time: 69.7 us -> 66.4 us (0.953)
  waiting for transfers between devices: 13.7 us -> 9.63 us
  starting transfers between devices: 9.63 us -> 10.8 us
    pallas_call x2, Pallas kernels: 6.99 us -> 1.06 us  [merge(): pl.pallas_call(functools.partial(merge_kernel, depth, levels, extra), out...]
    pallas_call x0 -> x2, Pallas kernels: none -> 5.58 us  [pivot(): pl.pallas_call(pivot_kernel, out_shape=(tri, tri, jax.ShapeDtypeStruct((S...]
    ppermute x8 -> x12, waiting for transfers between devices: 13.7 us -> 9.63 us  [swapped(): return lax.ppermute(value, axis, pairs)]
    ppermute x8 -> x12, starting transfers between devices: 9.63 us -> 10.8 us  [swapped(): return lax.ppermute(value, axis, pairs)]
  transfers between devices with their start and end apart: 8 -> 12, of which waited for: 5 -> 8; matrix products, arithmetic and copies ran while one was open for 0% -> 0% of each run, Pallas kernels for 29% -> 39%
where the time goes in v3:
time: 66.4 us; the launch traced here: 66.3 us
  Pallas kernels  45.1 us (68%)
  starting transfers between devices  10.8 us (16%)
  waiting for transfers between devices  9.63 us (15%)
  between operations  0.76 us (1%)
    pallas_call x1, Pallas kernels, forward(): pl.pallas_call(functools.partial(forward_kernel, levels, len(pieces)), ou...  14.1 us
    pallas_call x1, Pallas kernels, head(): pl.pallas_call(functools.partial(head_kernel, cut), out_shape=(low, low,...  14 us
    ppermute x12, starting transfers between devices, swapped(): return lax.ppermute(value, axis, pairs)  10.8 us
    ppermute x12, waiting for transfers between devices, swapped(): return lax.ppermute(value, axis, pairs)  9.63 us
    pallas_call x2, Pallas kernels, pivot(): pl.pallas_call(pivot_kernel, out_shape=(tri, tri, jax.ShapeDtypeStruct((S...  5.58 us
    pallas_call x1, Pallas kernels, solve(): pl.pallas_call(solve_kernel, out_shape=jax.ShapeDtypeStruct(w_hi.shape, F...  4.45 us
    pallas_call x1, Pallas kernels, finish(): pl.pallas_call(functools.partial(finish_kernel, levels, leaf_count), out_...  4.14 us
  transfers between devices with their start and end apart: 12, of which 8 were waited for; matrix products, arithmetic and copies ran while one was open for 0% of the time, Pallas kernels for 39%

profile of v3, /device:TPU:0, one launch (start us, length us, event | category | flops | bytes accessed | tf_op | source)
XLA Modules:
  0.0 66.3 jit_solution(3551965909348887222)
XLA Ops:
  0.7 3.0 %collective-permute-start = (f32[3,32,1024]{2,1,0:T(8,128)}, f32[3,32,1024]{2,1,0:T(8,128)S(1)}, u32[]{:S(2)}, u32[]{:S(2)}) collective-permute-start(f32[3,32,1024]{2,1,0:T(8,128)} %refs_7_.1), channel_id=1, source_target_pairs={{0,2},{1,3},{2,0},{3,1},{4,6},{5,7},{6,4},{7,5},{8,10},{9,11},{10,... | collective-permute-start | bytes 1179656 | tf_op jit(solution)/shard_map/ppermute | solution.py:618
  3.7 14.0 %head.1 = (bf16[3,896,128]{2,1,0:T(8,128)(2,1)S(1)}, bf16[3,896,128]{2,1,0:T(8,128)(2,1)S(1)}, bf16[4,256,128]{2,1,0:T(8,128)(2,1)S(1)}, bf16[4,256,128]{2,1,0:T...) custom-call(f32[1024,1024]{1,0:T(8,128)} %blocks.1), custom_call_target="tpu_custom_call" | custom-call | bytes 1048576 | tf_op jit(solution)/shard_map/head/pallas_call | solution.py:195
  17.7 0.6 collective-permute-start.2
  18.3 0.6 prepare.1
  19.0 0.7 %collective-permute-done.2.refs_10_ = f32[3,32,1024]{2,1,0:T(8,128)S(1)} collective-permute-done((f32[3,32,1024]{2,1,0:T(8,128)S(1)}, f32[3,32,1024]{2,1,0:T(8,128)S(1)}, u32[]{:S(2)}, u32[]{:S(2)}) %collective-permute-start.2) | collective-permute-done | bytes 393248 | tf_op jit(solution)/shard_map/ppermute | solution.py:618
  19.7 14.1 %forward.1 = (f32[768,128]{1,0:T(8,128)S(1)}, f32[104,128]{1,0:T(8,128)S(1)}, f32[64,128]{1,0:T(8,128)S(1)}, f32[424,128]{1,0:T(8,128)S(1)}, bf16[416,1024]{1,0:...) custom-call(bf16[3,896,128]{2,1,0:T(8,128)(2,1)S(1)} %get-tuple-elem, ...), custom_call_target="tpu_custom_call" | custom-call | bytes 1048576 | tf_op jit(solution)/shard_map/forward/pallas_call | solution.py:410
  33.8 1.6 %collective-permute-start.4 = (f32[64,128]{1,0:T(8,128)S(1)}, f32[64,128]{1,0:T(8,128)S(1)}, u32[]{:S(2)}, u32[]{:S(2)}) collective-permute-start(f32[64,128]{1,0:T(8,128)S(1)} %get-tuple-element.73), channel_id=1, source_target_pairs={{0,4},{4,0},{8,12},{12,8},{16,20},{20,16},{24,28},{28,24},{1,5},{5... | collective-permute-start | bytes 98312 | tf_op jit(solution)/shard_map/ppermute | solution.py:618
  35.3 0.5 collective-permute-start.3
  35.9 1.9 %collective-permute-done.4.received = f32[64,128]{1,0:T(8,128)S(1)} collective-permute-done((f32[64,128]{1,0:T(8,128)S(1)}, f32[64,128]{1,0:T(8,128)S(1)}, u32[]{:S(2)}, u32[]{:S(2)}) %collective-permute-start.4) | collective-permute-done | bytes 32800 | tf_op jit(solution)/shard_map/ppermute | solution.py:618
  37.8 1.2 %collective-permute-done.5.other = f32[64,128]{1,0:T(8,128)S(1)} collective-permute-done((f32[64,128]{1,0:T(8,128)S(1)}, f32[64,128]{1,0:T(8,128)S(1)}, u32[]{:S(2)}, u32[]{:S(2)}) %collective-permute-start.5) | collective-permute-done | bytes 32800 | tf_op jit(solution)/shard_map/ppermute | solution.py:618
  39.0 2.8 %pivot.2 = (bf16[256,128]{1,0:T(8,128)(2,1)S(1)}, bf16[256,128]{1,0:T(8,128)(2,1)S(1)}, f32[8,128]{1,0:T(8,128)S(1)}) custom-call(f32[768,128]{1,0:T(8,128)S(1)} %get-tuple-element.70.shared.refs_0_, f32[64,128]{1,0:T(8,128)S(1)} %collective-permute-done.4.received, f32[64,128]{1,0:T(8,128)S(1)} %collective-permute-done.5.other), custom_call_target="tpu_custom_call" | custom-call | flops 1800000000 | bytes 1048576 | tf_op jit(solution)/shard_map/pivot/pallas_call | solution.py:513
  41.8 0.9 %collective-permute-done.3.refs_2_ = f32[424,128]{1,0:T(8,128)S(1)} collective-permute-done((f32[424,128]{1,0:T(8,128)S(1)}, f32[424,128]{1,0:T(8,128)S(1)}, u32[]{:S(2)}, u32[]{:S(2)}) %collective-permute-start.3) | collective-permute-done | bytes 217120 | tf_op jit(solution)/shard_map/ppermute | solution.py:618
  42.8 1.4 %collective-permute-done.6.refs_3_ = f32[320,128]{1,0:T(8,128)S(1)} collective-permute-done((f32[320,128]{1,0:T(8,128)S(1)}, f32[320,128]{1,0:T(8,128)S(1)}, u32[]{:S(2)}, u32[]{:S(2)}) %collective-permute-start.6) | collective-permute-done | bytes 163872 | tf_op jit(solution)/shard_map/ppermute | solution.py:618
  44.1 0.6 merge.2
  44.8 1.6 %collective-permute-start.8 = (f32[64,128]{1,0:T(8,128)S(1)}, f32[64,128]{1,0:T(8,128)S(1)}, u32[]{:S(2)}, u32[]{:S(2)}) collective-permute-start(f32[64,128]{1,0:T(8,128)S(1)} %get-tuple-element.87), channel_id=1, source_target_pairs={{0,8},{4,12},{8,0},{12,4},{16,24},{20,28},{24,16},{28,20},{1,9},{5... | collective-permute-start | bytes 98312 | tf_op jit(solution)/shard_map/ppermute | solution.py:618
  46.8 0.6 reduce.2
  47.5 1.2 %collective-permute-done.8.received = f32[64,128]{1,0:T(8,128)S(1)} collective-permute-done((f32[64,128]{1,0:T(8,128)S(1)}, f32[64,128]{1,0:T(8,128)S(1)}, u32[]{:S(2)}, u32[]{:S(2)}) %collective-permute-start.8) | collective-permute-done | bytes 32800 | tf_op jit(solution)/shard_map/ppermute | solution.py:618
  48.7 1.2 %collective-permute-done.9.other = f32[64,128]{1,0:T(8,128)S(1)} collective-permute-done((f32[64,128]{1,0:T(8,128)S(1)}, f32[64,128]{1,0:T(8,128)S(1)}, u32[]{:S(2)}, u32[]{:S(2)}) %collective-permute-start.9) | collective-permute-done | bytes 32800 | tf_op jit(solution)/shard_map/ppermute | solution.py:618
  49.9 2.8 %pivot.3 = (bf16[256,128]{1,0:T(8,128)(2,1)S(1)}, bf16[256,128]{1,0:T(8,128)(2,1)S(1)}, f32[8,128]{1,0:T(8,128)S(1)}) custom-call(f32[384,128]{1,0:T(8,128)S(1)} %get-tuple-element.84.shared.refs_0_, f32[64,128]{1,0:T(8,128)S(1)} %collective-permute-done.8.received, f32[64,128]{1,0:T(8,128)S(1)} %collective-permute-done.9.other), custom_call_target="tpu_custom_call" | custom-call | flops 500000000 | bytes 1048576 | tf_op jit(solution)/shard_map/pivot/pallas_call | solution.py:513
  53.0 1.1 %collective-permute-done.10.refs_3_ = f32[128,128]{1,0:T(8,128)S(1)} collective-permute-done((f32[128,128]{1,0:T(8,128)S(1)}, f32[128,128]{1,0:T(8,128)S(1)}, u32[]{:S(2)}, u32[]{:S(2)}) %collective-permute-start.10) | collective-permute-done | bytes 65568 | tf_op jit(solution)/shard_map/ppermute | solution.py:618
  54.5 2.7 %collective-permute-start.11 = (f32[168,128]{1,0:T(8,128)S(1)}, f32[168,128]{1,0:T(8,128)S(1)}, u32[]{:S(2)}, u32[]{:S(2)}) collective-permute-start(f32[168,128]{1,0:T(8,128)S(1)} %get-tuple-element.104), channel_id=1, source_target_pairs={{0,16},{4,20},{8,24},{12,28},{16,0},{20,4},{24,8},{28,12},{1,17},{... | collective-permute-start | bytes 258056 | tf_op jit(solution)/shard_map/ppermute | solution.py:618
  57.2 0.5 reduce.3
  57.7 4.5 %solve.1.solved = f32[160,1024]{1,0:T(8,128)S(1)} custom-call(bf16[3,896,128]{2,1,0:T(8,128)(2,1)S(1)} %get-tuple-element.61.refs_0_.head_hi, bf16[3,896,128]{2,1,0:T(8,128)(2,1)S(1)} %get-tuple-element.62.refs_1_.head_lo, bf16[4,256,128]{2,1,0:T(8,128)(2,1)S(1)} %get-tuple-element.63.refs_2_.first_hi, ...), custom_call_target="tpu_custom_call" | custom-call | flops 4000000000 | bytes 1048576 | tf_op jit(solution)/shard_map/solve/pallas_call | solution.py:483
  62.2 4.1 %finish.1 = (f32[32,1024]{1,0:T(8,128)}, f32[1,4]{1,0:T(1,128)}) custom-call(f32[128,128]{1,0:T(8,128)S(1)} %get-tuple-element.102.shared, f32[40,128]{1,0:T(8,128)S(1)} %get-tuple-element.103.tail, f32[168,128]{1,0:T(8,128)S(1)} %collective-permute-done.11.received, f32[160,1024]{1,0:T(8,128)S(1)} %solve.1.solved), custom_call_target="tpu_custom_call" | custom-call | bytes 1048576 | tf_op jit(solution)/shard_map/finish/pallas_call | solution.py:602
  (21 shorter events, 1.3 us)
Async XLA Ops:
  0.6 19.0 %copy-start = (f32[3,32,1024]{2,1,0:T(8,128)S(1)}, f32[3,32,1024]{2,1,0:T(8,128)}, u32[]{:S(2)}) copy-start(f32[3,32,1024]{2,1,0:T(8,128)} %refs_7_.1) | copy-start | bytes 1179652
  0.6 17.7 %copy-start.3 = (s32[1,1024]{1,0:T(1,128)S(1)}, s32[1,1024]{1,0:T(1,128)}, u32[]{:S(2)}) copy-start(s32[1,1024]{1,0:T(1,128)} %order.1) | copy-start | bytes 12292
  0.7 17.7 %copy-start.2 = (f32[32,1024]{1,0:T(8,128)S(1)}, f32[32,1024]{1,0:T(8,128)}, u32[]{:S(2)}) copy-start(f32[32,1024]{1,0:T(8,128)} %rhs.1) | copy-start | bytes 393220
  0.7 19.0 %copy-start.1 = (s32[3,1]{0,1:T(1,128)S(1)}, s32[3,1]{0,1:T(1,128)}, u32[]{:S(2)}) copy-start(s32[3,1]{0,1:T(1,128)} %param.9) | copy-start | bytes 40
  0.7 17.1 %collective-permute-start = (f32[3,32,1024]{2,1,0:T(8,128)}, f32[3,32,1024]{2,1,0:T(8,128)S(1)}, u32[]{:S(2)}, u32[]{:S(2)}) collective-permute-start(f32[3,32,1024]{2,1,0:T(8,128)} %refs_7_.1), channel_id=1, source_target_pairs={{0,2},{1,3},{2,0},{3,1},{4,6},{5,7},{6,4},{7,5},{8,10},{9,11},{10,... | collective-permute-start | bytes 1179656 | tf_op jit(solution)/shard_map/ppermute | solution.py:618
  3.7 15.3 %collective-permute-start.1 = (f32[3,32,1024]{2,1,0:T(8,128)}, f32[3,32,1024]{2,1,0:T(8,128)S(1)}, u32[]{:S(2)}, u32[]{:S(2)}) collective-permute-start(f32[3,32,1024]{2,1,0:T(8,128)} %refs_7_.1), channel_id=1, source_target_pairs={{0,1},{1,0},{2,3},{3,2},{4,5},{5,4},{6,7},{7,6},{8,9},{9,8},{10,11... | collective-permute-start | bytes 1179656 | tf_op jit(solution)/shard_map/ppermute | solution.py:618
  17.7 1.9 %collective-permute-start.2 = (f32[3,32,1024]{2,1,0:T(8,128)S(1)}, f32[3,32,1024]{2,1,0:T(8,128)S(1)}, u32[]{:S(2)}, u32[]{:S(2)}) collective-permute-start(f32[3,32,1024]{2,1,0:T(8,128)S(1)} %collective-permute-done.refs_9_), channel_id=1, source_target_pairs={{0,1},{1,0},{2,3},{3,2},{4,5},{5,4},{6,7},{7,6},{8,9},{9,8},{10,11... | collective-permute-start | bytes 1179656 | tf_op jit(solution)/shard_map/ppermute | solution.py:618
  33.8 4.0 %collective-permute-start.4 = (f32[64,128]{1,0:T(8,128)S(1)}, f32[64,128]{1,0:T(8,128)S(1)}, u32[]{:S(2)}, u32[]{:S(2)}) collective-permute-start(f32[64,128]{1,0:T(8,128)S(1)} %get-tuple-element.73), channel_id=1, source_target_pairs={{0,4},{4,0},{8,12},{12,8},{16,20},{20,16},{24,28},{28,24},{1,5},{5... | collective-permute-start | bytes 98312 | tf_op jit(solution)/shard_map/ppermute | solution.py:618
  35.3 7.3 %collective-permute-start.3 = (f32[424,128]{1,0:T(8,128)S(1)}, f32[424,128]{1,0:T(8,128)S(1)}, u32[]{:S(2)}, u32[]{:S(2)}) collective-permute-start(f32[424,128]{1,0:T(8,128)S(1)} %get-tuple-element.72), channel_id=1, source_target_pairs={{0,4},{4,0},{8,12},{12,8},{16,20},{20,16},{24,28},{28,24},{1,5},{5... | collective-permute-start | bytes 651272 | tf_op jit(solution)/shard_map/ppermute | solution.py:618
  37.8 1.2 %collective-permute-start.5 = (f32[64,128]{1,0:T(8,128)S(1)}, f32[64,128]{1,0:T(8,128)S(1)}, u32[]{:S(2)}, u32[]{:S(2)}) collective-permute-start(f32[64,128]{1,0:T(8,128)S(1)} %collective-permute-done.4.received), channel_id=1, source_target_pairs={{0,1},{1,0},{2,3},{3,2},{4,5},{5,4},{6,7},{7,6},{8,9},{9,8},{10,11... | collective-permute-start | bytes 98312 | tf_op jit(solution)/shard_map/ppermute | solution.py:618
  42.7 1.5 %collective-permute-start.6 = (f32[320,128]{1,0:T(8,128)S(1)}, f32[320,128]{1,0:T(8,128)S(1)}, u32[]{:S(2)}, u32[]{:S(2)}) collective-permute-start(f32[320,128]{1,0:T(8,128)S(1)} %slice.6), channel_id=1, source_target_pairs={{0,1},{1,0},{2,3},{3,2},{4,5},{5,4},{6,7},{7,6},{8,9},{9,8},{10,11... | collective-permute-start | bytes 491528 | tf_op jit(solution)/shard_map/ppermute | solution.py:618
  44.8 4.0 %collective-permute-start.8 = (f32[64,128]{1,0:T(8,128)S(1)}, f32[64,128]{1,0:T(8,128)S(1)}, u32[]{:S(2)}, u32[]{:S(2)}) collective-permute-start(f32[64,128]{1,0:T(8,128)S(1)} %get-tuple-element.87), channel_id=1, source_target_pairs={{0,8},{4,12},{8,0},{12,4},{16,24},{20,28},{24,16},{28,20},{1,9},{5... | collective-permute-start | bytes 98312 | tf_op jit(solution)/shard_map/ppermute | solution.py:618
  46.4 6.3 %collective-permute-start.7 = (f32[200,128]{1,0:T(8,128)S(1)}, f32[200,128]{1,0:T(8,128)S(1)}, u32[]{:S(2)}, u32[]{:S(2)}) collective-permute-start(f32[200,128]{1,0:T(8,128)S(1)} %get-tuple-element.86), channel_id=1, source_target_pairs={{0,8},{4,12},{8,0},{12,4},{16,24},{20,28},{24,16},{28,20},{1,9},{5... | collective-permute-start | bytes 307208 | tf_op jit(solution)/shard_map/ppermute | solution.py:618
  48.7 1.2 %collective-permute-start.9 = (f32[64,128]{1,0:T(8,128)S(1)}, f32[64,128]{1,0:T(8,128)S(1)}, u32[]{:S(2)}, u32[]{:S(2)}) collective-permute-start(f32[64,128]{1,0:T(8,128)S(1)} %collective-permute-done.8.received), channel_id=1, source_target_pairs={{0,1},{1,0},{2,3},{3,2},{4,5},{5,4},{6,7},{7,6},{8,9},{9,8},{10,11... | collective-permute-start | bytes 98312 | tf_op jit(solution)/shard_map/ppermute | solution.py:618
  52.8 1.3 %collective-permute-start.10 = (f32[128,128]{1,0:T(8,128)S(1)}, f32[128,128]{1,0:T(8,128)S(1)}, u32[]{:S(2)}, u32[]{:S(2)}) collective-permute-start(f32[128,128]{1,0:T(8,128)S(1)} %slice.7), channel_id=1, source_target_pairs={{0,1},{1,0},{2,3},{3,2},{4,5},{5,4},{6,7},{7,6},{8,9},{9,8},{10,11... | collective-permute-start | bytes 196616 | tf_op jit(solution)/shard_map/ppermute | solution.py:618
  54.5 7.6 %collective-permute-start.11 = (f32[168,128]{1,0:T(8,128)S(1)}, f32[168,128]{1,0:T(8,128)S(1)}, u32[]{:S(2)}, u32[]{:S(2)}) collective-permute-start(f32[168,128]{1,0:T(8,128)S(1)} %get-tuple-element.104), channel_id=1, source_target_pairs={{0,16},{4,20},{8,24},{12,28},{16,0},{20,4},{24,8},{28,12},{1,17},{... | collective-permute-start | bytes 258056 | tf_op jit(solution)/shard_map/ppermute | solution.py:618

commit v4 on v3

--- a/solution.py
+++ b/solution.py
@@ -232,7 +232,9 @@
 
 def halves(levels):
     rest = sum((levels - entry) * B for entry in range(levels)) - B
-    return B, rest, B // 2 if levels > 1 else B, rest // 2
+    if levels > 2:
+        return B, rest, B // 2, rest // 2
+    return B, rest, B, rest
 
 
 def half_of(size):
@@ -381,9 +383,13 @@
         sends[0][B:, :] = tail[...]
         return
     corner, others = sends
-    corner[...] = shared[pl.ds(half_of(B // 2)[0], B // 2), :]
     half = others.shape[0] - tail.shape[0]
-    others[:half, :] = shared[pl.ds(B + half_of(half)[0], half), :]
+    if corner.shape[0] == B:
+        corner[...] = shared[:B, :]
+        others[:half, :] = shared[B:, :]
+    else:
+        corner[...] = shared[pl.ds(half_of(B // 2)[0], B // 2), :]
+        others[:half, :] = shared[pl.ds(B + half_of(half)[0], half), :]
     others[half:, :] = tail[...]
 
 
@@ -446,14 +452,11 @@
     )(w_panel, tri, w_hi, w_lo)
 
 
-def solve_kernel(
-    head_hi, head_lo, first_hi, first_lo, low_hi, low_lo, last_hi, last_lo, perm,
-    w_hi, w_lo, out, v_hi, v_mid, v_last,
-):
+def solve_blocks(first, last, factors, w_hi, w_lo, v):
+    head_hi, head_lo, first_hi, first_lo, low_hi, low_lo, last_hi, last_lo = factors
     points = w_hi.shape[1]
-    count = points // B
     cut = head_hi.shape[0]
-    for k in reversed(range(count)):
+    for k in reversed(range(first, last)):
         start, end = k * B, (k + 1) * B
         here = w_hi[:, start:end].astype(F32) + w_lo[:, start:end].astype(F32)
         for left, right in ((end + B, points), (end, min(end + B, points))):
@@ -466,22 +469,50 @@
                 rows = slice(left - (cut + 1) * B, right - (cut + 1) * B)
                 columns = slice((k - cut) * B, (k - cut + 1) * B)
                 below = low_hi[rows, columns], low_lo[rows, columns]
-            here = here - product_nn((v_hi[:, left:right], v_mid[:, left:right]), below)
+            here = here - product_nn((v[0][:, left:right], v[1][:, left:right]), below)
         if k <= cut:
             tri = first_hi[k, B:, :], first_lo[k, B:, :]
         else:
             tri = last_hi[k - cut - 1, B:, :], last_lo[k - cut - 1, B:, :]
-        parts = thirds(product_nn(split(here), tri))
-        v_hi[:, start:end], v_mid[:, start:end], v_last[:, start:end] = parts
+        for ref, part in zip(v, thirds(product_nn(split(here), tri))):
+            ref[:, start:end] = part
+
+
+def begin_kernel(ahead, *refs):
+    factors, (w_hi, w_lo), v = refs[:8], refs[8:10], refs[10:12]
+    points = w_hi.shape[1]
+    stop = points - ahead * B
+    solve_blocks(stop // B, points // B, factors, w_hi, w_lo, v)
+    v[0][:, :stop] = w_hi[:, :stop]
+    v[1][:, :stop] = w_lo[:, :stop]
+
+
+def begin(ahead, factors, w_hi, w_lo):
+    return pl.pallas_call(
+        functools.partial(begin_kernel, ahead),
+        out_shape=(jax.ShapeDtypeStruct(w_hi.shape, BF16),) * 2,
+        in_specs=[vmem()] * 10,
+        out_specs=(vmem(),) * 2,
+        **limit(8, 10**8),
+        name="begin",
+    )(*factors, w_hi, w_lo)
+
+
+def solve_kernel(ahead, *refs):
+    factors, (perm, w_hi, w_lo, out), v = refs[:8], refs[8:12], refs[12:]
+    points = w_hi.shape[1]
+    stop = points - ahead * B
+    v[0][:, stop:] = w_hi[:, stop:]
+    v[1][:, stop:] = w_lo[:, stop:]
+    solve_blocks(0, stop // B, factors, w_hi, w_lo, v)
     sensors = perm[...]
-    out[...] = dot_nt(v_hi[...], sensors) + (
-        dot_nt(v_mid[...], sensors) + dot_nt(v_last[...], sensors)
-    )
-
-
-def solve(factors, perm, w_hi, w_lo):
-    return pl.pallas_call(
-        solve_kernel,
+    last = dot_nt(v[2][:, :stop], perm[:, :stop])
+    out[...] = dot_nt(v[0][...], sensors) + (dot_nt(v[1][...], sensors) + last)
+
+
+def solve(ahead, factors, perm, w_hi, w_lo):
+    return pl.pallas_call(
+        functools.partial(solve_kernel, ahead),
         out_shape=jax.ShapeDtypeStruct(w_hi.shape, F32),
         in_specs=[vmem()] * (3 + len(factors)),
         out_specs=vmem(),
@@ -499,38 +530,46 @@
     return split(tri), log_sum(pivots) / B
 
 
-def pivot_kernel(shared, received, other, tri_hi, tri_lo, logs, corner, spare):
-    half = B // 2
+def add_halves(out, shared, skip, received, other):
+    if not other:
+        out[...] = shared[skip : skip + out.shape[0], :] + received
+        return
+    half = out.shape[0] // 2
     start, across = half_of(half)
-    corner[pl.ds(start, half), :] = shared[pl.ds(start, half), :] + received[...]
-    corner[pl.ds(across, half), :] = shared[pl.ds(across, half), :] + other[...]
+    out[pl.ds(start, half), :] = shared[pl.ds(skip + start, half), :] + received
+    out[pl.ds(across, half), :] = shared[pl.ds(skip + across, half), :] + other[0][...]
+
+
+def pivot_kernel(shared, received, *refs):
+    *other, tri_hi, tri_lo, logs, corner, spare = refs
+    add_halves(corner, shared, 0, received[...], other)
     (tri_hi[...], tri_lo[...]), log = pivot_block(corner, spare)
     logs[...] = jnp.broadcast_to(log, logs.shape)
 
 
-def pivot(depth, shared, received, other):
+def pivot(depth, shared, *received):
     tri = jax.ShapeDtypeStruct((2 * B, B), BF16)
     return pl.pallas_call(
         pivot_kernel,
         out_shape=(tri, tri, jax.ShapeDtypeStruct((SUB, B), F32)),
-        in_specs=[vmem()] * 3,
+        in_specs=[vmem()] * (1 + len(received)),
         out_specs=(vmem(),) * 3,
         scratch_shapes=[pltpu.VMEM((B, B), F32), spare_rows()],
         **limit(6, 18 * 10**8 if depth == 0 else 5 * 10**8),
         name="pivot",
-    )(shared, received, other)
+    )(shared, *received)
 
 
 def merge_kernel(depth, levels, extra, *refs):
-    shared, tail, received, other, tri_hi, tri_lo, logs = refs[:7]
-    next_shared, next_tail = refs[7:9]
-    *sends, w_out, tri_out = refs[9:-2]
+    left = levels - depth
+    split_up = int(left > 2)
+    shared, tail, received = refs[:3]
+    other = refs[3 : 3 + split_up]
+    tri_hi, tri_lo, logs, next_shared, next_tail = refs[3 + split_up : 8 + split_up]
+    *sends, w_out, tri_out = refs[8 + split_up : -2]
     merged, below = refs[-2:]
-    left = levels - depth
     half = halves(left)[3]
-    start, across = half_of(half)
-    merged[pl.ds(start, half), :] = shared[pl.ds(B + start, half), :] + received[:half, :]
-    merged[pl.ds(across, half), :] = shared[pl.ds(B + across, half), :] + other[...]
+    add_halves(merged, shared, B, received[:half, :], other)
     below[...] = tail[...] + received[half:, :]
     left -= 1
     panel = join([merged[: left * B, :], below[:extra, :]], 0)
@@ -570,7 +609,7 @@
             jax.ShapeDtypeStruct(((left - 1) * B + extra, B), F32),
             jax.ShapeDtypeStruct((B, B), F32),
         ),
-        in_specs=[vmem()] * 7,
+        in_specs=[vmem()] * len(arrived),
         out_specs=(vmem(),) * (2 + len(messages)),
         scratch_shapes=[
             pltpu.VMEM((halves(left)[1], B), F32),
@@ -624,6 +663,8 @@
     received[0], done = lax.optimization_barrier((received[0], meanwhile()))
     if len(sends) == 1:
         return (shared, tail, received[0]), done
+    if left <= 2:
+        return (shared, tail, received[1], *pivot(depth, shared, received[0])), done
     tri = pivot(depth, shared, received[0], swapped(received[0], "rep", 1))
     late, tri = lax.optimization_barrier((received[1], tri))
     other = swapped(late[: halves(left)[3]], "rep", 1)
@@ -646,12 +687,16 @@
     )
     factors += [a, b, c, d]
     halves_of = (w_hi, w_lo)
+    ahead = leaf_blocks.shape[1] // B // 2
     level = None
     for depth in range(levels):
 
         def meanwhile():
-            rows = halves_of if level is None else reduce(*level, *halves_of)
-            return solve(factors, perm, *rows) if depth + 1 == levels else rows
+            if depth == 0:
+                rows = begin(ahead, factors, *halves_of)
+            else:
+                rows = reduce(*level, *halves_of)
+            return solve(ahead, factors, perm, *rows) if depth + 1 == levels else rows
 
         arrived, halves_of = exchange(message, depth, levels - depth, meanwhile)
         if depth + 1 < levels:

time: 66.4 us -> 64 us (0.964)
  waiting for transfers between devices: 9.63 us -> 7.18 us
    ppermute x12 -> x10, waiting for transfers between devices: 9.63 us -> 7.18 us  [swapped(): return lax.ppermute(value, axis, pairs)]
    pallas_call x1 -> x2, Pallas kernels: 4.45 us -> 4.69 us  [the longest x1 3.24 us: solve(): pl.pallas_call(functools.partial(solve_kernel, ahead), out_shape=jax.Shap...]
    ppermute x12 -> x10, starting transfers between devices: 10.8 us -> 10.5 us  [swapped(): return lax.ppermute(value, axis, pairs)]
  transfers between devices with their start and end apart: 12 -> 10, of which waited for: 8 -> 8; matrix products, arithmetic and copies ran while one was open for 0% -> 0% of each run, Pallas kernels for 39% -> 41%
where the time goes in v4:
time: 64 us; the launch traced here: 63.8 us
  Pallas kernels  45.3 us (71%)
  starting transfers between devices  10.5 us (16%)
  waiting for transfers between devices  7.18 us (11%)
  between operations  0.75 us (1%)
    pallas_call x1, Pallas kernels, forward(): pl.pallas_call(functools.partial(forward_kernel, levels, len(pieces)), ou...  14.1 us
    pallas_call x1, Pallas kernels, head(): pl.pallas_call(functools.partial(head_kernel, cut), out_shape=(low, low,...  14 us
    ppermute x10, starting transfers between devices, swapped(): return lax.ppermute(value, axis, pairs)  10.5 us
    ppermute x10, waiting for transfers between devices, swapped(): return lax.ppermute(value, axis, pairs)  7.18 us
    pallas_call x2, Pallas kernels, pivot(): pl.pallas_call(pivot_kernel, out_shape=(tri, tri, jax.ShapeDtypeStruct((S...  5.56 us
    pallas_call x1, Pallas kernels, finish(): pl.pallas_call(functools.partial(finish_kernel, levels, leaf_count), out_...  4.13 us
    pallas_call x1, Pallas kernels, solve(): pl.pallas_call(functools.partial(solve_kernel, ahead), out_shape=jax.Shap...  3.24 us
    pallas_call x1, Pallas kernels, begin(): pl.pallas_call(functools.partial(begin_kernel, ahead), out_shape=(jax.Sha...  1.45 us
  transfers between devices with their start and end apart: 10, of which 8 were waited for; matrix products, arithmetic and copies ran while one was open for 0% of the time, Pallas kernels for 41%

profile of v4, /device:TPU:0, one launch (start us, length us, event | category | flops | bytes accessed | tf_op | source)
XLA Modules:
  0.0 63.8 jit_solution(13875313335520871717)
XLA Ops:
  0.7 3.0 %collective-permute-start = (f32[3,32,1024]{2,1,0:T(8,128)}, f32[3,32,1024]{2,1,0:T(8,128)S(1)}, u32[]{:S(2)}, u32[]{:S(2)}) collective-permute-start(f32[3,32,1024]{2,1,0:T(8,128)} %refs_7_.1), channel_id=1, source_target_pairs={{0,2},{1,3},{2,0},{3,1},{4,6},{5,7},{6,4},{7,5},{8,10},{9,11},{10,... | collective-permute-start | bytes 1179656 | tf_op jit(solution)/shard_map/ppermute | solution.py:657
  3.7 14.0 %head.1 = (bf16[3,896,128]{2,1,0:T(8,128)(2,1)S(1)}, bf16[3,896,128]{2,1,0:T(8,128)(2,1)S(1)}, bf16[4,256,128]{2,1,0:T(8,128)(2,1)S(1)}, bf16[4,256,128]{2,1,0:T...) custom-call(f32[1024,1024]{1,0:T(8,128)} %blocks.1), custom_call_target="tpu_custom_call" | custom-call | bytes 1048576 | tf_op jit(solution)/shard_map/head/pallas_call | solution.py:195
  17.7 0.6 collective-permute-start.2
  18.3 0.6 prepare.1
  19.0 0.7 %collective-permute-done.2.refs_10_ = f32[3,32,1024]{2,1,0:T(8,128)S(1)} collective-permute-done((f32[3,32,1024]{2,1,0:T(8,128)S(1)}, f32[3,32,1024]{2,1,0:T(8,128)S(1)}, u32[]{:S(2)}, u32[]{:S(2)}) %collective-permute-start.2) | collective-permute-done | bytes 393248 | tf_op jit(solution)/shard_map/ppermute | solution.py:657
  19.7 14.1 %forward.1 = (f32[768,128]{1,0:T(8,128)S(1)}, f32[104,128]{1,0:T(8,128)S(1)}, f32[64,128]{1,0:T(8,128)S(1)}, f32[424,128]{1,0:T(8,128)S(1)}, bf16[416,1024]{1,0:...) custom-call(bf16[3,896,128]{2,1,0:T(8,128)(2,1)S(1)} %get-tuple-elem, ...), custom_call_target="tpu_custom_call" | custom-call | bytes 1048576 | tf_op jit(solution)/shard_map/forward/pallas_call | solution.py:416
  33.8 1.6 %collective-permute-start.4 = (f32[64,128]{1,0:T(8,128)S(1)}, f32[64,128]{1,0:T(8,128)S(1)}, u32[]{:S(2)}, u32[]{:S(2)}) collective-permute-start(f32[64,128]{1,0:T(8,128)S(1)} %get-tuple-element.71), channel_id=1, source_target_pairs={{0,4},{4,0},{8,12},{12,8},{16,20},{20,16},{24,28},{28,24},{1,5},{5... | collective-permute-start | bytes 98312 | tf_op jit(solution)/shard_map/ppermute | solution.py:657
  35.3 0.5 collective-permute-start.3
  35.9 1.4 %begin.1 = (bf16[416,1024]{1,0:T(8,128)(2,1)S(1)}, bf16[416,1024]{1,0:T(8,128)(2,1)S(1)}) custom-call(bf16[3,896,128]{2,1,0:T(8,128)(2,1)S(1)} %get-tuple-element.59.refs_0_, bf16[3,896,128]{2,1,0:T(8,128)(2,1)S(1)} %get-tuple-element.60.refs_1_, bf16[4,256,128]{2,1,0:T(8,128)(2,1)S(1)} %get-tuple-element.61.refs_2_, ...), custom_call_target="tpu_custom_call" | custom-call | flops 100000000 | bytes 1048576 | tf_op jit(solution)/shard_map/begin/pallas_call | solution.py:491
  37.8 1.2 %collective-permute-done.5.refs_0_ = f32[64,128]{1,0:T(8,128)S(1)} collective-permute-done((f32[64,128]{1,0:T(8,128)S(1)}, f32[64,128]{1,0:T(8,128)S(1)}, u32[]{:S(2)}, u32[]{:S(2)}) %collective-permute-start.5) | collective-permute-done | bytes 32800 | tf_op jit(solution)/shard_map/ppermute | solution.py:657
  39.0 2.8 %pivot.2 = (bf16[256,128]{1,0:T(8,128)(2,1)S(1)}, bf16[256,128]{1,0:T(8,128)(2,1)S(1)}, f32[8,128]{1,0:T(8,128)S(1)}) custom-call(f32[768,128]{1,0:T(8,128)S(1)} %get-tuple-element.68.shared.refs_0_, f32[64,128]{1,0:T(8,128)S(1)} %collective-permute-done.4.received, f32[64,128]{1,0:T(8,128)S(1)} %collective-permute-done.5.refs_0_), custom_call_target="tpu_custom_call" | custom-call | flops 1800000000 | bytes 1048576 | tf_op jit(solution)/shard_map/pivot/pallas_call | solution.py:552
  41.8 0.9 %collective-permute-done.3.refs_2_ = f32[424,128]{1,0:T(8,128)S(1)} collective-permute-done((f32[424,128]{1,0:T(8,128)S(1)}, f32[424,128]{1,0:T(8,128)S(1)}, u32[]{:S(2)}, u32[]{:S(2)}) %collective-permute-start.3) | collective-permute-done | bytes 217120 | tf_op jit(solution)/shard_map/ppermute | solution.py:657
  42.8 1.4 %collective-permute-done.6.refs_3_ = f32[320,128]{1,0:T(8,128)S(1)} collective-permute-done((f32[320,128]{1,0:T(8,128)S(1)}, f32[320,128]{1,0:T(8,128)S(1)}, u32[]{:S(2)}, u32[]{:S(2)}) %collective-permute-start.6) | collective-permute-done | bytes 163872 | tf_op jit(solution)/shard_map/ppermute | solution.py:657
  44.1 0.6 merge.2
  44.8 1.6 %collective-permute-start.8 = (f32[128,128]{1,0:T(8,128)S(1)}, f32[128,128]{1,0:T(8,128)S(1)}, u32[]{:S(2)}, u32[]{:S(2)}) collective-permute-start(f32[128,128]{1,0:T(8,128)S(1)} %get-tuple-element.91), channel_id=1, source_target_pairs={{0,8},{4,12},{8,0},{12,4},{16,24},{20,28},{24,16},{28,20},{1,9},{5... | collective-permute-start | bytes 196616 | tf_op jit(solution)/shard_map/ppermute | solution.py:657
  46.4 0.4 collective-permute-start.7
  46.8 0.6 %reduce.2 = (bf16[288,1024]{1,0:T(8,128)(2,1)S(1)}, bf16[288,1024]{1,0:T(8,128)(2,1)S(1)}) custom-call(f32[288,128]{1,0:T(8,128)S(1)} %get-tuple-element.92.w_panel, f32[128,128]{1,0:T(8,128)S(1)} %get-tuple-element.93.tri, bf16[416,1024]{1,0:T(8,128)(2,1)S(1)} %get-tuple-element.94.w_hi, bf16[416,1024]{1,0:T(8,128)(2,1)S(1)} %get-tuple-element.95.w_lo), custom_call_target="tpu_custom_call" | custom-call | flops 4000000000 | bytes 1048576 | tf_op jit(solution)/shard_map/reduce/pallas_call | solution.py:445
  47.5 1.9 %collective-permute-done.8.received = f32[128,128]{1,0:T(8,128)S(1)} collective-permute-done((f32[128,128]{1,0:T(8,128)S(1)}, f32[128,128]{1,0:T(8,128)S(1)}, u32[]{:S(2)}, u32[]{:S(2)}) %collective-permute-start.8) | collective-permute-done | bytes 65568 | tf_op jit(solution)/shard_map/ppermute | solution.py:657
  49.4 2.8 %pivot.3 = (bf16[256,128]{1,0:T(8,128)(2,1)S(1)}, bf16[256,128]{1,0:T(8,128)(2,1)S(1)}, f32[8,128]{1,0:T(8,128)S(1)}) custom-call(f32[384,128]{1,0:T(8,128)S(1)} %get-tuple-element.88.shared.refs_0_, f32[128,128]{1,0:T(8,128)S(1)} %collective-permute-done.8.received), custom_call_target="tpu_custom_call" | custom-call | flops 500000000 | bytes 1048576 | tf_op jit(solution)/shard_map/pivot/pallas_call | solution.py:552
  52.2 0.5 collective-permute-done.7.refs_2_
  53.1 2.7 %collective-permute-start.9 = (f32[168,128]{1,0:T(8,128)S(1)}, f32[168,128]{1,0:T(8,128)S(1)}, u32[]{:S(2)}, u32[]{:S(2)}) collective-permute-start(f32[168,128]{1,0:T(8,128)S(1)} %get-tuple-element.104), channel_id=1, source_target_pairs={{0,16},{4,20},{8,24},{12,28},{16,0},{20,4},{24,8},{28,12},{1,17},{... | collective-permute-start | bytes 258056 | tf_op jit(solution)/shard_map/ppermute | solution.py:657
  55.8 0.5 reduce.3
  56.3 3.2 %solve.1.solved = f32[160,1024]{1,0:T(8,128)S(1)} custom-call(bf16[3,896,128]{2,1,0:T(8,128)(2,1)S(1)} %get-tuple-element.59.refs_0_, bf16[3,896,128]{2,1,0:T(8,128)(2,1)S(1)} %get-tuple-element.60.refs_1_, bf16[4,256,128]{2,1,0:T(8,128)(2,1)S(1)} %get-tuple-element.61.refs_2_, bf16[4,256,128]{2,1,0:T(8,128)(2,1)S(1)} %get-tuple-element.62.refs_3_, ...), custom_call_target="tpu_custom_call" | custom-call | flops 4000000000 | bytes 1048576 | tf_op jit(solution)/shard_map/solve/pallas_call | solution.py:514
  59.7 4.1 %finish.1 = (f32[32,1024]{1,0:T(8,128)}, f32[1,4]{1,0:T(1,128)}) custom-call(f32[128,128]{1,0:T(8,128)S(1)} %get-tuple-element.102.shared, f32[40,128]{1,0:T(8,128)S(1)} %get-tuple-element.103.tail, f32[168,128]{1,0:T(8,128)S(1)} %collective-permute-done.9.received, f32[160,1024]{1,0:T(8,128)S(1)} %solve.1.solved), custom_call_target="tpu_custom_call" | custom-call | bytes 1048576 | tf_op jit(solution)/shard_map/finish/pallas_call | solution.py:641
  (17 shorter events, 1.1 us)
Async XLA Ops:
  0.6 19.0 %copy-start = (f32[3,32,1024]{2,1,0:T(8,128)S(1)}, f32[3,32,1024]{2,1,0:T(8,128)}, u32[]{:S(2)}) copy-start(f32[3,32,1024]{2,1,0:T(8,128)} %refs_7_.1) | copy-start | bytes 1179652
  0.6 17.7 %copy-start.3 = (s32[1,1024]{1,0:T(1,128)S(1)}, s32[1,1024]{1,0:T(1,128)}, u32[]{:S(2)}) copy-start(s32[1,1024]{1,0:T(1,128)} %order.1) | copy-start | bytes 12292
  0.7 17.7 %copy-start.2 = (f32[32,1024]{1,0:T(8,128)S(1)}, f32[32,1024]{1,0:T(8,128)}, u32[]{:S(2)}) copy-start(f32[32,1024]{1,0:T(8,128)} %rhs.1) | copy-start | bytes 393220
  0.7 19.0 %copy-start.1 = (s32[3,1]{0,1:T(1,128)S(1)}, s32[3,1]{0,1:T(1,128)}, u32[]{:S(2)}) copy-start(s32[3,1]{0,1:T(1,128)} %param.9) | copy-start | bytes 40
  0.7 17.1 %collective-permute-start = (f32[3,32,1024]{2,1,0:T(8,128)}, f32[3,32,1024]{2,1,0:T(8,128)S(1)}, u32[]{:S(2)}, u32[]{:S(2)}) collective-permute-start(f32[3,32,1024]{2,1,0:T(8,128)} %refs_7_.1), channel_id=1, source_target_pairs={{0,2},{1,3},{2,0},{3,1},{4,6},{5,7},{6,4},{7,5},{8,10},{9,11},{10,... | collective-permute-start | bytes 1179656 | tf_op jit(solution)/shard_map/ppermute | solution.py:657
  3.7 15.3 %collective-permute-start.1 = (f32[3,32,1024]{2,1,0:T(8,128)}, f32[3,32,1024]{2,1,0:T(8,128)S(1)}, u32[]{:S(2)}, u32[]{:S(2)}) collective-permute-start(f32[3,32,1024]{2,1,0:T(8,128)} %refs_7_.1), channel_id=1, source_target_pairs={{0,1},{1,0},{2,3},{3,2},{4,5},{5,4},{6,7},{7,6},{8,9},{9,8},{10,11... | collective-permute-start | bytes 1179656 | tf_op jit(solution)/shard_map/ppermute | solution.py:657
  17.7 1.9 %collective-permute-start.2 = (f32[3,32,1024]{2,1,0:T(8,128)S(1)}, f32[3,32,1024]{2,1,0:T(8,128)S(1)}, u32[]{:S(2)}, u32[]{:S(2)}) collective-permute-start(f32[3,32,1024]{2,1,0:T(8,128)S(1)} %collective-permute-done.refs_9_), channel_id=1, source_target_pairs={{0,1},{1,0},{2,3},{3,2},{4,5},{5,4},{6,7},{7,6},{8,9},{9,8},{10,11... | collective-permute-start | bytes 1179656 | tf_op jit(solution)/shard_map/ppermute | solution.py:657
  33.8 4.0 %collective-permute-start.4 = (f32[64,128]{1,0:T(8,128)S(1)}, f32[64,128]{1,0:T(8,128)S(1)}, u32[]{:S(2)}, u32[]{:S(2)}) collective-permute-start(f32[64,128]{1,0:T(8,128)S(1)} %get-tuple-element.71), channel_id=1, source_target_pairs={{0,4},{4,0},{8,12},{12,8},{16,20},{20,16},{24,28},{28,24},{1,5},{5... | collective-permute-start | bytes 98312 | tf_op jit(solution)/shard_map/ppermute | solution.py:657
  35.3 7.3 %collective-permute-start.3 = (f32[424,128]{1,0:T(8,128)S(1)}, f32[424,128]{1,0:T(8,128)S(1)}, u32[]{:S(2)}, u32[]{:S(2)}) collective-permute-start(f32[424,128]{1,0:T(8,128)S(1)} %get-tuple-element.70), channel_id=1, source_target_pairs={{0,4},{4,0},{8,12},{12,8},{16,20},{20,16},{24,28},{28,24},{1,5},{5... | collective-permute-start | bytes 651272 | tf_op jit(solution)/shard_map/ppermute | solution.py:657
  37.8 1.2 %collective-permute-start.5 = (f32[64,128]{1,0:T(8,128)S(1)}, f32[64,128]{1,0:T(8,128)S(1)}, u32[]{:S(2)}, u32[]{:S(2)}) collective-permute-start(f32[64,128]{1,0:T(8,128)S(1)} %collective-permute-done.4.received), channel_id=1, source_target_pairs={{0,1},{1,0},{2,3},{3,2},{4,5},{5,4},{6,7},{7,6},{8,9},{9,8},{10,11... | collective-permute-start | bytes 98312 | tf_op jit(solution)/shard_map/ppermute | solution.py:657
  42.7 1.5 %collective-permute-start.6 = (f32[320,128]{1,0:T(8,128)S(1)}, f32[320,128]{1,0:T(8,128)S(1)}, u32[]{:S(2)}, u32[]{:S(2)}) collective-permute-start(f32[320,128]{1,0:T(8,128)S(1)} %slice.3), channel_id=1, source_target_pairs={{0,1},{1,0},{2,3},{3,2},{4,5},{5,4},{6,7},{7,6},{8,9},{9,8},{10,11... | collective-permute-start | bytes 491528 | tf_op jit(solution)/shard_map/ppermute | solution.py:657
  44.8 4.6 %collective-permute-start.8 = (f32[128,128]{1,0:T(8,128)S(1)}, f32[128,128]{1,0:T(8,128)S(1)}, u32[]{:S(2)}, u32[]{:S(2)}) collective-permute-start(f32[128,128]{1,0:T(8,128)S(1)} %get-tuple-element.91), channel_id=1, source_target_pairs={{0,8},{4,12},{8,0},{12,4},{16,24},{20,28},{24,16},{28,20},{1,9},{5... | collective-permute-start | bytes 196616 | tf_op jit(solution)/shard_map/ppermute | solution.py:657
  46.4 6.3 %collective-permute-start.7 = (f32[328,128]{1,0:T(8,128)S(1)}, f32[328,128]{1,0:T(8,128)S(1)}, u32[]{:S(2)}, u32[]{:S(2)}) collective-permute-start(f32[328,128]{1,0:T(8,128)S(1)} %get-tuple-element.90), channel_id=1, source_target_pairs={{0,8},{4,12},{8,0},{12,4},{16,24},{20,28},{24,16},{28,20},{1,9},{5... | collective-permute-start | bytes 503816 | tf_op jit(solution)/shard_map/ppermute | solution.py:657
  53.1 6.5 %collective-permute-start.9 = (f32[168,128]{1,0:T(8,128)S(1)}, f32[168,128]{1,0:T(8,128)S(1)}, u32[]{:S(2)}, u32[]{:S(2)}) collective-permute-start(f32[168,128]{1,0:T(8,128)S(1)} %get-tuple-element.104), channel_id=1, source_target_pairs={{0,16},{4,20},{8,24},{12,28},{16,0},{20,4},{24,8},{28,12},{1,17},{... | collective-permute-start | bytes 258056 | tf_op jit(solution)/shard_map/ppermute | solution.py:657

commit v5 on v4

--- a/solution.py
+++ b/solution.py
@@ -65,11 +65,11 @@
         panel = jnp.where(inside, jnp.where(lane - base == sub, 1.0, 0.0), rows[p])
         t[p] = jnp.where(upto, panel, 0.0)
         following = p + 1 < count
-        ahead = None
         if following:
             first = [lanes_of(rows[p + 1], base + l) for l in range(SUB)]
             below = list(first)
-            ahead = [lanes_of(rows[p + 1], base + SUB + l) for l in range(SUB)]
+            start = [lanes_of(rows[p + 1], base + SUB + l) for l in range(SUB)]
+            ahead = [None] * SUB
         for j in range(SUB):
             across = {l: row_of(cols[l], j) for l in range(j, SUB)}
             pivots = jnp.where(lane == base + j, across[j], pivots)
@@ -83,7 +83,8 @@
                 spare[slot, :SUB, :] = below[j]
                 factor = below[j] * inverse
                 for l in range(SUB):
-                    ahead[l] = ahead[l] - factor * spare[slot, pl.ds(l, SUB, stride=0), :]
+                    term = factor * spare[slot, pl.ds(l, SUB, stride=0), :]
+                    ahead[l] = term if ahead[l] is None else ahead[l] + term
                 for l in range(j + 1, SUB):
                     below[l] = below[l] - factor * across[l]
         rt[p] = jnp.where(upto, panel, 0.0)
@@ -93,7 +94,7 @@
             update(list(range(p + 2, min(p + 3, count))), base, inside, spread)
             for q in range(p + 3, count, 3):
                 update(list(range(q, min(q + 3, count))), base, inside, spread)
-        cols = ahead
+            cols = [before - change for before, change in zip(start, ahead)]
     return jnp.concatenate(t + rt, axis=0), pivots
 
 

time: 64 us -> 63.7 us (level)
  no operation moved by 1% of the time
where the time goes in v5:
time: 63.7 us; the launch traced here: 63.5 us
  Pallas kernels  45.2 us (71%)
  starting transfers between devices  10.6 us (17%)
  waiting for transfers between devices  7.05 us (11%)
  between operations  0.75 us (1%)
    pallas_call x1, Pallas kernels, head(): pl.pallas_call(functools.partial(head_kernel, cut), out_shape=(low, low,...  14.1 us
    pallas_call x1, Pallas kernels, forward(): pl.pallas_call(functools.partial(forward_kernel, levels, len(pieces)), ou...  13.8 us
    ppermute x10, starting transfers between devices, swapped(): return lax.ppermute(value, axis, pairs)  10.6 us
    ppermute x10, waiting for transfers between devices, swapped(): return lax.ppermute(value, axis, pairs)  7.05 us
    pallas_call x2, Pallas kernels, pivot(): pl.pallas_call(pivot_kernel, out_shape=(tri, tri, jax.ShapeDtypeStruct((S...  5.7 us
    pallas_call x1, Pallas kernels, finish(): pl.pallas_call(functools.partial(finish_kernel, levels, leaf_count), out_...  4.09 us
    pallas_call x1, Pallas kernels, solve(): pl.pallas_call(functools.partial(solve_kernel, ahead), out_shape=jax.Shap...  3.24 us
    pallas_call x1, Pallas kernels, begin(): pl.pallas_call(functools.partial(begin_kernel, ahead), out_shape=(jax.Sha...  1.44 us
  transfers between devices with their start and end apart: 10, of which 8 were waited for; matrix products, arithmetic and copies ran while one was open for 0% of the time, Pallas kernels for 41%

profile of v5, /device:TPU:0, one launch (start us, length us, event | category | flops | bytes accessed | tf_op | source)
XLA Modules:
  0.0 63.5 jit_solution(174131138810308575)
XLA Ops:
  0.7 3.0 %collective-permute-start = (f32[3,32,1024]{2,1,0:T(8,128)}, f32[3,32,1024]{2,1,0:T(8,128)S(1)}, u32[]{:S(2)}, u32[]{:S(2)}) collective-permute-start(f32[3,32,1024]{2,1,0:T(8,128)} %refs_7_.1), channel_id=1, source_target_pairs={{0,2},{1,3},{2,0},{3,1},{4,6},{5,7},{6,4},{7,5},{8,10},{9,11},{10,... | collective-permute-start | bytes 1179656 | tf_op jit(solution)/shard_map/ppermute | solution.py:658
  3.7 14.1 %head.1 = (bf16[3,896,128]{2,1,0:T(8,128)(2,1)S(1)}, bf16[3,896,128]{2,1,0:T(8,128)(2,1)S(1)}, bf16[4,256,128]{2,1,0:T(8,128)(2,1)S(1)}, bf16[4,256,128]{2,1,0:T...) custom-call(f32[1024,1024]{1,0:T(8,128)} %blocks.1), custom_call_target="tpu_custom_call" | custom-call | bytes 1048576 | tf_op jit(solution)/shard_map/head/pallas_call | solution.py:196
  17.8 0.6 collective-permute-start.2
  18.4 0.6 prepare.1
  19.0 0.7 %collective-permute-done.2.refs_10_ = f32[3,32,1024]{2,1,0:T(8,128)S(1)} collective-permute-done((f32[3,32,1024]{2,1,0:T(8,128)S(1)}, f32[3,32,1024]{2,1,0:T(8,128)S(1)}, u32[]{:S(2)}, u32[]{:S(2)}) %collective-permute-start.2) | collective-permute-done | bytes 393248 | tf_op jit(solution)/shard_map/ppermute | solution.py:658
  19.7 13.8 %forward.1 = (f32[768,128]{1,0:T(8,128)S(1)}, f32[104,128]{1,0:T(8,128)S(1)}, f32[64,128]{1,0:T(8,128)S(1)}, f32[424,128]{1,0:T(8,128)S(1)}, bf16[416,1024]{1,0:...) custom-call(bf16[3,896,128]{2,1,0:T(8,128)(2,1)S(1)} %get-tuple-elem, ...), custom_call_target="tpu_custom_call" | custom-call | bytes 1048576 | tf_op jit(solution)/shard_map/forward/pallas_call | solution.py:417
  33.5 1.6 %collective-permute-start.4 = (f32[64,128]{1,0:T(8,128)S(1)}, f32[64,128]{1,0:T(8,128)S(1)}, u32[]{:S(2)}, u32[]{:S(2)}) collective-permute-start(f32[64,128]{1,0:T(8,128)S(1)} %get-tuple-element.71), channel_id=1, source_target_pairs={{0,4},{4,0},{8,12},{12,8},{16,20},{20,16},{24,28},{28,24},{1,5},{5... | collective-permute-start | bytes 98312 | tf_op jit(solution)/shard_map/ppermute | solution.py:658
  35.1 0.5 collective-permute-start.3
  35.7 1.4 %begin.1 = (bf16[416,1024]{1,0:T(8,128)(2,1)S(1)}, bf16[416,1024]{1,0:T(8,128)(2,1)S(1)}) custom-call(bf16[3,896,128]{2,1,0:T(8,128)(2,1)S(1)} %get-tuple-element.59.refs_0_, bf16[3,896,128]{2,1,0:T(8,128)(2,1)S(1)} %get-tuple-element.60.refs_1_, bf16[4,256,128]{2,1,0:T(8,128)(2,1)S(1)} %get-tuple-element.61.refs_2_, ...), custom_call_target="tpu_custom_call" | custom-call | flops 100000000 | bytes 1048576 | tf_op jit(solution)/shard_map/begin/pallas_call | solution.py:492
  37.6 1.2 %collective-permute-done.5.refs_0_ = f32[64,128]{1,0:T(8,128)S(1)} collective-permute-done((f32[64,128]{1,0:T(8,128)S(1)}, f32[64,128]{1,0:T(8,128)S(1)}, u32[]{:S(2)}, u32[]{:S(2)}) %collective-permute-start.5) | collective-permute-done | bytes 32800 | tf_op jit(solution)/shard_map/ppermute | solution.py:658
  38.8 2.9 %pivot.2 = (bf16[256,128]{1,0:T(8,128)(2,1)S(1)}, bf16[256,128]{1,0:T(8,128)(2,1)S(1)}, f32[8,128]{1,0:T(8,128)S(1)}) custom-call(f32[768,128]{1,0:T(8,128)S(1)} %get-tuple-element.68.shared.refs_0_, f32[64,128]{1,0:T(8,128)S(1)} %collective-permute-done.4.received, f32[64,128]{1,0:T(8,128)S(1)} %collective-permute-done.5.refs_0_), custom_call_target="tpu_custom_call" | custom-call | flops 1800000000 | bytes 1048576 | tf_op jit(solution)/shard_map/pivot/pallas_call | solution.py:553
  41.6 0.8 %collective-permute-done.3.refs_2_ = f32[424,128]{1,0:T(8,128)S(1)} collective-permute-done((f32[424,128]{1,0:T(8,128)S(1)}, f32[424,128]{1,0:T(8,128)S(1)}, u32[]{:S(2)}, u32[]{:S(2)}) %collective-permute-start.3) | collective-permute-done | bytes 217120 | tf_op jit(solution)/shard_map/ppermute | solution.py:658
  42.5 1.4 %collective-permute-done.6.refs_3_ = f32[320,128]{1,0:T(8,128)S(1)} collective-permute-done((f32[320,128]{1,0:T(8,128)S(1)}, f32[320,128]{1,0:T(8,128)S(1)}, u32[]{:S(2)}, u32[]{:S(2)}) %collective-permute-start.6) | collective-permute-done | bytes 163872 | tf_op jit(solution)/shard_map/ppermute | solution.py:658
  43.9 0.6 merge.2
  44.5 1.6 %collective-permute-start.8 = (f32[128,128]{1,0:T(8,128)S(1)}, f32[128,128]{1,0:T(8,128)S(1)}, u32[]{:S(2)}, u32[]{:S(2)}) collective-permute-start(f32[128,128]{1,0:T(8,128)S(1)} %get-tuple-element.91), channel_id=1, source_target_pairs={{0,8},{4,12},{8,0},{12,4},{16,24},{20,28},{24,16},{28,20},{1,9},{5... | collective-permute-start | bytes 196616 | tf_op jit(solution)/shard_map/ppermute | solution.py:658
  46.2 0.4 collective-permute-start.7
  46.6 0.6 %reduce.2 = (bf16[288,1024]{1,0:T(8,128)(2,1)S(1)}, bf16[288,1024]{1,0:T(8,128)(2,1)S(1)}) custom-call(f32[288,128]{1,0:T(8,128)S(1)} %get-tuple-element.92.w_panel, f32[128,128]{1,0:T(8,128)S(1)} %get-tuple-element.93.tri, bf16[416,1024]{1,0:T(8,128)(2,1)S(1)} %get-tuple-element.94.w_hi, bf16[416,1024]{1,0:T(8,128)(2,1)S(1)} %get-tuple-element.95.w_lo), custom_call_target="tpu_custom_call" | custom-call | flops 4000000000 | bytes 1048576 | tf_op jit(solution)/shard_map/reduce/pallas_call | solution.py:446
  47.3 1.9 %collective-permute-done.8.received = f32[128,128]{1,0:T(8,128)S(1)} collective-permute-done((f32[128,128]{1,0:T(8,128)S(1)}, f32[128,128]{1,0:T(8,128)S(1)}, u32[]{:S(2)}, u32[]{:S(2)}) %collective-permute-start.8) | collective-permute-done | bytes 65568 | tf_op jit(solution)/shard_map/ppermute | solution.py:658
  49.2 2.8 %pivot.3 = (bf16[256,128]{1,0:T(8,128)(2,1)S(1)}, bf16[256,128]{1,0:T(8,128)(2,1)S(1)}, f32[8,128]{1,0:T(8,128)S(1)}) custom-call(f32[384,128]{1,0:T(8,128)S(1)} %get-tuple-element.88.shared.refs_0_, f32[128,128]{1,0:T(8,128)S(1)} %collective-permute-done.8.received), custom_call_target="tpu_custom_call" | custom-call | flops 500000000 | bytes 1048576 | tf_op jit(solution)/shard_map/pivot/pallas_call | solution.py:553
  52.0 0.4 collective-permute-done.7.refs_2_
  52.9 2.7 %collective-permute-start.9 = (f32[168,128]{1,0:T(8,128)S(1)}, f32[168,128]{1,0:T(8,128)S(1)}, u32[]{:S(2)}, u32[]{:S(2)}) collective-permute-start(f32[168,128]{1,0:T(8,128)S(1)} %get-tuple-element.104), channel_id=1, source_target_pairs={{0,16},{4,20},{8,24},{12,28},{16,0},{20,4},{24,8},{28,12},{1,17},{... | collective-permute-start | bytes 258056 | tf_op jit(solution)/shard_map/ppermute | solution.py:658
  55.6 0.5 reduce.3
  56.1 3.2 %solve.1.solved = f32[160,1024]{1,0:T(8,128)S(1)} custom-call(bf16[3,896,128]{2,1,0:T(8,128)(2,1)S(1)} %get-tuple-element.59.refs_0_, bf16[3,896,128]{2,1,0:T(8,128)(2,1)S(1)} %get-tuple-element.60.refs_1_, bf16[4,256,128]{2,1,0:T(8,128)(2,1)S(1)} %get-tuple-element.61.refs_2_, bf16[4,256,128]{2,1,0:T(8,128)(2,1)S(1)} %get-tuple-element.62.refs_3_, ...), custom_call_target="tpu_custom_call" | custom-call | flops 4000000000 | bytes 1048576 | tf_op jit(solution)/shard_map/solve/pallas_call | solution.py:515
  59.5 4.1 %finish.1 = (f32[32,1024]{1,0:T(8,128)}, f32[1,4]{1,0:T(1,128)}) custom-call(f32[128,128]{1,0:T(8,128)S(1)} %get-tuple-element.102.shared, f32[40,128]{1,0:T(8,128)S(1)} %get-tuple-element.103.tail, f32[168,128]{1,0:T(8,128)S(1)} %collective-permute-done.9.received, f32[160,1024]{1,0:T(8,128)S(1)} %solve.1.solved), custom_call_target="tpu_custom_call" | custom-call | bytes 1048576 | tf_op jit(solution)/shard_map/finish/pallas_call | solution.py:642
  (17 shorter events, 1.1 us)
Async XLA Ops:
  0.6 19.1 %copy-start = (f32[3,32,1024]{2,1,0:T(8,128)S(1)}, f32[3,32,1024]{2,1,0:T(8,128)}, u32[]{:S(2)}) copy-start(f32[3,32,1024]{2,1,0:T(8,128)} %refs_7_.1) | copy-start | bytes 1179652
  0.6 17.7 %copy-start.3 = (s32[1,1024]{1,0:T(1,128)S(1)}, s32[1,1024]{1,0:T(1,128)}, u32[]{:S(2)}) copy-start(s32[1,1024]{1,0:T(1,128)} %order.1) | copy-start | bytes 12292
  0.7 17.7 %copy-start.2 = (f32[32,1024]{1,0:T(8,128)S(1)}, f32[32,1024]{1,0:T(8,128)}, u32[]{:S(2)}) copy-start(f32[32,1024]{1,0:T(8,128)} %rhs.1) | copy-start | bytes 393220
  0.7 19.1 %copy-start.1 = (s32[3,1]{0,1:T(1,128)S(1)}, s32[3,1]{0,1:T(1,128)}, u32[]{:S(2)}) copy-start(s32[3,1]{0,1:T(1,128)} %param.9) | copy-start | bytes 40
  0.7 17.1 %collective-permute-start = (f32[3,32,1024]{2,1,0:T(8,128)}, f32[3,32,1024]{2,1,0:T(8,128)S(1)}, u32[]{:S(2)}, u32[]{:S(2)}) collective-permute-start(f32[3,32,1024]{2,1,0:T(8,128)} %refs_7_.1), channel_id=1, source_target_pairs={{0,2},{1,3},{2,0},{3,1},{4,6},{5,7},{6,4},{7,5},{8,10},{9,11},{10,... | collective-permute-start | bytes 1179656 | tf_op jit(solution)/shard_map/ppermute | solution.py:658
  3.7 15.3 %collective-permute-start.1 = (f32[3,32,1024]{2,1,0:T(8,128)}, f32[3,32,1024]{2,1,0:T(8,128)S(1)}, u32[]{:S(2)}, u32[]{:S(2)}) collective-permute-start(f32[3,32,1024]{2,1,0:T(8,128)} %refs_7_.1), channel_id=1, source_target_pairs={{0,1},{1,0},{2,3},{3,2},{4,5},{5,4},{6,7},{7,6},{8,9},{9,8},{10,11... | collective-permute-start | bytes 1179656 | tf_op jit(solution)/shard_map/ppermute | solution.py:658
  17.8 1.9 %collective-permute-start.2 = (f32[3,32,1024]{2,1,0:T(8,128)S(1)}, f32[3,32,1024]{2,1,0:T(8,128)S(1)}, u32[]{:S(2)}, u32[]{:S(2)}) collective-permute-start(f32[3,32,1024]{2,1,0:T(8,128)S(1)} %collective-permute-done.refs_9_), channel_id=1, source_target_pairs={{0,1},{1,0},{2,3},{3,2},{4,5},{5,4},{6,7},{7,6},{8,9},{9,8},{10,11... | collective-permute-start | bytes 1179656 | tf_op jit(solution)/shard_map/ppermute | solution.py:658
  33.5 4.0 %collective-permute-start.4 = (f32[64,128]{1,0:T(8,128)S(1)}, f32[64,128]{1,0:T(8,128)S(1)}, u32[]{:S(2)}, u32[]{:S(2)}) collective-permute-start(f32[64,128]{1,0:T(8,128)S(1)} %get-tuple-element.71), channel_id=1, source_target_pairs={{0,4},{4,0},{8,12},{12,8},{16,20},{20,16},{24,28},{28,24},{1,5},{5... | collective-permute-start | bytes 98312 | tf_op jit(solution)/shard_map/ppermute | solution.py:658
  35.1 7.3 %collective-permute-start.3 = (f32[424,128]{1,0:T(8,128)S(1)}, f32[424,128]{1,0:T(8,128)S(1)}, u32[]{:S(2)}, u32[]{:S(2)}) collective-permute-start(f32[424,128]{1,0:T(8,128)S(1)} %get-tuple-element.70), channel_id=1, source_target_pairs={{0,4},{4,0},{8,12},{12,8},{16,20},{20,16},{24,28},{28,24},{1,5},{5... | collective-permute-start | bytes 651272 | tf_op jit(solution)/shard_map/ppermute | solution.py:658
  37.6 1.2 %collective-permute-start.5 = (f32[64,128]{1,0:T(8,128)S(1)}, f32[64,128]{1,0:T(8,128)S(1)}, u32[]{:S(2)}, u32[]{:S(2)}) collective-permute-start(f32[64,128]{1,0:T(8,128)S(1)} %collective-permute-done.4.received), channel_id=1, source_target_pairs={{0,1},{1,0},{2,3},{3,2},{4,5},{5,4},{6,7},{7,6},{8,9},{9,8},{10,11... | collective-permute-start | bytes 98312 | tf_op jit(solution)/shard_map/ppermute | solution.py:658
  42.5 1.5 %collective-permute-start.6 = (f32[320,128]{1,0:T(8,128)S(1)}, f32[320,128]{1,0:T(8,128)S(1)}, u32[]{:S(2)}, u32[]{:S(2)}) collective-permute-start(f32[320,128]{1,0:T(8,128)S(1)} %slice.3), channel_id=1, source_target_pairs={{0,1},{1,0},{2,3},{3,2},{4,5},{5,4},{6,7},{7,6},{8,9},{9,8},{10,11... | collective-permute-start | bytes 491528 | tf_op jit(solution)/shard_map/ppermute | solution.py:658
  44.5 4.6 %collective-permute-start.8 = (f32[128,128]{1,0:T(8,128)S(1)}, f32[128,128]{1,0:T(8,128)S(1)}, u32[]{:S(2)}, u32[]{:S(2)}) collective-permute-start(f32[128,128]{1,0:T(8,128)S(1)} %get-tuple-element.91), channel_id=1, source_target_pairs={{0,8},{4,12},{8,0},{12,4},{16,24},{20,28},{24,16},{28,20},{1,9},{5... | collective-permute-start | bytes 196616 | tf_op jit(solution)/shard_map/ppermute | solution.py:658
  46.2 6.3 %collective-permute-start.7 = (f32[328,128]{1,0:T(8,128)S(1)}, f32[328,128]{1,0:T(8,128)S(1)}, u32[]{:S(2)}, u32[]{:S(2)}) collective-permute-start(f32[328,128]{1,0:T(8,128)S(1)} %get-tuple-element.90), channel_id=1, source_target_pairs={{0,8},{4,12},{8,0},{12,4},{16,24},{20,28},{24,16},{28,20},{1,9},{5... | collective-permute-start | bytes 503816 | tf_op jit(solution)/shard_map/ppermute | solution.py:658
  52.9 6.5 %collective-permute-start.9 = (f32[168,128]{1,0:T(8,128)S(1)}, f32[168,128]{1,0:T(8,128)S(1)}, u32[]{:S(2)}, u32[]{:S(2)}) collective-permute-start(f32[168,128]{1,0:T(8,128)S(1)} %get-tuple-element.104), channel_id=1, source_target_pairs={{0,16},{4,20},{8,24},{12,28},{16,0},{20,4},{24,8},{28,12},{1,17},{... | collective-permute-start | bytes 258056 | tf_op jit(solution)/shard_map/ppermute | solution.py:658
